TPU v7x, 32 devices: a whole 2x2x4 slice. The times are simulated.
32 devices in a mesh: ctx: 16 (over z, y, core), wt: 2 (over x).
Axes of the slice: x: 2, y: 2, z: 4, core: 2. Of those that a mesh axis runs over, the one named last changes fastest.
Arguments:
- activations: bfloat16 [2, 16384, 1024], P('wt', 'ctx'), may hold values from -6 to 6
- block_order: int32 [32], replicated, may hold values from 0 to 31, as said below
- qkv_weight: bfloat16 [1024, 3072], P('wt'), may hold values from -0.1875 to 0.1875
- qv_bias: bfloat16 [2048], P('wt'), may hold values from -3 to 3
- proj_weight: bfloat16 [1024, 1024], P('wt'), may hold values from -0.1875 to 0.1875
- proj_bias: bfloat16 [1024], P('wt'), may hold values from -3 to 3
- up_weight: bfloat16 [4096, 1024], P('wt'), may hold values from -0.1875 to 0.1875
- up_bias: bfloat16 [4096], P('wt'), may hold values from -3 to 3
- down_weight: bfloat16 [4096, 1024], P('wt'), may hold values from -0.09375 to 0.09375
- down_bias: bfloat16 [1024], P('wt'), may hold values from -3 to 3
- norm_gains: bfloat16 [4, 1024], P(None, 'wt'), may hold values from 0.25 to 1.75
- norm_biases: bfloat16 [4, 1024], P(None, 'wt'), may hold values from -2 to 2
- cotangent: bfloat16 [2, 16384, 1024], P('wt', 'ctx'), may hold values from -6 to 6
Outputs:
- layer_output: bfloat16 [2, 16384, 1024], P('wt', 'ctx')
- input_grad: float32 [2, 16384, 1024], P('wt', 'ctx')
- grad_qkv: float32 [1024, 3072], P('wt')
- grad_qvbias: float32 [2048], P('wt')
- grad_proj: float32 [1024, 1024], P('wt')
- grad_projbias: float32 [1024], P('wt')
- grad_upward: float32 [4096, 1024], P('wt')
- grad_upbias: float32 [4096], P('wt')
- grad_downward: float32 [4096, 1024], P('wt')
- grad_downbias: float32 [1024], P('wt')
- grad_gains: float32 [4, 1024], P(None, 'wt')
- grad_biases: float32 [4, 1024], P(None, 'wt')
Inputs may be any that keep to these rules, and one draw needn't show every extreme that they name: `block_order`: for each index d of ctx, slots 2 d and 2 d + 1 hold blocks m and 31 - m for some m below 16, so that every block is held once; all sequences use the same order.
All inputs are finite; a program needn't handle non-finite values.
Results may differ from a plain program's by a relative error of at most 0.02.
Values may be sent and summed in bfloat16 or wider, within the bound.
No kernel may reach another device: no remote copies, remote signals or barrier semaphores. Data moves between devices by JAX's collectives and lax.ppermute only.
A program may use at most 704 MiB of HBM per device.

v0:
```python
import math

import jax
import jax.numpy as jnp
from jax import lax
from jax.sharding import PartitionSpec as P

HEADS = 16


relax_alpha = 32.0
norm_eps = 1e-05
huge_negative = -1e30


def layer_norm(values, norm_gain, norm_shift):
    average = jnp.mean(values, axis=-1, keepdims=True)
    centered = values - average
    variance = jnp.mean(centered * centered, axis=-1, keepdims=True)
    return centered * lax.rsqrt(variance + norm_eps) * norm_gain + norm_shift


def norm_backward(values, norm_gain, norm_shift, upstream):
    result, pullback = jax.vjp(layer_norm, values, norm_gain, norm_shift)
    return pullback(upstream)


def gelu_tanh(values):
    return jax.nn.gelu(values, approximate=True)


def gelu_backward(values, upstream):
    result, pullback = jax.vjp(gelu_tanh, values)
    return pullback(upstream)[0]


def pair_positions(block_order, device, half_rows):
    firsts = lax.dynamic_slice(block_order, (2 * device,), (2,))
    offsets = jnp.arange(half_rows, dtype=jnp.int32)
    return jnp.concatenate([firsts[0] * half_rows + offsets, firsts[1] * half_rows + offsets])


def add_slot(total, part, row_start):
    current = lax.dynamic_slice_in_dim(total, row_start, part.shape[1], 1)
    return lax.dynamic_update_slice_in_dim(total, current + part, row_start, 1)


def tile_forward(query_heads, key_heads, value_heads, query_pos, key_pos):
    scores = (
        jnp.einsum("sqhd,skhd->shqk", query_heads, key_heads, preferred_element_type=jnp.float32)
        * relax_alpha
    )
    visible = query_pos[:, None] >= key_pos[None, :]
    scores = jnp.where(visible, scores, huge_negative)
    row_peak = jnp.max(scores, axis=-1)
    weights = jnp.exp(scores - row_peak[..., None])
    row_total = jnp.sum(weights, axis=-1)
    summed = jnp.einsum(
        "shqk,skhd->sqhd",
        weights.astype(jnp.bfloat16),
        value_heads,
        preferred_element_type=jnp.float32,
    )
    return (row_peak, row_total, summed)


def combine_stats(older, newer):
    row_peak = jnp.maximum(older[0], newer[0])
    keep_old = jnp.exp(older[0] - row_peak)
    keep_new = jnp.exp(newer[0] - row_peak)
    row_total = older[1] * keep_old + newer[1] * keep_new
    summed = (
        older[2] * jnp.transpose(keep_old, (0, 2, 1))[..., None]
        + newer[2] * jnp.transpose(keep_new, (0, 2, 1))[..., None]
    )
    return (row_peak, row_total, summed)


def upper_rows(partial_stats, half_rows):
    return (
        partial_stats[0][:, :, half_rows:],
        partial_stats[1][:, :, half_rows:],
        partial_stats[2][:, half_rows:],
    )


def join_rows(partial_stats, upper_part, half_rows):
    return (
        jnp.concatenate([partial_stats[0][:, :, :half_rows], upper_part[0]], axis=2),
        jnp.concatenate([partial_stats[1][:, :, :half_rows], upper_part[1]], axis=2),
        jnp.concatenate([partial_stats[2][:, :half_rows], upper_part[2]], axis=1),
    )


def tile_backward(
    query_heads, grad_heads, log_total, row_shift, key_heads, value_heads, query_pos, key_pos
):
    scores = (
        jnp.einsum("sqhd,skhd->shqk", query_heads, key_heads, preferred_element_type=jnp.float32)
        * relax_alpha
    )
    visible = query_pos[:, None] >= key_pos[None, :]
    scores = jnp.where(visible, scores, huge_negative)
    probs_full = jnp.exp(scores - log_total[..., None])
    grad_probs = jnp.einsum(
        "sqhd,skhd->shqk", grad_heads, value_heads, preferred_element_type=jnp.float32
    )
    grad_scores = (relax_alpha * probs_full * (grad_probs - row_shift[..., None])).astype(
        jnp.bfloat16
    )
    return (grad_scores, probs_full.astype(jnp.bfloat16))


def local(
    activations,
    block_order,
    qkv_weight,
    qv_bias,
    proj_weight,
    proj_bias,
    up_weight,
    up_bias,
    down_weight,
    down_bias,
    norm_gains,
    norm_biases,
    cotangent,
):
    seq_count, shard_rows, model_width = activations.shape
    half_rows = shard_rows // 2
    head_count = HEADS
    head_dim = model_width // head_count
    token_count = seq_count * shard_rows
    query_scale = 1.0 / (relax_alpha * math.sqrt(head_dim))

    def split_heads(array):
        return array.reshape(array.shape[0], array.shape[1], head_count, head_dim)

    def rows_of(array, shard_index):
        return lax.dynamic_slice_in_dim(array, shard_index * shard_rows, shard_rows, 1)

    full_qkv, full_qvbias, full_proj, full_projbias, full_downbias, full_gains, full_biases = (
        lax.all_gather(qkv_weight, "wt", axis=0, tiled=True),
        lax.all_gather(qv_bias, "wt", axis=0, tiled=True),
        lax.all_gather(proj_weight, "wt", axis=0, tiled=True),
        lax.all_gather(proj_bias, "wt", axis=0, tiled=True),
        lax.all_gather(down_bias, "wt", axis=0, tiled=True),
        lax.all_gather(norm_gains, "wt", axis=1, tiled=True),
        lax.all_gather(norm_biases, "wt", axis=1, tiled=True),
    )
    gains = full_gains.astype(jnp.float32)
    shifts = full_biases.astype(jnp.float32)
    qvbias = full_qvbias.astype(jnp.float32)
    inputs = activations.reshape(token_count, model_width).astype(jnp.float32)
    normed_low = layer_norm(inputs, gains[0], shifts[0]).astype(jnp.bfloat16)
    projected = jnp.dot(normed_low, full_qkv, preferred_element_type=jnp.float32)
    query_low = ((projected[:, :model_width] + qvbias[:model_width]) * query_scale).astype(
        jnp.bfloat16
    )
    query_low = query_low.reshape(seq_count, shard_rows, model_width)
    key_low = (
        projected[:, model_width : 2 * model_width]
        .astype(jnp.bfloat16)
        .reshape(seq_count, shard_rows, model_width)
    )
    value_low = (projected[:, 2 * model_width :] + qvbias[model_width:]).astype(jnp.bfloat16)
    value_low = value_low.reshape(seq_count, shard_rows, model_width)
    query_heads = split_heads(query_low)
    my_device = lax.axis_index("ctx")
    my_pair = lax.dynamic_index_in_dim(block_order, 2 * my_device, keepdims=False)
    my_pos = pair_positions(block_order, my_device, half_rows)

    def attend_piece(running, pieces):
        key_piece, value_piece = pieces

        def attend_one_shard(shard_index, carried):
            key_heads = split_heads(rows_of(key_piece, shard_index))
            value_heads = split_heads(rows_of(value_piece, shard_index))
            their_pair = lax.dynamic_index_in_dim(block_order, 2 * shard_index, keepdims=False)
            key_pos = pair_positions(block_order, shard_index, half_rows)

            def attend_earlier(partial_stats):
                return combine_stats(
                    partial_stats,
                    tile_forward(
                        query_heads,
                        key_heads[:, :half_rows],
                        value_heads[:, :half_rows],
                        my_pos,
                        key_pos[:half_rows],
                    ),
                )

            def attend_later(partial_stats):
                upper_part = combine_stats(
                    upper_rows(partial_stats, half_rows),
                    tile_forward(
                        query_heads[:, half_rows:],
                        key_heads,
                        value_heads,
                        my_pos[half_rows:],
                        key_pos,
                    ),
                )
                return join_rows(partial_stats, upper_part, half_rows)

            def attend_diagonal(partial_stats):
                return combine_stats(
                    partial_stats,
                    tile_forward(query_heads, key_heads, value_heads, my_pos, key_pos),
                )

            case_index = jnp.where(their_pair < my_pair, 0, jnp.where(their_pair > my_pair, 1, 2))
            return lax.switch(case_index, [attend_earlier, attend_later, attend_diagonal], carried)

        return lax.fori_loop(0, key_piece.shape[1] // shard_rows, attend_one_shard, running)

    start_stats = (
        jnp.full((seq_count, head_count, shard_rows), -jnp.inf, jnp.float32),
        jnp.zeros((seq_count, head_count, shard_rows), jnp.float32),
        jnp.zeros((seq_count, shard_rows, head_count, head_dim), jnp.float32),
    )
    row_peak, row_total, summed = attend_piece(
        start_stats,
        (
            lax.all_gather(key_low, "ctx", axis=1, tiled=True),
            lax.all_gather(value_low, "ctx", axis=1, tiled=True),
        ),
    )
    attention = summed / jnp.transpose(row_total, (0, 2, 1))[..., None]
    log_total = row_peak + jnp.log(row_total)
    attended_low = attention.reshape(token_count, model_width).astype(jnp.bfloat16)
    proj_pre = jnp.dot(
        attended_low, full_proj, preferred_element_type=jnp.float32
    ) + full_projbias.astype(jnp.float32)
    residual = inputs + layer_norm(proj_pre, gains[1], shifts[1])
    normed_mid = layer_norm(residual, gains[2], shifts[2]).astype(jnp.bfloat16)
    downbias = full_downbias.astype(jnp.float32)
    up_full, upbias_full, down_full = (
        lax.all_gather(up_weight, "wt", axis=0, tiled=True),
        lax.all_gather(up_bias, "wt", axis=0, tiled=True),
        lax.all_gather(down_weight, "wt", axis=0, tiled=True),
    )
    pre_act = lax.dot_general(
        normed_mid, up_full, (((1,), (1,)), ((), ())), preferred_element_type=jnp.float32
    ) + upbias_full.astype(jnp.float32)
    hidden_low = gelu_tanh(pre_act).astype(jnp.bfloat16)
    branch_out = jnp.dot(hidden_low, down_full, preferred_element_type=jnp.float32) + downbias
    layer_output = (residual + layer_norm(branch_out, gains[3], shifts[3])).astype(jnp.bfloat16)
    upstream = cotangent.reshape(token_count, model_width).astype(jnp.float32)
    grad_branch, gain_three, shift_three = norm_backward(branch_out, gains[3], shifts[3], upstream)
    grad_branch_low = grad_branch.astype(jnp.bfloat16)
    grad_downbias = jnp.sum(grad_branch_low.astype(jnp.float32), axis=0)
    grad_downward = lax.dot_general(
        hidden_low, grad_branch_low, (((0,), (0,)), ((), ())), preferred_element_type=jnp.float32
    )
    grad_hidden = lax.dot_general(
        grad_branch_low, down_full, (((1,), (1,)), ((), ())), preferred_element_type=jnp.float32
    )
    grad_pre = gelu_backward(pre_act, grad_hidden).astype(jnp.bfloat16)
    grad_upbias = jnp.sum(grad_pre.astype(jnp.float32), axis=0)
    grad_upward = lax.dot_general(
        grad_pre, normed_mid, (((0,), (0,)), ((), ())), preferred_element_type=jnp.float32
    )
    grad_mid = jnp.dot(grad_pre, up_full, preferred_element_type=jnp.float32)
    grad_resid, gain_two, shift_two = norm_backward(residual, gains[2], shifts[2], grad_mid)
    grad_residual = upstream + grad_resid
    grad_proj_pre, gain_one, shift_one = norm_backward(proj_pre, gains[1], shifts[1], grad_residual)
    grad_proj_low = grad_proj_pre.astype(jnp.bfloat16)
    grad_projbias = jnp.sum(grad_proj_low.astype(jnp.float32), axis=0)
    grad_proj = lax.dot_general(
        attended_low, grad_proj_low, (((0,), (0,)), ((), ())), preferred_element_type=jnp.float32
    )
    grad_attn_low = lax.dot_general(
        grad_proj_low, full_proj, (((1,), (1,)), ((), ())), preferred_element_type=jnp.float32
    ).astype(jnp.bfloat16)
    grad_attn_low = grad_attn_low.reshape(seq_count, shard_rows, model_width)
    grad_heads = split_heads(grad_attn_low)
    row_shift = jnp.einsum("sqhd,sqhd->shq", grad_heads.astype(jnp.float32), attention)
    zero_heads = jnp.zeros((seq_count, shard_rows, head_count, head_dim), jnp.float32)

    def all_grads(running, pieces):
        key_piece, value_piece = pieces

        def all_one_shard(shard_index, carried):
            key_heads = split_heads(rows_of(key_piece, shard_index))
            value_heads = split_heads(rows_of(value_piece, shard_index))
            their_pair = lax.dynamic_index_in_dim(block_order, 2 * shard_index, keepdims=False)
            key_pos = pair_positions(block_order, shard_index, half_rows)
            slot_start = shard_index * shard_rows

            def all_earlier(accumulated):
                grad_now, key_sums, value_sums = accumulated
                grad_scores, probs_low = tile_backward(
                    query_heads,
                    grad_heads,
                    log_total,
                    row_shift,
                    key_heads[:, :half_rows],
                    value_heads[:, :half_rows],
                    my_pos,
                    key_pos[:half_rows],
                )
                grad_now = grad_now + jnp.einsum(
                    "shqk,skhd->sqhd",
                    grad_scores,
                    key_heads[:, :half_rows],
                    preferred_element_type=jnp.float32,
                )
                key_part = jnp.einsum(
                    "shqk,sqhd->skhd", grad_scores, query_heads, preferred_element_type=jnp.float32
                )
                value_part = jnp.einsum(
                    "shqk,sqhd->skhd", probs_low, grad_heads, preferred_element_type=jnp.float32
                )
                return (
                    grad_now,
                    add_slot(key_sums, key_part, slot_start),
                    add_slot(value_sums, value_part, slot_start),
                )

            def all_later(accumulated):
                grad_now, key_sums, value_sums = accumulated
                upper_query = query_heads[:, half_rows:]
                upper_grad = grad_heads[:, half_rows:]
                grad_scores, probs_low = tile_backward(
                    upper_query,
                    upper_grad,
                    log_total[:, :, half_rows:],
                    row_shift[:, :, half_rows:],
                    key_heads,
                    value_heads,
                    my_pos[half_rows:],
                    key_pos,
                )
                grad_now = grad_now.at[:, half_rows:].add(
                    jnp.einsum(
                        "shqk,skhd->sqhd",
                        grad_scores,
                        key_heads,
                        preferred_element_type=jnp.float32,
                    )
                )
                key_part = jnp.einsum(
                    "shqk,sqhd->skhd", grad_scores, upper_query, preferred_element_type=jnp.float32
                )
                value_part = jnp.einsum(
                    "shqk,sqhd->skhd", probs_low, upper_grad, preferred_element_type=jnp.float32
                )
                return (
                    grad_now,
                    add_slot(key_sums, key_part, slot_start),
                    add_slot(value_sums, value_part, slot_start),
                )

            def all_diagonal(accumulated):
                grad_now, key_sums, value_sums = accumulated
                grad_scores, probs_low = tile_backward(
                    query_heads,
                    grad_heads,
                    log_total,
                    row_shift,
                    key_heads,
                    value_heads,
                    my_pos,
                    key_pos,
                )
                grad_now = grad_now + jnp.einsum(
                    "shqk,skhd->sqhd", grad_scores, key_heads, preferred_element_type=jnp.float32
                )
                key_part = jnp.einsum(
                    "shqk,sqhd->skhd", grad_scores, query_heads, preferred_element_type=jnp.float32
                )
                value_part = jnp.einsum(
                    "shqk,sqhd->skhd", probs_low, grad_heads, preferred_element_type=jnp.float32
                )
                return (
                    grad_now,
                    add_slot(key_sums, key_part, slot_start),
                    add_slot(value_sums, value_part, slot_start),
                )

            case_index = jnp.where(their_pair < my_pair, 0, jnp.where(their_pair > my_pair, 1, 2))
            return lax.switch(case_index, [all_earlier, all_later, all_diagonal], carried)

        return lax.fori_loop(0, key_piece.shape[1] // shard_rows, all_one_shard, running)

    zero_whole = jnp.zeros(
        (seq_count, shard_rows * lax.axis_size("ctx"), head_count, head_dim), jnp.float32
    )
    grad_query, key_sums, value_sums = all_grads(
        (zero_heads, zero_whole, zero_whole),
        (
            lax.all_gather(key_low, "ctx", axis=1, tiled=True),
            lax.all_gather(value_low, "ctx", axis=1, tiled=True),
        ),
    )
    grad_key, grad_value = (
        lax.psum_scatter(
            key_sums.astype(jnp.bfloat16), "ctx", scatter_dimension=1, tiled=True
        ).astype(jnp.float32),
        lax.psum_scatter(
            value_sums.astype(jnp.bfloat16), "ctx", scatter_dimension=1, tiled=True
        ).astype(jnp.float32),
    )
    grad_query_low = (
        (grad_query * query_scale).astype(jnp.bfloat16).reshape(token_count, model_width)
    )
    grad_key_low = grad_key.astype(jnp.bfloat16).reshape(token_count, model_width)
    grad_value_low = grad_value.astype(jnp.bfloat16).reshape(token_count, model_width)
    grad_qkv_low = jnp.concatenate([grad_query_low, grad_key_low, grad_value_low], axis=1)
    grad_qkv = lax.dot_general(
        normed_low, grad_qkv_low, (((0,), (0,)), ((), ())), preferred_element_type=jnp.float32
    )
    grad_qvbias = jnp.concatenate(
        [
            jnp.sum(grad_query_low.astype(jnp.float32), axis=0),
            jnp.sum(grad_value_low.astype(jnp.float32), axis=0),
        ]
    )
    grad_normed = lax.dot_general(
        grad_qkv_low, full_qkv, (((1,), (1,)), ((), ())), preferred_element_type=jnp.float32
    )
    grad_inputs, gain_zero, shift_zero = norm_backward(inputs, gains[0], shifts[0], grad_normed)
    input_grad = (grad_residual + grad_inputs).reshape(seq_count, shard_rows, model_width)
    grad_gains = jnp.stack([gain_zero, gain_one, gain_two, gain_three])
    grad_biases = jnp.stack([shift_zero, shift_one, shift_two, shift_three])
    (
        grad_qkv,
        grad_qvbias,
        grad_proj,
        grad_projbias,
        grad_downbias,
        grad_gains,
        grad_biases,
        grad_upward,
        grad_upbias,
        grad_downward,
    ) = (
        lax.psum_scatter(
            grad_qkv.astype(jnp.bfloat16), "wt", scatter_dimension=0, tiled=True
        ).astype(jnp.float32),
        lax.psum_scatter(
            grad_qvbias.astype(jnp.bfloat16), "wt", scatter_dimension=0, tiled=True
        ).astype(jnp.float32),
        lax.psum_scatter(
            grad_proj.astype(jnp.bfloat16), "wt", scatter_dimension=0, tiled=True
        ).astype(jnp.float32),
        lax.psum_scatter(
            grad_projbias.astype(jnp.bfloat16), "wt", scatter_dimension=0, tiled=True
        ).astype(jnp.float32),
        lax.psum_scatter(
            grad_downbias.astype(jnp.bfloat16), "wt", scatter_dimension=0, tiled=True
        ).astype(jnp.float32),
        lax.psum_scatter(
            grad_gains.astype(jnp.bfloat16), "wt", scatter_dimension=1, tiled=True
        ).astype(jnp.float32),
        lax.psum_scatter(
            grad_biases.astype(jnp.bfloat16), "wt", scatter_dimension=1, tiled=True
        ).astype(jnp.float32),
        lax.psum_scatter(
            grad_upward.astype(jnp.bfloat16), "wt", scatter_dimension=0, tiled=True
        ).astype(jnp.float32),
        lax.psum_scatter(
            grad_upbias.astype(jnp.bfloat16), "wt", scatter_dimension=0, tiled=True
        ).astype(jnp.float32),
        lax.psum_scatter(
            grad_downward.astype(jnp.bfloat16), "wt", scatter_dimension=0, tiled=True
        ).astype(jnp.float32),
    )
    (
        grad_qkv,
        grad_qvbias,
        grad_proj,
        grad_projbias,
        grad_upward,
        grad_upbias,
        grad_downward,
        grad_downbias,
        grad_gains,
        grad_biases,
    ) = (
        lax.psum(grad_qkv.astype(jnp.bfloat16), "ctx").astype(jnp.float32),
        lax.psum(grad_qvbias.astype(jnp.bfloat16), "ctx").astype(jnp.float32),
        lax.psum(grad_proj.astype(jnp.bfloat16), "ctx").astype(jnp.float32),
        lax.psum(grad_projbias.astype(jnp.bfloat16), "ctx").astype(jnp.float32),
        lax.psum(grad_upward.astype(jnp.bfloat16), "ctx").astype(jnp.float32),
        lax.psum(grad_upbias.astype(jnp.bfloat16), "ctx").astype(jnp.float32),
        lax.psum(grad_downward.astype(jnp.bfloat16), "ctx").astype(jnp.float32),
        lax.psum(grad_downbias.astype(jnp.bfloat16), "ctx").astype(jnp.float32),
        lax.psum(grad_gains.astype(jnp.bfloat16), "ctx").astype(jnp.float32),
        lax.psum(grad_biases.astype(jnp.bfloat16), "ctx").astype(jnp.float32),
    )
    return (
        layer_output.reshape(seq_count, shard_rows, model_width),
        input_grad,
        grad_qkv,
        grad_qvbias,
        grad_proj,
        grad_projbias,
        grad_upward,
        grad_upbias,
        grad_downward,
        grad_downbias,
        grad_gains,
        grad_biases,
    )


def solution(mesh):
    return jax.shard_map(
        local,
        mesh=mesh,
        in_specs=(
            P("wt", "ctx", None),
            P(),
            P("wt", None),
            P("wt"),
            P("wt", None),
            P("wt"),
            P("wt", None),
            P("wt"),
            P("wt", None),
            P("wt"),
            P(None, "wt"),
            P(None, "wt"),
            P("wt", "ctx", None),
        ),
        out_specs=(
            P("wt", "ctx", None),
            P("wt", "ctx", None),
            P("wt", None),
            P("wt"),
            P("wt", None),
            P("wt"),
            P("wt", None),
            P("wt"),
            P("wt", None),
            P("wt"),
            P(None, "wt"),
            P(None, "wt"),
        ),
        check_vma=False,
    )
```

profile of v0, /device:TPU:13, one launch (start us, length us, event | category | flops | bytes accessed | tf_op | source)
XLA Modules:
  0.0 4843.1 jit_solution(4239791513970785047)
XLA Ops:
  23.2 68.0 %all-gather.11.cloned.1.call-done = bf16[1024,3072]{1,0:T(8,128)(2,1)} async-done(((bf16[512,3072]{1,0:T(8,128)(2,1)}), bf16[1024,3072]{1,0:T(8,128)(2,1)}) %all-gather.11.cloned.1.call-update) | async-done | bytes 6291472 | tf_op jit(solution)/shard_map/all_gather | solution.py:143
  134.4 140.2 %all-gather.21.cloned.1.call-done = bf16[16384,1024]{1,0:T(8,128)(2,1)} async-done(((bf16[1024,1024]{1,0:T(8,128)(2,1)}), bf16[16384,1024]{1,0:T(8,128)(2,1)}) %all-gather.21.cloned.1.call-update) | async-done | bytes 33554448 | tf_op jit(solution)/shard_map/all_gather | solution.py:227
  315.1 129.8 %all-gather.19.cloned.1.call-done = bf16[16384,1024]{1,0:T(8,128)(2,1)} async-done(((bf16[1024,1024]{1,0:T(8,128)(2,1)}), bf16[16384,1024]{1,0:T(8,128)(2,1)}) %all-gather.19.cloned.1.call-update) | async-done | bytes 33554448 | tf_op jit(solution)/shard_map/all_gather | solution.py:226
  491.9 1079.3 %while.37 = (s32[]{:T(128)}, f32[1,16,1024]{2,1,0:T(8,128)S(1)}, f32[1,16,1024]{2,1,0:T(8,128)S(1)}, f32[1,1024,16,64]{1,3,2,0:T(8,128)}, s32[32]{0:T(128)}, /*i...) while((s32[]{:T(128)}, f32[1,16,1024]{2,1,0:T(8,128)S(1)}, ...), condition=%wide.region_12.13_spmd.clone, body=%wide.region_2.12_spmd.clone.sunk | while | flops 4483794944 | bytes 229857920 | solution.py:216
  503.5 56.2 %conditional.6 = (f32[1,16,1024]{2,1,0:T(8,128)}, f32[1,16,1024]{2,1,0:T(8,128)S(1)}, f32[1,1024,16,64]{1,3,2,0:T(8,128)}) conditional(s32[]{:T(128)} %clamp.18, (s32[1024]{0:T(1024)}, s32[512]{0:T(512)S(1)}, bf16[1,1024,16,64]{1,3,2,0:T(8,128)(2,1)S(1)}, bf16[1,1024,16,64]{1,3,2,0:T(8,128)(2,1)}, f32[1,16,1024]{2,1,0:T(8,128)S(1)}, ...), branch_computations={%region_3.5_spmd, %region_6.8_spmd, %region_9.11_spmd} | conditional | flops 4483792896 | bytes 221323296 | solution.py:214
  695.8 56.2 %conditional.6 = (f32[1,16,1024]{2,1,0:T(8,128)}, f32[1,16,1024]{2,1,0:T(8,128)S(1)}, f32[1,1024,16,64]{1,3,2,0:T(8,128)}) conditional(s32[]{:T(128)} %clamp.18, (s32[1024]{0:T(1024)}, s32[512]{0:T(512)S(1)}, bf16[1,1024,16,64]{1,3,2,0:T(8,128)(2,1)S(1)}, bf16[1,1024,16,64]{1,3,2,0:T(8,128)(2,1)}, f32[1,16,1024]{2,1,0:T(8,128)S(1)}, ...), branch_computations={%region_3.5_spmd, %region_6.8_spmd, %region_9.11_spmd} | conditional | flops 4483792896 | bytes 221323296 | solution.py:214
  886.0 56.2 %conditional.6 = (f32[1,16,1024]{2,1,0:T(8,128)}, f32[1,16,1024]{2,1,0:T(8,128)S(1)}, f32[1,1024,16,64]{1,3,2,0:T(8,128)}) conditional(s32[]{:T(128)} %clamp.18, (s32[1024]{0:T(1024)}, s32[512]{0:T(512)S(1)}, bf16[1,1024,16,64]{1,3,2,0:T(8,128)(2,1)S(1)}, bf16[1,1024,16,64]{1,3,2,0:T(8,128)(2,1)}, f32[1,16,1024]{2,1,0:T(8,128)S(1)}, ...), branch_computations={%region_3.5_spmd, %region_6.8_spmd, %region_9.11_spmd} | conditional | flops 4483792896 | bytes 221323296 | solution.py:214
  954.0 77.6 %conditional.6 = (f32[1,16,1024]{2,1,0:T(8,128)}, f32[1,16,1024]{2,1,0:T(8,128)S(1)}, f32[1,1024,16,64]{1,3,2,0:T(8,128)}) conditional(s32[]{:T(128)} %clamp.18, (s32[1024]{0:T(1024)}, s32[512]{0:T(512)S(1)}, bf16[1,1024,16,64]{1,3,2,0:T(8,128)(2,1)S(1)}, bf16[1,1024,16,64]{1,3,2,0:T(8,128)(2,1)}, f32[1,16,1024]{2,1,0:T(8,128)S(1)}, ...), branch_computations={%region_3.5_spmd, %region_6.8_spmd, %region_9.11_spmd} | conditional | flops 4483792896 | bytes 221323296 | solution.py:214
  1111.4 56.2 %conditional.6 = (f32[1,16,1024]{2,1,0:T(8,128)}, f32[1,16,1024]{2,1,0:T(8,128)S(1)}, f32[1,1024,16,64]{1,3,2,0:T(8,128)}) conditional(s32[]{:T(128)} %clamp.18, (s32[1024]{0:T(1024)}, s32[512]{0:T(512)S(1)}, bf16[1,1024,16,64]{1,3,2,0:T(8,128)(2,1)S(1)}, bf16[1,1024,16,64]{1,3,2,0:T(8,128)(2,1)}, f32[1,16,1024]{2,1,0:T(8,128)S(1)}, ...), branch_computations={%region_3.5_spmd, %region_6.8_spmd, %region_9.11_spmd} | conditional | flops 4483792896 | bytes 221323296 | solution.py:214
  1750.9 1653.8 %while.38 = (s32[]{:T(128)}, f32[1,1024,16,64]{1,3,2,0:T(8,128)}, f32[1,16384,16,64]{1,3,2,0:T(8,128)}, f32[1,16384,16,64]{1,3,2,0:T(8,128)}, s32[32]{0:T(128)},...) while((s32[]{:T(128)}, f32[1,1024,16,64]{1,3,2,0:T(8,128)}, ...), condition=%wide.region_29.30_spmd.clone, body=%wide.region_25.29_spmd.clone.sunk | while | flops 10926163968 | bytes 370367328 | solution.py:386
  1762.2 83.8 %conditional.7 = (f32[1,1024,16,64]{1,3,2,0:T(8,128)}, f32[1,16384,16,64]{1,3,2,0:T(8,128)}, f32[1,16384,16,64]{1,3,2,0:T(8,128)}) conditional(s32[]{:T(128)} %clamp.19, (s32[1024]{0:T(1024)}, s32[512]{0:T(512)S(1)}, bf16[1,1024,16,64]{1,3,2,0:T(8,128)(2,1)S(1)}, bf16[1,1024,16,64]{1,3,2,0:T(8,128)(2,1)}, ...), branch_computations={%region_26.26_spmd, %region_27.27_spmd, %region_28.28_spmd} | conditional | flops 10926161920 | bytes 361963680 | solution.py:384
  1866.2 79.7 %conditional.7 = (f32[1,1024,16,64]{1,3,2,0:T(8,128)}, f32[1,16384,16,64]{1,3,2,0:T(8,128)}, f32[1,16384,16,64]{1,3,2,0:T(8,128)}) conditional(s32[]{:T(128)} %clamp.19, (s32[1024]{0:T(1024)}, s32[512]{0:T(512)S(1)}, bf16[1,1024,16,64]{1,3,2,0:T(8,128)(2,1)S(1)}, bf16[1,1024,16,64]{1,3,2,0:T(8,128)(2,1)}, ...), branch_computations={%region_26.26_spmd, %region_27.27_spmd, %region_28.28_spmd} | conditional | flops 10926161920 | bytes 361963680 | solution.py:384
  1965.8 78.6 %conditional.7 = (f32[1,1024,16,64]{1,3,2,0:T(8,128)}, f32[1,16384,16,64]{1,3,2,0:T(8,128)}, f32[1,16384,16,64]{1,3,2,0:T(8,128)}) conditional(s32[]{:T(128)} %clamp.19, (s32[1024]{0:T(1024)}, s32[512]{0:T(512)S(1)}, bf16[1,1024,16,64]{1,3,2,0:T(8,128)(2,1)S(1)}, bf16[1,1024,16,64]{1,3,2,0:T(8,128)(2,1)}, ...), branch_computations={%region_26.26_spmd, %region_27.27_spmd, %region_28.28_spmd} | conditional | flops 10926161920 | bytes 361963680 | solution.py:384
  2055.5 83.6 %conditional.7 = (f32[1,1024,16,64]{1,3,2,0:T(8,128)}, f32[1,16384,16,64]{1,3,2,0:T(8,128)}, f32[1,16384,16,64]{1,3,2,0:T(8,128)}) conditional(s32[]{:T(128)} %clamp.19, (s32[1024]{0:T(1024)}, s32[512]{0:T(512)S(1)}, bf16[1,1024,16,64]{1,3,2,0:T(8,128)(2,1)S(1)}, bf16[1,1024,16,64]{1,3,2,0:T(8,128)(2,1)}, ...), branch_computations={%region_26.26_spmd, %region_27.27_spmd, %region_28.28_spmd} | conditional | flops 10926161920 | bytes 361963680 | solution.py:384
  2159.0 79.8 %conditional.7 = (f32[1,1024,16,64]{1,3,2,0:T(8,128)}, f32[1,16384,16,64]{1,3,2,0:T(8,128)}, f32[1,16384,16,64]{1,3,2,0:T(8,128)}) conditional(s32[]{:T(128)} %clamp.19, (s32[1024]{0:T(1024)}, s32[512]{0:T(512)S(1)}, bf16[1,1024,16,64]{1,3,2,0:T(8,128)(2,1)S(1)}, bf16[1,1024,16,64]{1,3,2,0:T(8,128)(2,1)}, ...), branch_computations={%region_26.26_spmd, %region_27.27_spmd, %region_28.28_spmd} | conditional | flops 10926161920 | bytes 361963680 | solution.py:384
  2250.1 78.8 %conditional.7 = (f32[1,1024,16,64]{1,3,2,0:T(8,128)}, f32[1,16384,16,64]{1,3,2,0:T(8,128)}, f32[1,16384,16,64]{1,3,2,0:T(8,128)}) conditional(s32[]{:T(128)} %clamp.19, (s32[1024]{0:T(1024)}, s32[512]{0:T(512)S(1)}, bf16[1,1024,16,64]{1,3,2,0:T(8,128)(2,1)S(1)}, bf16[1,1024,16,64]{1,3,2,0:T(8,128)(2,1)}, ...), branch_computations={%region_26.26_spmd, %region_27.27_spmd, %region_28.28_spmd} | conditional | flops 10926161920 | bytes 361963680 | solution.py:384
  2340.1 83.7 %conditional.7 = (f32[1,1024,16,64]{1,3,2,0:T(8,128)}, f32[1,16384,16,64]{1,3,2,0:T(8,128)}, f32[1,16384,16,64]{1,3,2,0:T(8,128)}) conditional(s32[]{:T(128)} %clamp.19, (s32[1024]{0:T(1024)}, s32[512]{0:T(512)S(1)}, bf16[1,1024,16,64]{1,3,2,0:T(8,128)(2,1)S(1)}, bf16[1,1024,16,64]{1,3,2,0:T(8,128)(2,1)}, ...), branch_computations={%region_26.26_spmd, %region_27.27_spmd, %region_28.28_spmd} | conditional | flops 10926161920 | bytes 361963680 | solution.py:384
  2444.1 141.4 %conditional.7 = (f32[1,1024,16,64]{1,3,2,0:T(8,128)}, f32[1,16384,16,64]{1,3,2,0:T(8,128)}, f32[1,16384,16,64]{1,3,2,0:T(8,128)}) conditional(s32[]{:T(128)} %clamp.19, (s32[1024]{0:T(1024)}, s32[512]{0:T(512)S(1)}, bf16[1,1024,16,64]{1,3,2,0:T(8,128)(2,1)S(1)}, bf16[1,1024,16,64]{1,3,2,0:T(8,128)(2,1)}, ...), branch_computations={%region_26.26_spmd, %region_27.27_spmd, %region_28.28_spmd} | conditional | flops 10926161920 | bytes 361963680 | solution.py:384
  2605.4 83.7 %conditional.7 = (f32[1,1024,16,64]{1,3,2,0:T(8,128)}, f32[1,16384,16,64]{1,3,2,0:T(8,128)}, f32[1,16384,16,64]{1,3,2,0:T(8,128)}) conditional(s32[]{:T(128)} %clamp.19, (s32[1024]{0:T(1024)}, s32[512]{0:T(512)S(1)}, bf16[1,1024,16,64]{1,3,2,0:T(8,128)(2,1)S(1)}, bf16[1,1024,16,64]{1,3,2,0:T(8,128)(2,1)}, ...), branch_computations={%region_26.26_spmd, %region_27.27_spmd, %region_28.28_spmd} | conditional | flops 10926161920 | bytes 361963680 | solution.py:384
  2709.4 84.2 %conditional.7 = (f32[1,1024,16,64]{1,3,2,0:T(8,128)}, f32[1,16384,16,64]{1,3,2,0:T(8,128)}, f32[1,16384,16,64]{1,3,2,0:T(8,128)}) conditional(s32[]{:T(128)} %clamp.19, (s32[1024]{0:T(1024)}, s32[512]{0:T(512)S(1)}, bf16[1,1024,16,64]{1,3,2,0:T(8,128)(2,1)S(1)}, bf16[1,1024,16,64]{1,3,2,0:T(8,128)(2,1)}, ...), branch_computations={%region_26.26_spmd, %region_27.27_spmd, %region_28.28_spmd} | conditional | flops 10926161920 | bytes 361963680 | solution.py:384
  2813.4 83.8 %conditional.7 = (f32[1,1024,16,64]{1,3,2,0:T(8,128)}, f32[1,16384,16,64]{1,3,2,0:T(8,128)}, f32[1,16384,16,64]{1,3,2,0:T(8,128)}) conditional(s32[]{:T(128)} %clamp.19, (s32[1024]{0:T(1024)}, s32[512]{0:T(512)S(1)}, bf16[1,1024,16,64]{1,3,2,0:T(8,128)(2,1)S(1)}, bf16[1,1024,16,64]{1,3,2,0:T(8,128)(2,1)}, ...), branch_computations={%region_26.26_spmd, %region_27.27_spmd, %region_28.28_spmd} | conditional | flops 10926161920 | bytes 361963680 | solution.py:384
  2917.5 83.8 %conditional.7 = (f32[1,1024,16,64]{1,3,2,0:T(8,128)}, f32[1,16384,16,64]{1,3,2,0:T(8,128)}, f32[1,16384,16,64]{1,3,2,0:T(8,128)}) conditional(s32[]{:T(128)} %clamp.19, (s32[1024]{0:T(1024)}, s32[512]{0:T(512)S(1)}, bf16[1,1024,16,64]{1,3,2,0:T(8,128)(2,1)S(1)}, bf16[1,1024,16,64]{1,3,2,0:T(8,128)(2,1)}, ...), branch_computations={%region_26.26_spmd, %region_27.27_spmd, %region_28.28_spmd} | conditional | flops 10926161920 | bytes 361963680 | solution.py:384
  3021.1 83.7 %conditional.7 = (f32[1,1024,16,64]{1,3,2,0:T(8,128)}, f32[1,16384,16,64]{1,3,2,0:T(8,128)}, f32[1,16384,16,64]{1,3,2,0:T(8,128)}) conditional(s32[]{:T(128)} %clamp.19, (s32[1024]{0:T(1024)}, s32[512]{0:T(512)S(1)}, bf16[1,1024,16,64]{1,3,2,0:T(8,128)(2,1)S(1)}, bf16[1,1024,16,64]{1,3,2,0:T(8,128)(2,1)}, ...), branch_computations={%region_26.26_spmd, %region_27.27_spmd, %region_28.28_spmd} | conditional | flops 10926161920 | bytes 361963680 | solution.py:384
  3125.1 83.9 %conditional.7 = (f32[1,1024,16,64]{1,3,2,0:T(8,128)}, f32[1,16384,16,64]{1,3,2,0:T(8,128)}, f32[1,16384,16,64]{1,3,2,0:T(8,128)}) conditional(s32[]{:T(128)} %clamp.19, (s32[1024]{0:T(1024)}, s32[512]{0:T(512)S(1)}, bf16[1,1024,16,64]{1,3,2,0:T(8,128)(2,1)S(1)}, bf16[1,1024,16,64]{1,3,2,0:T(8,128)(2,1)}, ...), branch_computations={%region_26.26_spmd, %region_27.27_spmd, %region_28.28_spmd} | conditional | flops 10926161920 | bytes 361963680 | solution.py:384
  3228.9 79.8 %conditional.7 = (f32[1,1024,16,64]{1,3,2,0:T(8,128)}, f32[1,16384,16,64]{1,3,2,0:T(8,128)}, f32[1,16384,16,64]{1,3,2,0:T(8,128)}) conditional(s32[]{:T(128)} %clamp.19, (s32[1024]{0:T(1024)}, s32[512]{0:T(512)S(1)}, bf16[1,1024,16,64]{1,3,2,0:T(8,128)(2,1)S(1)}, bf16[1,1024,16,64]{1,3,2,0:T(8,128)(2,1)}, ...), branch_computations={%region_26.26_spmd, %region_27.27_spmd, %region_28.28_spmd} | conditional | flops 10926161920 | bytes 361963680 | solution.py:384
  3319.9 78.8 %conditional.7 = (f32[1,1024,16,64]{1,3,2,0:T(8,128)}, f32[1,16384,16,64]{1,3,2,0:T(8,128)}, f32[1,16384,16,64]{1,3,2,0:T(8,128)}) conditional(s32[]{:T(128)} %clamp.19, (s32[1024]{0:T(1024)}, s32[512]{0:T(512)S(1)}, bf16[1,1024,16,64]{1,3,2,0:T(8,128)(2,1)S(1)}, bf16[1,1024,16,64]{1,3,2,0:T(8,128)(2,1)}, ...), branch_computations={%region_26.26_spmd, %region_27.27_spmd, %region_28.28_spmd} | conditional | flops 10926161920 | bytes 361963680 | solution.py:384
  3512.3 386.4 %reduce-scatter.15.cloned.1.call-done = bf16[1,1024,16,64]{1,3,2,0:T(8,128)(2,1)} async-done(((bf16[1,16384,16,64]{1,3,2,0:T(8,128)(2,1)}), bf16[1,1024,16,64]{1,3,2,0:T(8,128)(2,1)}) %reduce-scatter.15.cloned.1.call-update) | async-done | bytes 2097168 | tf_op jit(solution)/shard_map/reduce_scatter | solution.py:402
  3898.8 336.0 %reduce-scatter.13.cloned.1.call-done = bf16[1,1024,16,64]{1,3,2,0:T(8,128)(2,1)} async-done(((bf16[1,16384,16,64]{1,3,2,0:T(8,128)(2,1)}), bf16[1,1024,16,64]{1,3,2,0:T(8,128)(2,1)}) %reduce-scatter.13.cloned.1.call-update) | async-done | bytes 2097168 | tf_op jit(solution)/shard_map/reduce_scatter | solution.py:399
  4274.9 96.3 %reduce-scatter.23.cloned.1.call-done = bf16[2048,1024]{1,0:T(8,128)(2,1)} async-done(((bf16[4096,1024]{1,0:T(8,128)(2,1)}), bf16[2048,1024]{1,0:T(8,128)(2,1)}) %reduce-scatter.23.cloned.1.call-update) | async-done | bytes 4194320 | tf_op jit(solution)/shard_map/reduce_scatter | solution.py:467
  4371.2 102.2 %reduce-scatter.21.cloned.1.call-done = bf16[2048,1024]{1,0:T(8,128)(2,1)} async-done(((bf16[4096,1024]{1,0:T(8,128)(2,1)}), bf16[2048,1024]{1,0:T(8,128)(2,1)}) %reduce-scatter.21.cloned.1.call-update) | async-done | bytes 4194320 | tf_op jit(solution)/shard_map/reduce_scatter | solution.py:461
  4473.3 79.9 %reduce-scatter.17.cloned.1.call-done = bf16[512,3072]{1,0:T(8,128)(2,1)} async-done(((bf16[1024,3072]{1,0:T(8,128)(2,1)}), bf16[512,3072]{1,0:T(8,128)(2,1)}) %reduce-scatter.17.cloned.1.call-update) | async-done | bytes 3145744 | tf_op jit(solution)/shard_map/reduce_scatter | solution.py:440
  4632.8 188.0 %all-reduce.9.cloned.1.call-done = (bf16[512,3072]{1,0:T(8,128)(2,1)}, bf16[512,1024]{1,0:T(8,128)(2,1)}, bf16[2048,1024]{1,0:T(8,128)(2,1)}, bf16[2048,1024]{1,0:T(8,128)(2,1)}) async-done(((bf16[512,3072]{1,0:T(8,128)(2,1)}, bf16[512,1024]{1,0:T(8,128)(2,1)}, bf16[2048,1024]{1,0:T(8,128)(2,1)}, bf16[2048,1024]{1,0:T(8,128)(2,1)}), (bf16[512,3072]{1,0:T(8,128)(2,1)}, bf16[512,1024]{1,0:T(8,128)(2,1)}, ...) | async-done | bytes 12582928 | tf_op jit(solution)/shard_map/psum | solution.py:483
  (875 shorter events, 3583.1 us)
Async XLA Ops:
  7.2 84.0 %all-gather.11.cloned.1.call-start = ((), (), s32[]{:S(2)}) async-start(), calls=%async_computation.8 | async-start | bytes 9437184 | tf_op jit(solution)/shard_map/all_gather | solution.py:143
  7.9 266.7 %all-gather.21.cloned.1.call-start = ((), (), s32[]{:S(2)}) async-start(), calls=%async_computation.19 | async-start | bytes 35651584 | tf_op jit(solution)/shard_map/all_gather | solution.py:227
  10.9 89.6 %copy-start.8 = (bf16[1,1024,1024]{1,2,0:T(8,128)(2,1)}, bf16[1,1024,1024]{1,2,0:T(8,128)(2,1)S(1)}, u32[]{:S(2)}) copy-start(bf16[1,1024,1024]{1,2,0:T(8,128)(2,1)S(1)} %copy.58) | copy-start | bytes 6291460
  20.8 79.7 %copy-start.33 = (f32[1024]{0:T(1024)}, f32[1024]{0:T(1024)S(1)}, u32[]{:S(2)}) copy-start(f32[1024]{0:T(1024)S(1)} %broadcast_multiply_fusion.3) | copy-start | bytes 12292
  21.4 79.1 %copy-start.44 = (f32[1024]{0:T(1024)}, f32[1024]{0:T(1024)S(1)}, u32[]{:S(2)}) copy-start(f32[1024]{0:T(1024)S(1)} %fusion.168) | copy-start | bytes 12292
  22.6 77.9 %copy-start.63 = (f32[1,1024]{1,0:T(1,128)}, f32[1,1024]{1,0:T(1,128)S(1)}, u32[]{:S(2)}) copy-start(f32[1,1024]{1,0:T(1,128)S(1)} %get-tuple-element.958) | copy-start | bytes 12292
  23.2 77.3 %copy-start.41 = (f32[1,1024]{1,0:T(1,128)}, f32[1,1024]{1,0:T(1,128)S(1)}, u32[]{:S(2)}) copy-start(f32[1,1024]{1,0:T(1,128)S(1)} %get-tuple-element.954) | copy-start | bytes 12292
  106.3 338.6 %all-gather.19.cloned.1.call-start = ((), (), s32[]{:S(2)}) async-start(), calls=%async_computation.18 | async-start | bytes 35651584 | tf_op jit(solution)/shard_map/all_gather | solution.py:226
  110.3 1465.8 %all-gather.13.cloned.1.call-start = ((), (), s32[]{:S(2)}) async-start(), calls=%async_computation.9 | async-start | bytes 3145728 | tf_op jit(solution)/shard_map/all_gather | solution.py:145
  110.9 1477.6 %all-gather.15.cloned.1.call-start = ((), (), s32[]{:S(2)}) async-start(), calls=%async_computation.10 | async-start | bytes 12582912 | tf_op jit(solution)/shard_map/all_gather | solution.py:240
  111.5 1499.5 %all-gather.17.cloned.1.call-start = ((), (), s32[]{:S(2)}) async-start(), calls=%async_computation.11 | async-start | bytes 12582912 | tf_op jit(solution)/shard_map/all_gather | solution.py:242
  112.1 3786.7 %reduce-scatter.15.cloned.1.call-start = ((), (), s32[]{:S(2)}) async-start(), calls=%async_computation.13 | async-start | bytes 35651584 | tf_op jit(solution)/shard_map/reduce_scatter | solution.py:402
  1585.4 106.9 %copy-start.35 = (f32[1024]{0:T(1024)}, f32[1024]{0:T(1024)S(1)}, u32[]{:S(2)}) copy-start(f32[1024]{0:T(1024)S(1)} %broadcast_multiply_fusion.1) | copy-start | bytes 12292
  1587.9 104.5 %copy-start.46 = (f32[1024]{0:T(1024)}, f32[1024]{0:T(1024)S(1)}, u32[]{:S(2)}) copy-start(f32[1024]{0:T(1024)S(1)} %fusion.170) | copy-start | bytes 12292
  1981.5 23.2 copy-start.2
  2174.7 23.2 copy-start.2
  2454.2 25.0 copy-start.18
  2454.2 25.0 copy-start.30
  3335.6 23.2 copy-start.2
  3437.0 797.8 %reduce-scatter.13.cloned.1.call-start = ((), (), s32[]{:S(2)}) async-start(), calls=%async_computation.12 | async-start | bytes 35651584 | tf_op jit(solution)/shard_map/reduce_scatter | solution.py:399
  3469.3 805.5 %reduce-scatter.19.cloned.1.call-start = ((), (), s32[]{:S(2)}) async-start(), calls=%async_computation.15 | async-start | bytes 3145728 | tf_op jit(solution)/shard_map/reduce_scatter | solution.py:446
  3476.2 894.9 %reduce-scatter.23.cloned.1.call-start = ((), (), s32[]{:S(2)}) async-start(), calls=%async_computation.17 | async-start | bytes 12582912 | tf_op jit(solution)/shard_map/reduce_scatter | solution.py:467
  3491.5 981.9 %reduce-scatter.21.cloned.1.call-start = ((), (), s32[]{:S(2)}) async-start(), calls=%async_computation.16 | async-start | bytes 12582912 | tf_op jit(solution)/shard_map/reduce_scatter | solution.py:461
  3508.3 726.5 %copy-start.10 = (bf16[1,1024,1024]{1,2,0:T(8,128)(2,1)S(1)}, bf16[1,1024,1024]{1,2,0:T(8,128)(2,1)}, u32[]{:S(2)}) copy-start(bf16[1,1024,1024]{1,2,0:T(8,128)(2,1)} %copy-done.8) | copy-start | bytes 6291460
  3508.3 726.5 %copy-start.34 = (f32[1024]{0:T(1024)S(1)}, f32[1024]{0:T(1024)}, u32[]{:S(2)}) copy-start(f32[1024]{0:T(1024)} %copy-done.33) | copy-start | bytes 12292
  3508.3 726.5 %copy-start.42 = (f32[1,1024]{1,0:T(1,128)S(1)}, f32[1,1024]{1,0:T(1,128)}, u32[]{:S(2)}) copy-start(f32[1,1024]{1,0:T(1,128)} %copy-done.41) | copy-start | bytes 12292
  3508.3 726.5 %copy-start.45 = (f32[1024]{0:T(1024)S(1)}, f32[1024]{0:T(1024)}, u32[]{:S(2)}) copy-start(f32[1024]{0:T(1024)} %copy-done.44) | copy-start | bytes 12292
  3508.3 726.5 %copy-start.64 = (f32[1,1024]{1,0:T(1,128)S(1)}, f32[1,1024]{1,0:T(1,128)}, u32[]{:S(2)}) copy-start(f32[1,1024]{1,0:T(1,128)} %copy-done.63) | copy-start | bytes 12292
  3508.3 1045.0 %reduce-scatter.17.cloned.1.call-start = ((), (), s32[]{:S(2)}) async-start(), calls=%async_computation.14 | async-start | bytes 9437184 | tf_op jit(solution)/shard_map/reduce_scatter | solution.py:440
  4247.3 333.0 %reduce-scatter.27.cloned.1.call-start = ((), (), s32[]{:S(2)}) async-start(), calls=%async_computation.21 | async-start | bytes 393216
  4273.8 307.9 %reduce-scatter.25.cloned.1.call-start = ((), (), s32[]{:S(2)}) async-start(), calls=%async_computation.20 | async-start | bytes 393216
  4274.8 546.0 %all-reduce.9.cloned.1.call-start = ((), (), s32[]{:S(2)}) async-start(), calls=%async_computation.22 | async-start | bytes 25165824 | tf_op jit(solution)/shard_map/psum | solution.py:483
  (94 other events, 1009.3 us)
Sparse Core Ops, SparseCore 0:
  9.6 81.5 all-gather.10
  106.5 168.1 all-gather.20
  276.8 168.0 all-gather.18
  446.3 33.0 all-gather.12
  480.7 104.0 all-gather.14
  586.2 104.0 all-gather.16
  3437.1 461.6 reduce-scatter.14
  3903.0 331.7 reduce-scatter.12
  4237.0 32.5 reduce-scatter.18
  4271.9 99.2 reduce-scatter.22
  4374.1 99.2 reduce-scatter.20
  4476.2 77.0 reduce-scatter.16
  4555.5 11.6 reduce-scatter.26
  4569.9 11.7 reduce-scatter.24
  4586.1 234.6 all-reduce.8
where the time goes:
time: 4860 us; the launch traced here: 4840 us
  matrix products  2000 us (41%)
  waiting for transfers between devices  1530 us (31%)
  other arithmetic  466 us (10%)
  local copies, waits for them, and re-layouts  465 us (10%)
  loops' own time  293 us (6%)
  blocking collectives  72.1 us (1%)
    reduce_scatter x1, waiting for transfers between devices, local(): lax.psum_scatter(value_sums.astype(jnp.bfloat16), 'ctx', scatter_dimensio...  386 us
    dot_general x16, matrix products, tile_backward(): jnp.einsum('sqhd,skhd->shqk', grad_heads, value_heads, preferred_element_...  376 us
    reduce_scatter x1, waiting for transfers between devices, local(): lax.psum_scatter(key_sums.astype(jnp.bfloat16), 'ctx', scatter_dimension=...  336 us
    dot_general x16, matrix products, tile_forward(): jnp.einsum('shqk,skhd->sqhd', weights.astype(jnp.bfloat16), value_heads,...  288 us
    dot_general x16, matrix products, tile_forward(): jnp.einsum('sqhd,skhd->shqk', query_heads, key_heads, preferred_element_t...  252 us
    dot_general x16, matrix products, tile_backward(): jnp.einsum('sqhd,skhd->shqk', query_heads, key_heads, preferred_element_t...  247 us
    reduce_sum x16, other arithmetic, tile_forward(): row_total = jnp.sum(weights, axis=-1)  242 us
    psum x1, waiting for transfers between devices, local(): lax.psum(grad_qkv.astype(jnp.bfloat16), 'ctx').astype(jnp.float32)  188 us
  transfers between devices with their start and end apart: 15, of which 10 were waited for; matrix products, arithmetic and copies ran while one was open for 27% of the time, Pallas kernels for 0%

commit v1 on v0

v1 whole, which is shorter than its diff:
```python
import functools
import math

import jax
import jax.numpy as jnp
from jax import lax
from jax.experimental import pallas as pl
from jax.experimental.pallas import tpu as pltpu
from jax.sharding import Mesh
from jax.sharding import PartitionSpec as P

HEADS = 16
ALPHA = 32.0
EPS = 1e-05
NEG = -1e30
bf16 = jnp.bfloat16
f32 = jnp.float32
MIB = 1 << 20


def layer_norm(values, norm_gain, norm_shift):
    average = jnp.mean(values, axis=-1, keepdims=True)
    centered = values - average
    variance = jnp.mean(centered * centered, axis=-1, keepdims=True)
    return centered * lax.rsqrt(variance + EPS) * norm_gain + norm_shift


def norm_backward(values, norm_gain, norm_shift, upstream):
    _, pullback = jax.vjp(layer_norm, values, norm_gain, norm_shift)
    return pullback(upstream)


def gelu_tanh(values):
    return jax.nn.gelu(values, approximate=True)


def gelu_backward(values, upstream):
    _, pullback = jax.vjp(gelu_tanh, values)
    return pullback(upstream)[0]


def dot(a, b, ca, cb):
    return lax.dot_general(a, b, (((ca,), (cb,)), ((), ())), preferred_element_type=f32)


def columns(index, width):
    return pl.ds(pl.multiple_of(index * width, width), width)


def whole(shape):
    return pl.BlockSpec(shape, lambda *_: (0,) * len(shape), pipeline_mode=pl.Buffered(1))


def project_kernel(table, a1_first, a1_second, weight, bias, q_t, k_n, v_t):
    width = k_n.shape[1]
    blk = a1_first.shape[0]
    for half, rows in enumerate((a1_first, a1_second)):
        part = slice(half * blk, (half + 1) * blk)
        heads = dot(rows[...], weight[...], 1, 0) + bias[...]
        turned = jnp.transpose(heads)
        q_t[:, part] = (turned[:width] * 0.125).astype(bf16)
        v_t[:, part] = turned[2 * width :].astype(bf16)
        k_n[part, :] = heads[:, width : 2 * width].astype(bf16)


def project(table, a1_full, weight, bias, blk, width):
    tokens, model = a1_full.shape
    tile = 2 * blk
    turned = pl.BlockSpec((width, tile), lambda i, t: (0, i))
    straight = pl.BlockSpec((tile, width), lambda i, t: (i, 0))
    return pl.pallas_call(
        project_kernel,
        grid_spec=pltpu.PrefetchScalarGridSpec(
            num_scalar_prefetch=1,
            grid=(tokens // tile,),
            in_specs=[
                pl.BlockSpec((blk, model), lambda i, t: (t[2 * i], 0)),
                pl.BlockSpec((blk, model), lambda i, t: (t[2 * i + 1], 0)),
                whole(weight.shape),
                whole(bias.shape),
            ],
            out_specs=[turned, straight, turned],
        ),
        out_shape=[
            jax.ShapeDtypeStruct((width, tokens), bf16),
            jax.ShapeDtypeStruct((tokens, width), bf16),
            jax.ShapeDtypeStruct((width, tokens), bf16),
        ],
        compiler_params=pltpu.CompilerParams(vmem_limit_bytes=48 * MIB),
        cost_estimate=pl.CostEstimate(
            flops=8 * tokens * model * width, bytes_accessed=2 * tokens * model, transcendentals=0
        ),
        name="project",
    )(table, a1_full, a1_full, weight, bias)


def forward_kernel(base, table, q_t, k_n, v_t, out_t, log_total, out_slots, scores):
    _, width, blk = out_slots.shape
    tile = q_t.shape[1]
    step = base + pl.program_id(0)
    query = q_t[...]

    def score(index):
        return dot(k_n[columns(index, blk), :], query, 1, 0)

    def prepare(index, slot):
        tile_scores = score(index)
        scores[slot] = tile_scores
        return jnp.max(tile_scores, axis=0, keepdims=True)

    def absorb(index, slot, peak, total, summed, tile_peak):
        new_peak = jnp.maximum(peak, tile_peak)
        weights = jnp.exp(scores[slot] - new_peak)
        keep = jnp.exp(peak - new_peak)
        total = total * keep + jnp.sum(weights, axis=0, keepdims=True)
        summed = summed * keep + dot(v_t[:, columns(index, blk)], weights.astype(bf16), 1, 0)
        return new_peak, total, summed

    def body(pair, carry):
        peak, total, summed, tile_peak = carry
        for slot in range(2):
            next_peak = prepare(2 * pair + slot + 1, 1 - slot)
            peak, total, summed = absorb(2 * pair + slot, slot, peak, total, summed, tile_peak)
            tile_peak = next_peak
        return peak, total, summed, tile_peak

    carry = (
        jnp.full((1, tile), -jnp.inf, f32),
        jnp.zeros((1, tile), f32),
        jnp.zeros((width, tile), f32),
        prepare(0, 0),
    )
    peak, total, summed, _ = lax.fori_loop(0, step, body, carry)
    for half in range(2):
        index = 2 * step + half
        key_pos = half * blk + lax.broadcasted_iota(jnp.int32, (blk, tile), 0)
        query_pos = lax.broadcasted_iota(jnp.int32, (blk, tile), 1)
        tile_scores = jnp.where(query_pos >= key_pos, score(index), NEG)
        scores[half] = tile_scores
        tile_peak = jnp.max(tile_scores, axis=0, keepdims=True)
        peak, total, summed = absorb(index, half, peak, total, summed, tile_peak)
    result = summed / total
    out_t[...] = result
    log_total[...] = peak + jnp.log(total)
    low = result.astype(bf16)
    for half in range(2):
        out_slots[table[2 * step + half]] = low[:, half * blk : (half + 1) * blk]


def forward(high, table, q_t, k_n, v_t, blk):
    width, tokens = q_t.shape
    slots = tokens // (2 * blk)
    tile = 2 * blk
    steps = slots // 2
    base = steps if high else 0
    seen = tokens if high else tokens // 2
    return pl.pallas_call(
        functools.partial(forward_kernel, base),
        grid_spec=pltpu.PrefetchScalarGridSpec(
            num_scalar_prefetch=1,
            grid=(steps,),
            in_specs=[
                pl.BlockSpec((width, tile), lambda i, t: (0, base + i)),
                whole((seen, width)),
                whole((width, seen)),
            ],
            out_specs=[
                pl.BlockSpec((width, tile), lambda i, t: (0, i)),
                pl.BlockSpec((1, tile), lambda i, t: (0, i)),
                whole((slots, width, blk)),
            ],
            scratch_shapes=[pltpu.VMEM((2, blk, tile), f32)],
        ),
        out_shape=[
            jax.ShapeDtypeStruct((width, tokens // 2), f32),
            jax.ShapeDtypeStruct((1, tokens // 2), f32),
            jax.ShapeDtypeStruct((slots, width, blk), bf16),
        ],
        compiler_params=pltpu.CompilerParams(vmem_limit_bytes=56 * MIB),
        cost_estimate=pl.CostEstimate(
            flops=(6 if high else 2) * tokens * tokens * width,
            bytes_accessed=12 * tokens * width,
            transcendentals=(3 if high else 1) * tokens * tokens // 8,
        ),
        name="forward_high" if high else "forward_low",
    )(table, q_t, k_n, v_t)


def delta_kernel(table, given, out_t, q_t, grad_t, grad_n, delta, q_n):
    block = given[0]
    grad_t[...] = block
    wide = block.astype(f32)
    delta[...] = jnp.sum(wide * out_t[...], axis=0, keepdims=True)
    grad_n[...] = jnp.transpose(wide).astype(bf16)
    q_n[...] = jnp.transpose(q_t[...].astype(f32)).astype(bf16)


def delta_rows(high, table, given, out_t, q_t):
    slots, width, blk = given.shape
    half = slots * blk
    base = slots if high else 0
    return pl.pallas_call(
        delta_kernel,
        grid_spec=pltpu.PrefetchScalarGridSpec(
            num_scalar_prefetch=1,
            grid=(slots,),
            in_specs=[
                pl.BlockSpec((1, width, blk), lambda p, t: (t[base + p], 0, 0)),
                pl.BlockSpec((width, blk), lambda p, t: (0, p)),
                pl.BlockSpec((width, blk), lambda p, t: (0, base + p)),
            ],
            out_specs=[
                pl.BlockSpec((width, blk), lambda p, t: (0, p)),
                pl.BlockSpec((blk, width), lambda p, t: (p, 0)),
                pl.BlockSpec((1, blk), lambda p, t: (0, p)),
                pl.BlockSpec((blk, width), lambda p, t: (p, 0)),
            ],
        ),
        out_shape=[
            jax.ShapeDtypeStruct((width, half), bf16),
            jax.ShapeDtypeStruct((half, width), bf16),
            jax.ShapeDtypeStruct((1, half), f32),
            jax.ShapeDtypeStruct((half, width), bf16),
        ],
        compiler_params=pltpu.CompilerParams(vmem_limit_bytes=32 * MIB),
        name="delta_high" if high else "delta_low",
    )(table, given, out_t, q_t)


def backward_kernel(kind, base, after, *refs):
    table, q_t, q_n, grad_t, grad_n, log_total, delta, k_n, v_t = refs[:9]
    refs = refs[9:]
    cross = kind in ("first", "second")
    query_out = key_out = value_out = None
    if cross:
        (query_start, key_start, value_start), refs = refs[:3], refs[3:]
    if kind == "second":
        earlier, refs = refs[0], refs[1:]
    refs = refs[after:]
    if kind in ("high", "first"):
        query_out, refs = refs[0], refs[1:]
    elif kind == "low":
        (key_out, value_out), refs = refs[:2], refs[2:]
    out_slots, refs = refs[0], refs[1:]
    scores, grads, query_sum, key_sum, value_sum = refs
    slots, _, blk = out_slots.shape
    tile, width = k_n.shape
    step = pl.program_id(0)

    @pl.when(step == 0)
    def _():
        if cross:
            query_sum[...] = query_start[...]
        else:
            query_sum[...] = jnp.zeros_like(query_sum)
        if kind == "second":
            out_slots[:, width:] = earlier[...]

    keys = k_n[...]
    keys_t = jnp.transpose(keys.astype(f32)).astype(bf16)
    values = jnp.transpose(v_t[...].astype(f32)).astype(bf16)
    if cross:
        key_sum[...] = key_start[...]
        value_sum[...] = value_start[...]
    else:
        key_sum[...] = jnp.zeros_like(key_sum)
        value_sum[...] = jnp.zeros_like(value_sum)

    def prepare(index, slot):
        at = columns(index, blk)
        scores[slot] = dot(keys, q_t[:, at], 1, 0)
        grads[slot] = dot(values, grad_t[:, at], 1, 0)

    def absorb(index, slot, diagonal):
        at = columns(index, blk)
        tile_scores = scores[slot]
        if diagonal is not None:
            key_pos = lax.broadcasted_iota(jnp.int32, (tile, blk), 0)
            query_pos = diagonal * blk + lax.broadcasted_iota(jnp.int32, (tile, blk), 1)
            tile_scores = jnp.where(query_pos >= key_pos, tile_scores, NEG)
        probs = jnp.exp(tile_scores - log_total[:, at])
        score_grads = (probs * (grads[slot] - delta[:, at])).astype(bf16)
        value_sum[...] += dot(probs.astype(bf16), grad_n[at, :], 1, 0)
        key_sum[...] += dot(score_grads, q_n[at, :], 1, 0)
        query_sum[:, at] += dot(keys_t, score_grads, 1, 0)

    def sweep(first, pairs):
        prepare(first, 0)

        def body(pair, carry):
            index = first + 2 * pair
            prepare(index + 1, 1)
            absorb(index, 0, None)
            prepare(jnp.minimum(index + 2, slots - 1), 0)
            absorb(index + 1, 1, None)
            return carry

        lax.fori_loop(0, pairs, body, 0)

    if cross:
        sweep(0, slots // 2)
    else:
        for half in range(2):
            prepare(2 * step + half, half)
            absorb(2 * step + half, half, half)

        @pl.when(2 * step + 2 < slots)
        def _():
            sweep(2 * step + 2, slots // 2 - 1 - step)

    def halves():
        for half in range(2):
            yield table[base + 2 * step + half], slice(half * blk, (half + 1) * blk), half

    if kind == "low":
        key_out[...] = key_sum[...]
        value_out[...] = value_sum[...]
        for slot, _, half in halves():
            own = query_sum[:, columns(2 * step + half, blk)] * 0.125
            out_slots[slot] = own.astype(bf16)
    else:
        start = width if kind == "second" else 0
        key_t = jnp.transpose(key_sum[...]).astype(bf16)
        value_t = jnp.transpose(value_sum[...]).astype(bf16)
        for slot, part, _ in halves():
            out_slots[slot, start : start + width] = key_t[:, part]
            out_slots[slot, start + width : start + 2 * width] = value_t[:, part]
    if query_out is not None:

        @pl.when(step == pl.num_programs(0) - 1)
        def _():
            query_out[...] = query_sum[...]

    if kind == "second":

        @pl.when(step == pl.num_programs(0) - 1)
        def _():
            def finish(index, carry):
                own = query_sum[:, columns(index, blk)] * 0.125
                out_slots[table[slots + index], 0:width] = own.astype(bf16)
                return carry

            lax.fori_loop(0, slots, finish, 0)


def backward(kind, table, queries, k_n, v_t, starts, after, blk):
    width, half = queries[0].shape
    slots = half // blk
    tile = 2 * blk
    cross = kind in ("first", "second")
    steps = slots // 4 if cross else slots // 2
    skip = {"high": slots // 2, "low": 0, "first": 0, "second": slots // 4}[kind]
    start_skip = skip if cross else 0
    straight = pl.BlockSpec((tile, width), lambda i, t: (start_skip + i, 0))
    in_specs = [whole(array.shape) for array in queries] + [
        pl.BlockSpec((tile, width), lambda i, t: (skip + i, 0)),
        pl.BlockSpec((width, tile), lambda i, t: (0, skip + i)),
    ]
    if cross:
        in_specs += [whole((width, half)), straight, straight]
    if kind == "second":
        in_specs += [whole(starts[3].shape)]
    in_specs += [pl.BlockSpec(memory_space=pl.ANY)] * len(after)
    rows = {"high": 2, "low": 1, "first": 2, "second": 3}[kind] * width
    out_specs = [whole((slots, rows, blk))]
    out_shape = [jax.ShapeDtypeStruct((slots, rows, blk), bf16)]
    if kind in ("high", "first"):
        out_specs = [whole((width, half))] + out_specs
        out_shape = [jax.ShapeDtypeStruct((width, half), f32)] + out_shape
    elif kind == "low":
        out_specs = [straight, straight] + out_specs
        out_shape = [jax.ShapeDtypeStruct((half, width), f32)] * 2 + out_shape
    return pl.pallas_call(
        functools.partial(backward_kernel, kind, 2 * skip, len(after)),
        grid_spec=pltpu.PrefetchScalarGridSpec(
            num_scalar_prefetch=1,
            grid=(steps,),
            in_specs=in_specs,
            out_specs=out_specs,
            scratch_shapes=[
                pltpu.VMEM((2, tile, blk), f32),
                pltpu.VMEM((2, tile, blk), f32),
                pltpu.VMEM((width, half), f32),
                pltpu.VMEM((tile, width), f32),
                pltpu.VMEM((tile, width), f32),
            ],
        ),
        out_shape=out_shape,
        compiler_params=pltpu.CompilerParams(vmem_limit_bytes=56 * MIB),
        cost_estimate=pl.CostEstimate(
            flops=4 * half * half * width,
            bytes_accessed=32 * half * width,
            transcendentals=half * half // 8,
        ),
        name="backward_" + kind,
    )(table, *queries, k_n, v_t, *starts, *after)


def weight_kernel(high_pair, low_query, rest, a1, total):
    blk = rest.shape[2]
    width = low_query.shape[1]

    @pl.when(pl.program_id(0) == 0)
    def _():
        total[...] = jnp.zeros_like(total)

    low = jnp.concatenate([low_query[0], rest[0, width:]], axis=0)
    high = jnp.concatenate([rest[0, :width], high_pair[0]], axis=0)
    total[...] += dot(low, a1[:blk], 1, 0) + dot(high, a1[blk:], 1, 0)


def weight_grad(high_pair, low_query, rest, a1_full):
    slots, rows, blk = rest.shape
    tokens, model = a1_full.shape
    return pl.pallas_call(
        weight_kernel,
        grid=(slots,),
        in_specs=[
            pl.BlockSpec((1,) + high_pair.shape[1:], lambda s: (s, 0, 0)),
            pl.BlockSpec((1,) + low_query.shape[1:], lambda s: (s, 0, 0)),
            pl.BlockSpec((1, rows, blk), lambda s: (s, 0, 0)),
            pl.BlockSpec((2 * blk, model), lambda s: (s, 0)),
        ],
        out_specs=pl.BlockSpec((rows, model), lambda s: (0, 0)),
        out_shape=jax.ShapeDtypeStruct((rows, model), f32),
        compiler_params=pltpu.CompilerParams(vmem_limit_bytes=48 * MIB),
        cost_estimate=pl.CostEstimate(
            flops=2 * rows * tokens * model, bytes_accessed=2 * tokens * model, transcendentals=0
        ),
        name="weight_grad",
    )(high_pair, low_query, rest, a1_full)


def local(
    groups,
    activations,
    block_order,
    qkv_weight,
    qv_bias,
    proj_weight,
    proj_bias,
    up_weight,
    up_bias,
    down_weight,
    down_bias,
    norm_gains,
    norm_biases,
    cotangent,
):
    _, rows, model = activations.shape
    blk = rows // 2
    width = model // HEADS
    ctx = ("r", "h")
    everywhere = ("r", "h", "wt")
    devices = groups * HEADS
    weight_parts = lax.axis_size("wt")
    head = lax.axis_index("h")
    group = lax.axis_index("r")
    part = lax.axis_index("wt")

    small = (qv_bias, proj_bias, up_bias, down_bias, norm_gains, norm_biases)
    packed = jnp.concatenate([array.reshape(-1) for array in small])
    gathered = lax.all_gather(packed, "wt", axis=0)
    pieces, start = [], 0
    for array in small:
        piece = gathered[:, start : start + array.size].reshape((weight_parts,) + array.shape)
        start += array.size
        if array.ndim == 2:
            piece = jnp.transpose(piece, (1, 0, 2)).reshape(array.shape[0], -1)
        else:
            piece = piece.reshape(-1)
        pieces.append(piece.astype(f32))
    qvbias, projbias, upbias, downbias, gains, shifts = pieces

    inputs = activations.reshape(rows, model).astype(f32)
    upstream = cotangent.reshape(rows, model).astype(f32)
    a1 = layer_norm(inputs, gains[0], shifts[0]).astype(bf16)
    a1_full = lax.all_gather(a1, ctx, axis=0, tiled=True)

    mine = lax.dynamic_index_in_dim(
        qkv_weight.reshape(-1, 3, HEADS, width), head, axis=2, keepdims=False
    )
    mine = lax.all_gather(mine.reshape(-1, 3 * width), "wt", axis=0, tiled=True)
    q_bias = lax.dynamic_slice(qvbias, (head * width,), (width,))
    v_bias = lax.dynamic_slice(qvbias, (model + head * width,), (width,))
    bias = jnp.concatenate([q_bias, jnp.zeros_like(q_bias), v_bias])

    lows = block_order.reshape(devices, 2)[:, 0]
    numbers = jnp.arange(devices, dtype=jnp.int32)
    owner = jnp.sum(jnp.where(lows[None, :] == numbers[:, None], numbers[None, :], 0), axis=1)
    owner = jnp.concatenate([owner, owner[::-1]]).astype(jnp.int32)
    is_high = (jnp.arange(2 * devices, dtype=jnp.int32) >= devices).astype(jnp.int32)
    slot_of = 2 * owner + is_high

    half = devices * blk
    q_t, k_n, v_t = project(slot_of, a1_full, mine, bias[None, :], blk, width)
    out_low, log_low, slots_low = forward(False, owner, q_t, k_n, v_t, blk)
    out_high, log_high, slots_high = forward(True, owner, q_t, k_n, v_t, blk)

    def to_tokens(array):
        own = lax.dynamic_slice_in_dim(array, group * HEADS, HEADS, 0)
        return lax.all_to_all(own, "h", 0, 0, tiled=True).reshape(-1, blk)

    def to_heads(array):
        array = lax.all_to_all(array.reshape(HEADS, width, blk), "h", 0, 0, tiled=True)
        if groups > 1:
            array = lax.all_gather(array, "r", axis=0, tiled=True)
        return array

    attended_t = jnp.concatenate([to_tokens(slots_low), to_tokens(slots_high)], axis=1)

    full_proj = lax.all_gather(proj_weight, "wt", axis=0, tiled=True)
    up_full = lax.all_gather(up_weight, "wt", axis=0, tiled=True)
    down_full = lax.all_gather(down_weight, "wt", axis=0, tiled=True)
    full_qkv = lax.all_gather(qkv_weight, "wt", axis=0, tiled=True)

    proj_pre = dot(attended_t, full_proj, 0, 0) + projbias
    residual = inputs + layer_norm(proj_pre, gains[1], shifts[1])
    normed_mid = layer_norm(residual, gains[2], shifts[2]).astype(bf16)
    pre_act = dot(normed_mid, up_full, 1, 1) + upbias
    hidden = gelu_tanh(pre_act).astype(bf16)
    branch = dot(hidden, down_full, 1, 0) + downbias
    layer_output = (residual + layer_norm(branch, gains[3], shifts[3])).astype(bf16)

    grad_branch, gain_three, shift_three = norm_backward(branch, gains[3], shifts[3], upstream)
    grad_branch = grad_branch.astype(bf16)
    grad_hidden = dot(grad_branch, down_full, 1, 1)
    grad_pre = gelu_backward(pre_act, grad_hidden).astype(bf16)
    grad_mid = dot(grad_pre, up_full, 1, 0)
    grad_residual, gain_two, shift_two = norm_backward(residual, gains[2], shifts[2], grad_mid)
    grad_residual = upstream + grad_residual
    grad_proj_pre, gain_one, shift_one = norm_backward(
        proj_pre, gains[1], shifts[1], grad_residual
    )
    grad_proj_pre = grad_proj_pre.astype(bf16)
    grad_attended_t = dot(full_proj, grad_proj_pre, 1, 1).astype(bf16)
    given_high = to_heads(grad_attended_t[:, blk:])
    given_low = to_heads(grad_attended_t[:, :blk])

    grad_downward = dot(hidden, grad_branch, 0, 0).astype(bf16)
    grad_upward = dot(grad_pre, normed_mid, 0, 0).astype(bf16)
    grad_proj = dot(attended_t, grad_proj_pre, 1, 0).astype(bf16)

    def own_rows(array):
        length = array.shape[0] // weight_parts
        return lax.dynamic_slice_in_dim(array, part * length, length, 0)

    early = jnp.concatenate(
        [
            jnp.sum(grad_pre.astype(f32), axis=0),
            jnp.sum(grad_branch.astype(f32), axis=0),
            jnp.sum(grad_proj_pre.astype(f32), axis=0),
            gain_one,
            gain_two,
            gain_three,
            shift_one,
            shift_two,
            shift_three,
        ]
    ).astype(bf16)
    grad_proj = jnp.concatenate([grad_proj, early.reshape(-1, model)], axis=0)
    given_high, given_low, grad_downward, grad_upward, grad_proj = lax.optimization_barrier(
        (given_high, given_low, grad_downward, grad_upward, grad_proj)
    )
    summed = lax.psum((grad_downward, grad_upward, grad_proj), everywhere)
    grad_downward, grad_upward, grad_proj = summed
    early = grad_proj[model:].astype(f32).reshape(-1)
    grad_proj = grad_proj[:model]
    grad_downward = own_rows(grad_downward).astype(f32)
    grad_upward = own_rows(grad_upward).astype(f32)
    grad_proj = own_rows(grad_proj).astype(f32)
    hidden_width = up_full.shape[0]
    grad_upbias = own_rows(early[:hidden_width])
    early = early[hidden_width:].reshape(8, model)
    grad_downbias = own_rows(early[0])
    grad_projbias = own_rows(early[1])

    def token_grads(array):
        own = lax.dynamic_slice_in_dim(array, group * HEADS, HEADS, 0)
        own = lax.all_to_all(own, "h", 0, 0, tiled=True).reshape(HEADS, -1, width, blk)
        return jnp.transpose(own, (1, 0, 2, 3)).reshape(-1, blk)

    grad_t, grad_n, delta, q_n = delta_rows(True, owner, given_high, out_high, q_t)
    high = (q_t[:, half:], q_n, grad_t, grad_n, log_high, delta)
    query_sum, high_pair = backward("high", owner, high, k_n, v_t, (), (), blk)
    high_tokens = token_grads(high_pair)
    grad_t, grad_n, delta, q_n = delta_rows(False, owner, given_low, out_low, q_t)
    low = (q_t[:, :half], q_n, grad_t, grad_n, log_low, delta)
    key_sum, value_sum, low_query = backward("low", owner, low, k_n, v_t, (), (), blk)
    low_tokens = token_grads(low_query)
    starts = (query_sum, key_sum, value_sum)
    query_sum, earlier = backward(
        "first", owner, high, k_n, v_t, starts, (high_tokens,), blk
    )
    starts = (query_sum, key_sum, value_sum, earlier)
    after = (low_tokens,) + tuple(summed)
    (rest,) = backward("second", owner, high, k_n, v_t, starts, after, blk)
    rest_tokens = token_grads(rest)

    columns_grad = weight_grad(high_pair, low_query, rest, a1_full).T.astype(bf16)
    columns_grad = columns_grad.reshape(weight_parts, -1, 3 * width)
    columns_grad = lax.all_to_all(columns_grad, "wt", 0, 0, tiled=True)
    columns_grad = jnp.sum(columns_grad.astype(f32), axis=0).astype(bf16)
    all_columns = lax.all_gather(columns_grad, "h", axis=0)
    all_columns = all_columns.reshape(HEADS, -1, 3, width)
    grad_qkv = jnp.transpose(all_columns, (1, 2, 0, 3)).reshape(-1, 3 * model).astype(f32)

    grads_t = jnp.concatenate(
        [
            jnp.concatenate([low_tokens, rest_tokens[model:]], axis=0),
            jnp.concatenate([rest_tokens[:model], high_tokens], axis=0),
        ],
        axis=1,
    )
    grad_normed = dot(grads_t, full_qkv, 0, 1)
    grad_inputs, gain_zero, shift_zero = norm_backward(inputs, gains[0], shifts[0], grad_normed)
    input_grad = (grad_residual + grad_inputs).reshape(1, rows, model)
    bias_sums = jnp.sum(grads_t.astype(f32), axis=1)

    def own_columns(array):
        length = array.shape[1] // weight_parts
        return lax.dynamic_slice_in_dim(array, part * length, length, 1)

    late = jnp.concatenate([bias_sums[:model], bias_sums[2 * model :], gain_zero, shift_zero])
    late = jnp.concatenate(
        [
            late[: 2 * model].reshape(weight_parts, -1),
            late[2 * model : 3 * model].reshape(weight_parts, -1),
            late[3 * model :].reshape(weight_parts, -1),
        ],
        axis=1,
    )
    late = jnp.broadcast_to(late[None], (devices,) + late.shape)
    late = late.reshape(devices * weight_parts, 1, -1)
    late = jnp.sum(lax.all_to_all(late, everywhere, 0, 0, tiled=True), axis=0)[0]
    length = model // weight_parts
    grad_qvbias = late[: 2 * length]
    late = late[2 * length :].reshape(2, length)
    early = own_columns(early)
    grad_gains = jnp.concatenate([late[0:1], early[2:5]], axis=0)
    grad_biases = jnp.concatenate([late[1:2], early[5:8]], axis=0)
    return (
        layer_output.reshape(1, rows, model),
        input_grad,
        grad_qkv,
        grad_qvbias,
        grad_proj,
        grad_projbias,
        grad_upward,
        grad_upbias,
        grad_downward,
        grad_downbias,
        grad_gains,
        grad_biases,
    )


def solution(mesh):
    groups = mesh.shape["ctx"] // HEADS
    split = Mesh(
        mesh.devices.reshape(groups, HEADS, mesh.shape["wt"]), ("r", "h", "wt")
    )
    tokens = P("wt", ("r", "h"), None)
    rows, flat, cols = P("wt", None), P("wt"), P(None, "wt")
    return jax.shard_map(
        functools.partial(local, groups),
        mesh=split,
        in_specs=(tokens, P(), rows, flat, rows, flat, rows, flat, rows, flat, cols, cols, tokens),
        out_specs=(tokens, tokens, rows, flat, rows, flat, rows, flat, rows, flat, cols, cols),
        check_vma=False,
    )
```

time: 4860 us -> 1290 us (0.27)
  matrix products: 2000 us -> 135 us
  waiting for transfers between devices: 1530 us -> 265 us
  Pallas kernels: 0 us -> 652 us
  local copies, waits for them, and re-layouts: 465 us -> 68.9 us
  other arithmetic: 466 us -> 77.4 us
  loops' own time: 293 us -> 0 us
  blocking collectives: 72.1 us -> 18.1 us
    dot_general x124 -> x10, matrix products: 2000 us -> 135 us  [dot(): lax.dot_general(a, b, (((ca,), (cb,)), ((), ())), preferred_element_type=...]
    reduce_scatter x6 -> x0, waiting for transfers between devices: 1000 us -> none  [the longest x1 386 us: local(): lax.psum_scatter(value_sums.astype(jnp.bfloat16), 'ctx', scatter_dimensio...]
    pallas_call x0 -> x10, Pallas kernels: none -> 652 us  [the longest x4 408 us: backward(): pl.pallas_call(functools.partial(backward_kernel, kind, 2 * skip, len(aft...]
    another operation x34 -> x0, loops' own time: 293 us -> none  [the longest x1 165 us: all_grads(): lax.fori_loop(0, key_piece.shape[1] // shard_rows, all_one_shard, running)]
    reduce_sum x28 -> x10, other arithmetic: 278 us -> 30.8 us  [the longest x1 19.9 us: local(): bias_sums = jnp.sum(grads_t.astype(f32), axis=1)]
    dynamic_slice x98 -> x4, local copies, waits for them, and re-layouts: 216 us -> 2.21 us  [the longest x2 1.19 us: own_rows(): return lax.dynamic_slice_in_dim(array, part * length, length, 0)]
    psum x1, waiting for transfers between devices: 188 us -> 1.54 us  [local(): summed = lax.psum((grad_downward, grad_upward, grad_proj), everywhere)]
    all_gather x6, waiting for transfers between devices: 338 us -> 156 us  [the longest x1 156 us: local(): a1_full = lax.all_gather(a1, ctx, axis=0, tiled=True)]
  transfers between devices with their start and end apart: 15 -> 15, of which waited for: 10 -> 6; matrix products, arithmetic and copies ran while one was open for 27% -> 13% of each run, Pallas kernels for 0% -> 51%
where the time goes in v1:
time: 1290 us; the launch traced here: 1280 us
  Pallas kernels  652 us (51%)
  waiting for transfers between devices  265 us (21%)
  matrix products  135 us (10%)
  other arithmetic  77.4 us (6%)
  local copies, waits for them, and re-layouts  68.9 us (5%)
  starting transfers between devices  44.7 us (3%)
  blocking collectives  18.1 us (1%)
  between operations  15.5 us (1%)
    pallas_call x4, Pallas kernels, backward(): pl.pallas_call(functools.partial(backward_kernel, kind, 2 * skip, len(aft...  408 us
    pallas_call x2, Pallas kernels, forward(): pl.pallas_call(functools.partial(forward_kernel, base), grid_spec=pltpu.P...  186 us
    all_gather x1, waiting for transfers between devices, local(): a1_full = lax.all_gather(a1, ctx, axis=0, tiled=True)  156 us
    dot_general x10, matrix products, dot(): lax.dot_general(a, b, (((ca,), (cb,)), ((), ())), preferred_element_type=...  135 us
    all_to_all x3, waiting for transfers between devices, token_grads(): lax.all_to_all(own, 'h', 0, 0, tiled=True).reshape(HEADS, -1, width, blk)  64.5 us
    unnamed x132, local copies, waits for them, and re-layouts  44.8 us
  transfers between devices with their start and end apart: 15, of which 6 were waited for; matrix products, arithmetic and copies ran while one was open for 13% of the time, Pallas kernels for 51%

profile of v1, /device:TPU:13, one launch (start us, length us, event | category | flops | bytes accessed | tf_op | source)
XLA Modules:
  0.0 1276.7 jit_solution(15811319913107258245)
XLA Ops:
  30.2 6.8 all_gather.33.weight
  38.1 156.1 %all-gather.9.cloned.1.call-done.a1_first.a1_second.a1 = bf16[16384,1024]{1,0:T(8,128)(2,1)} async-done(((bf16[1024,1024]{1,0:T(8,128)(2,1)}), bf16[16384,1024]{1,0:T(8,128)(2,1)}) %all-gather.9.cloned.1.call-update) | async-done | bytes 33554448 | tf_op jit(solution)/shard_map/all_gather | solution.py:478
  194.2 25.6 %project.1 = (bf16[64,16384]{1,0:T(8,128)(2,1)S(1)}, bf16[16384,64]{1,0:T(8,128)(2,1)}, bf16[64,16384]{1,0:T(8,128)(2,1)S(1)}) custom-call(s32[32]{0:T(128)S(1)} %get-tuple-element.135.table, bf16[16384,1024]{1,0:T(8,128)(2,1)} %all-gather.9.cloned.1.call-done.a1_first.a1_second.a1, bf16[16384,1024]{1,0:T(8,128)(2,1)} %all-gather.9.cloned.1.call-done.a1_first.a1_second.a1, ...), custom_call_target="tpu_custom_call" | custom-call | flops 8589934592 | bytes 33554432 | tf_op jit(solution)/shard_map/project/pallas_call | solution.py:71
  222.5 52.8 %forward_low.1 = (f32[64,8192]{1,0:T(8,128)}, f32[1,8192]{1,0:T(1,128)}, bf16[16,64,512]{2,1,0:T(8,128)(2,1)}) custom-call(s32[32]{0:T(128)} %get-tuple-element.136.table.refs_0_, bf16[64,16384]{1,0:T(8,128)(2,1)} %copy-done, bf16[16384,64]{1,0:T(8,128)(2,1)} %get-tuple-element.42.k_n.refs_7_, bf16[64,16384]{1,0:T(8,128)(2,1)} %copy-done.8), custom_call_target="tpu_custom_call" | custom-call | flops 34359738368 | bytes 12582912 | tf_op jit(solution)/shard_map/forward_low/pallas_call | solution.py:157
  280.8 133.5 %forward_high.1 = (f32[64,8192]{1,0:T(8,128)}, f32[1,8192]{1,0:T(1,128)}, bf16[16,64,512]{2,1,0:T(8,128)(2,1)}) custom-call(s32[32]{0:T(128)} %get-tuple-element.136.table.refs_0_, bf16[64,16384]{1,0:T(8,128)(2,1)} %copy-done, bf16[16384,64]{1,0:T(8,128)(2,1)} %get-tuple-element.42.k_n.refs_7_, bf16[64,16384]{1,0:T(8,128)(2,1)} %copy-done.8), custom_call_target="tpu_custom_call" | custom-call | flops 103079215104 | bytes 12582912 | tf_op jit(solution)/shard_map/forward_high/pallas_call | solution.py:157
  414.3 6.4 all-to-all-start.1
  421.8 23.7 %all-to-all-done.1 = bf16[16,64,512]{2,1,0:T(8,128)(2,1)} async-done(((bf16[16,64,512]{2,1,0:T(8,128)(2,1)}), bf16[16,64,512]{2,1,0:T(8,128)(2,1)}, u32[]{:S(2)}, u32[]{:S(2)}) %all-to-all-start.1) | async-done | bytes 1048608 | tf_op jit(solution)/shard_map/all_to_all | solution.py:502
  457.4 21.9 %multiply_convert_fusion = (bf16[1024,4096]{1,0:T(8,128)(2,1)}, f32[1024,4096]{1,0:T(8,128)}) fusion(f32[4096]{0:T(1024)S(1)} %bitcast.182, bf16[4096,1024]{1,0:T(8,128)(2,1)} %all-gather.13.cloned.1.call-done, f32[1024,1024]{1,0:T(8,128)} %copy-done.20, f32[1024]{0:T(1024)S(1)} %bitcast.191, f32[1024]{0:T(1024)S(1)} %bitcast.176, f32[1024]{0:T(1024)S(1)} %fusion.29, ...), kind=kOutput, calls=%fused_computation.9 | convolution fusion | flops 8637120512 | bytes 37781504 | tf_op jit(solution)/shard_map/dot_general | solution.py:43
  479.4 13.3 %add_reduce_fusion = (f32[1024]{0:T(1024)S(1)}, f32[1024,1024]{1,0:T(8,128)S(1)}) fusion(f32[1024]{0:T(1024)S(1)} %bitcast.158, bf16[1024,4096]{1,0:T(8,128)(2,1)} %get-tuple-element.167, bf16[4096,1024]{1,0:T(8,128)(2,1)} %all-gather.15.cloned.1.call-done), kind=kOutput, calls=%fused_computation.55 | convolution fusion | flops 8592030720 | bytes 20979712 | tf_op jit(solution)/shard_map/dot_general | solution.py:43
  501.1 26.0 %fusion.39 = (bf16[4096]{0:T(1024)(128)(2,1)S(1)}, bf16[1024,4096]{1,0:T(8,128)(2,1)}) fusion(f32[1024,4096]{1,0:T(8,128)} %get-tuple-element.168, f32[4096]{0:T(1024)S(1)} %bitcast.183, bf16[1024,1024]{1,0:T(8,128)(2,1)} %get-tuple-element.123, bf16[4096,1024]{1,0:T(8,128)(2,1)} %all-gather.15.cloned.1.call-done), kind=kOutput, calls=%fused_computation.130 | convolution fusion | flops 8682205184 | bytes 35676160 | tf_op jit(solution)/shard_map/dot_general | solution.py:43
  527.1 15.7 %multiply_reduce_fusion = (bf16[1024]{0:T(1024)(128)(2,1)S(1)}, f32[1024]{0:T(1024)S(1)}, bf16[1024]{0:T(1024)(128)(2,1)S(1)}, f32[1024,1024]{1,0:T(8,128)S(1)}) fusion(f32[1024,1024]{1,0:T(8,128)} %copy-done.20, f32[1024]{0:T(1024)S(1)} %fusion.29, f32[1024]{0:T(1024)S(1)} %broadcast_multiply_fusion.1, f32[1024]{0:T(1024)S(1)} %bitcast.177, ...), kind=kOutput, calls=%fused_computation.43 | convolution fusion | flops 8598320128 | bytes 25186304 | tf_op jit(solution)/shard_map/dot_general | solution.py:43
  565.5 15.7 %convolution_convert_fusion = bf16[4096,1024]{1,0:T(8,128)(2,1)} fusion(bf16[1024,4096]{1,0:T(8,128)(2,1)} %get-tuple-element.125, f32[1024,1024]{1,0:T(8,128)} %copy-done.20, f32[1024]{0:T(1024)S(1)} %bitcast.192, f32[1024]{0:T(1024)S(1)} %bitcast.179, f32[1024]{0:T(1024)S(1)} %fusion.29, f32[1024]{0:T(1024)S(1)} %broadcast_multiply_fusion.1), kind=kOutput, calls=%fused_computation.11 | convolution fusion | flops 8599371776 | bytes 20987904 | tf_op jit(solution)/shard_map/dot_general | solution.py:43
  581.1 9.1 all-to-all-done.2.given
  598.4 14.6 %convolution_convert_fusion.1 = bf16[4096,1024]{1,0:T(8,128)(2,1)} fusion(bf16[1024,4096]{1,0:T(8,128)(2,1)} %get-tuple-element.167, bf16[1024,1024]{1,0:T(8,128)(2,1)S(1)} %copy-done.35), kind=kOutput, calls=%fused_computation.12 | convolution fusion | flops 8594128896 | bytes 18874368 | tf_op jit(solution)/shard_map/dot_general | solution.py:43
  612.9 7.2 all-to-all-done.3.given
  630.1 108.8 %backward_high.1 = (f32[64,8192]{1,0:T(8,128)}, bf16[16,128,512]{2,1,0:T(8,128)(2,1)}) custom-call(s32[32]{0:T(128)} %get-tuple-element.136.table.refs_0_, bf16[64,8192]{1,0:T(8,128)(2,1)} %get-tuple-element.139.refs_1_, bf16[8192,64]{1,0:T(8,128)(2,1)} %copy-done.10, bf16[64,8192]{1,0:T(8,128)(2,1)} %copy-done.13, bf16[8192,64]{1,0:T(8,128)(2,1)} %copy-done.9, ...), custom_call_target="tpu_custom_call" | custom-call | flops 17179869184 | bytes 16777216 | tf_op jit(solution)/shard_map/backward_high/pallas_call | solution.py:373
  738.9 5.4 all-to-all-start.5
  746.0 8.8 delta_low.1
  759.0 107.0 %backward_low.1 = (f32[8192,64]{1,0:T(8,128)}, f32[8192,64]{1,0:T(8,128)}, bf16[16,64,512]{2,1,0:T(8,128)(2,1)}) custom-call(s32[32]{0:T(128)} %get-tuple-element.136.table.refs_0_, bf16[64,8192]{1,0:T(8,128)(2,1)} %get-tuple-element.138.refs_1_, bf16[8192,64]{1,0:T(8,128)(2,1)} %copy-done.12, bf16[64,8192]{1,0:T(8,128)(2,1)} %copy-done.14, ...), custom_call_target="tpu_custom_call" | custom-call | flops 17179869184 | bytes 16777216 | tf_op jit(solution)/shard_map/backward_low/pallas_call | solution.py:373
  866.0 6.1 all-to-all-start.4
  875.8 96.0 %backward_first.1 = (f32[64,8192]{1,0:T(8,128)}, bf16[16,128,512]{2,1,0:T(8,128)(2,1)}) custom-call(s32[32]{0:T(128)} %get-tuple-element.136.table.refs_0_, bf16[64,8192]{1,0:T(8,128)(2,1)} %get-tuple-element.139.refs_1_, bf16[8192,64]{1,0:T(8,128)(2,1)} %copy-done.10, bf16[64,8192]{1,0:T(8,128)(2,1)} %copy-done.13, bf16[8192,64]{1,0:T(8,128)(2,1)} %copy-done.9, ...), custom_call_target="tpu_custom_call" | custom-call | flops 17179869184 | bytes 16777216 | tf_op jit(solution)/shard_map/backward_first/pallas_call | solution.py:373
  973.3 96.3 %backward_second.1.rest = bf16[16,192,512]{2,1,0:T(8,128)(2,1)} custom-call(s32[32]{0:T(128)} %get-tuple-element.136.table.refs_0_, bf16[64,8192]{1,0:T(8,128)(2,1)} %get-tuple-element.139.refs_1_, bf16[8192,64]{1,0:T(8,128)(2,1)} %copy-done.10, bf16[64,8192]{1,0:T(8,128)(2,1)} %copy-done.13, bf16[8192,64]{1,0:T(8,128)(2,1)} %copy-done.9, ...), custom_call_target="tpu_custom_call" | custom-call | flops 17179869184 | bytes 16777216 | tf_op jit(solution)/shard_map/backward_second/pallas_call | solution.py:373
  1069.7 19.9 %weight_grad.1 = f32[192,1024]{1,0:T(8,128)S(1)} custom-call(bf16[16,128,512]{2,1,0:T(8,128)(2,1)S(1)} %copy-done.2, bf16[16,64,512]{2,1,0:T(8,128)(2,1)S(1)} %copy-done.3, bf16[16,192,512]{2,1,0:T(8,128)(2,1)} %backward_second.1.rest, bf16[16384,1024]{1,0:T(8,128)(2,1)} %all-gather.9.cloned.1.call-done.a1_first.a1_second.a1), custom_call_target="tpu_custom_call" | custom-call | flops 6442450944 | bytes 33554432 | tf_op jit(solution)/shard_map/weight_grad/pallas_call | solution.py:415
  1089.7 8.1 all_to_all.45
  1097.8 7.2 all-to-all-start.6
  1117.4 12.0 dynamic-slice_convert_fusion
  1129.4 64.5 %all-to-all-done.6 = bf16[16,192,512]{2,1,0:T(8,128)(2,1)S(1)} async-done(((bf16[16,192,512]{2,1,0:T(8,128)(2,1)}), bf16[16,192,512]{2,1,0:T(8,128)(2,1)S(1)}, u32[]{:S(2)}, u32[]{:S(2)}) %all-to-all-start.6) | async-done | bytes 3145760 | tf_op jit(solution)/shard_map/all_to_all | solution.py:580
  1197.0 19.9 %convert_reduce_fusion = f32[3072]{0:T(1024)S(1)} fusion(bf16[2048,512]{1,0:T(8,128)(2,1)S(1)} %bitcast.139, bf16[1024,512]{1,0:T(8,128)(2,1)S(1)} %bitcast.145, bf16[2048,512]{1,0:T(8,128)(2,1)S(1)} %bitcast.140, bf16[1024,512]{1,0:T(8,128)(2,1)S(1)} %bitcast.143), kind=kLoop, calls=%fused_computation.10 | loop fusion | flops 28308480 | bytes 6303744 | tf_op jit(solution)/shard_map/reduce_sum | solution.py:618
  1217.1 14.8 %fusion.22 = (f32[1024]{0:T(1024)S(1)}, f32[1024,1024]{1,0:T(8,128)S(1)}) fusion(bf16[1,1024,1024]{2,1,0:T(8,128)(2,1)S(1)} %copy-done.19, f32[1024]{0:T(1024)S(1)} %bitcast.168, f32[1024]{0:T(1024)S(1)} %copy-done.39, bf16[1024,3072]{1,0:T(8,128)(2,1)} %all-gather.17.cloned.1.call-done, bf16[2048,512]{1,0:T(8,128)(2,1)} %bitcast.138, ...), kind=kOutput, calls=%fused_computation.38 | convolution fusion | flops 6472858624 | bytes 18886656 | tf_op jit(solution)/shard_map/dot_general | solution.py:43
  1241.7 5.6 add_bitcast_fusion
  1255.3 6.3 copy.54
  1261.6 6.6 copy.55
  (248 shorter events, 139.6 us)
Async XLA Ops:
  7.2 14.3 %copy-start.17 = (bf16[1,1024,1024]{2,1,0:T(8,128)(2,1)S(1)}, bf16[1,1024,1024]{2,1,0:T(8,128)(2,1)}, u32[]{:S(2)}) copy-start(bf16[1,1024,1024]{2,1,0:T(8,128)(2,1)} %param.13) | copy-start | bytes 6291460
  7.2 187.0 %all-gather.9.cloned.1.call-start = ((), (), s32[]{:S(2)}) async-start(), calls=%async_computation.9 | async-start | bytes 35651584 | tf_op jit(solution)/shard_map/all_gather | solution.py:478
  15.3 10.5 copy-start.37
  23.7 398.2 %all-gather.11.cloned.1.call-start = ((), (), s32[]{:S(2)}) async-start(), calls=%async_computation.10 | async-start | bytes 3145728 | tf_op jit(solution)/shard_map/all_gather | solution.py:512
  24.4 433.0 %all-gather.13.cloned.1.call-start = ((), (), s32[]{:S(2)}) async-start(), calls=%async_computation.11 | async-start | bytes 12582912 | tf_op jit(solution)/shard_map/all_gather | solution.py:513
  25.2 454.2 %all-gather.15.cloned.1.call-start = ((), (), s32[]{:S(2)}) async-start(), calls=%async_computation.12 | async-start | bytes 12582912 | tf_op jit(solution)/shard_map/all_gather | solution.py:514
  25.7 11.2 copy-start.53
  275.4 138.9 %all-to-all-start = ((bf16[16,64,512]{2,1,0:T(8,128)(2,1)}), bf16[16,64,512]{2,1,0:T(8,128)(2,1)S(1)}, u32[]{:S(2)}, u32[]{:S(2)}) async-start(bf16[16,64,512]{2,1,0:T(8,128)(2,1)} %get-tuple-element.44), calls=%async_computation | async-start | bytes 2097152 | tf_op jit(solution)/shard_map/all_to_all | solution.py:502
  280.7 140.7 %copy-start.41 = (f32[1,16,2,128]{3,2,1,0:T(2,128)S(1)}, f32[1,16,2,128]{3,2,1,0:T(2,128)}, u32[]{:S(2)}) copy-start(f32[1,16,2,128]{3,2,1,0:T(2,128)} %get-tuple-element.148) | copy-start | bytes 49156
  280.7 140.7 %copy-start.26 = (bf16[1,1024,1024]{2,1,0:T(8,128)(2,1)S(1)}, bf16[1,1024,1024]{2,1,0:T(8,128)(2,1)}, u32[]{:S(2)}) copy-start(bf16[1,1024,1024]{2,1,0:T(8,128)(2,1)} %param.25) | copy-start | bytes 6291460
  414.3 31.2 %all-to-all-start.1 = ((bf16[16,64,512]{2,1,0:T(8,128)(2,1)}), bf16[16,64,512]{2,1,0:T(8,128)(2,1)}, u32[]{:S(2)}, u32[]{:S(2)}) async-start(bf16[16,64,512]{2,1,0:T(8,128)(2,1)} %get-tuple-element.45), calls=%async_computation.1 | async-start | bytes 2097152 | tf_op jit(solution)/shard_map/all_to_all | solution.py:502
  527.1 15.7 %copy-start.22 = (f32[1024,1024]{1,0:T(8,128)S(1)}, f32[1024,1024]{1,0:T(8,128)}, u32[]{:S(2)}) copy-start(f32[1024,1024]{1,0:T(8,128)} %copy-done.20) | copy-start | bytes 12582916
  560.3 30.0 %all-to-all-start.2 = ((bf16[16,64,512]{2,1,0:T(8,128)(2,1)}), bf16[16,64,512]{2,1,0:T(8,128)(2,1)S(1)}, u32[]{:S(2)}, u32[]{:S(2)}) async-start(bf16[16,64,512]{2,1,0:T(8,128)(2,1)} %bitcast.20), calls=%async_computation.2 | async-start | bytes 2097152 | tf_op jit(solution)/shard_map/all_to_all | solution.py:505
  581.1 17.2 %copy-start.35 = (bf16[1024,1024]{1,0:T(8,128)(2,1)S(1)}, bf16[1024,1024]{1,0:T(8,128)(2,1)}, u32[]{:S(2)}) copy-start(bf16[1024,1024]{1,0:T(8,128)(2,1)} %get-tuple-element.123) | copy-start | bytes 6291460
  590.2 29.9 %all-to-all-start.3 = ((bf16[16,64,512]{2,1,0:T(8,128)(2,1)}), bf16[16,64,512]{2,1,0:T(8,128)(2,1)}, u32[]{:S(2)}, u32[]{:S(2)}) async-start(bf16[16,64,512]{2,1,0:T(8,128)(2,1)} %bitcast.21), calls=%async_computation.3 | async-start | bytes 2097152 | tf_op jit(solution)/shard_map/all_to_all | solution.py:505
  595.2 378.2 %all-reduce.3.cloned.1.call-start = ((), (), s32[]{:S(2)}) async-start(), calls=%async_computation.15 | async-start | bytes 37814272 | tf_op jit(solution)/shard_map/psum | solution.py:565
  738.9 127.0 %all-to-all-start.5 = ((bf16[16,128,512]{2,1,0:T(8,128)(2,1)}), bf16[16,128,512]{2,1,0:T(8,128)(2,1)}, u32[]{:S(2)}, u32[]{:S(2)}) async-start(bf16[16,128,512]{2,1,0:T(8,128)(2,1)} %get-tuple-element.64.high_pair), calls=%async_computation.5 | async-start | bytes 4194304 | tf_op jit(solution)/shard_map/all_to_all | solution.py:580
  866.0 105.8 %all-to-all-start.4 = ((bf16[16,64,512]{2,1,0:T(8,128)(2,1)}), bf16[16,64,512]{2,1,0:T(8,128)(2,1)S(1)}, u32[]{:S(2)}, u32[]{:S(2)}) async-start(bf16[16,64,512]{2,1,0:T(8,128)(2,1)} %get-tuple-element.53.low_query), calls=%async_computation.4 | async-start | bytes 2097152 | tf_op jit(solution)/shard_map/all_to_all | solution.py:580
  872.1 345.0 %all-gather.17.cloned.1.call-start = ((), (), s32[]{:S(2)}) async-start(), calls=%async_computation.13 | async-start | bytes 9437184 | tf_op jit(solution)/shard_map/all_gather | solution.py:515
  973.3 96.3 %copy-start.2 = (bf16[16,128,512]{2,1,0:T(8,128)(2,1)S(1)}, bf16[16,128,512]{2,1,0:T(8,128)(2,1)}, u32[]{:S(2)}) copy-start(bf16[16,128,512]{2,1,0:T(8,128)(2,1)} %get-tuple-element.64.high_pair) | copy-start | bytes 6291460
  973.3 96.3 %copy-start.3 = (bf16[16,64,512]{2,1,0:T(8,128)(2,1)S(1)}, bf16[16,64,512]{2,1,0:T(8,128)(2,1)}, u32[]{:S(2)}) copy-start(bf16[16,64,512]{2,1,0:T(8,128)(2,1)} %get-tuple-element.53.low_query) | copy-start | bytes 3145732
  1097.8 96.1 %all-to-all-start.6 = ((bf16[16,192,512]{2,1,0:T(8,128)(2,1)}), bf16[16,192,512]{2,1,0:T(8,128)(2,1)S(1)}, u32[]{:S(2)}, u32[]{:S(2)}) async-start(bf16[16,192,512]{2,1,0:T(8,128)(2,1)} %backward_second.1.rest), calls=%async_computation.6 | async-start | bytes 6291456 | tf_op jit(solution)/shard_map/all_to_all | solution.py:580
  1105.0 142.3 %all-gather.19.cloned.1.call-start = ((), (), s32[]{:S(2)}) async-start(), calls=%async_computation.14 | async-start | bytes 3342336 | tf_op jit(solution)/shard_map/all_gather | solution.py:604
  1194.2 22.8 %copy-start.34 = (bf16[1,16,64,512]{3,2,0,1:T(8,128)(2,1)}, bf16[1,16,64,512]{3,2,0,1:T(8,128)(2,1)S(1)}, u32[]{:S(2)}) copy-start(bf16[1,16,64,512]{3,2,0,1:T(8,128)(2,1)S(1)} %slice.192) | copy-start | bytes 3145732
  1194.4 22.6 %copy-start.30 = (bf16[2,16,64,512]{3,2,1,0:T(8,128)(2,1)}, bf16[2,16,64,512]{3,2,1,0:T(8,128)(2,1)S(1)}, u32[]{:S(2)}) copy-start(bf16[2,16,64,512]{3,2,1,0:T(8,128)(2,1)S(1)} %copy.52) | copy-start | bytes 6291460
  1194.4 22.7 %copy-start.19 = (bf16[1,1024,1024]{2,1,0:T(8,128)(2,1)S(1)}, bf16[1,1024,1024]{2,1,0:T(8,128)(2,1)}, u32[]{:S(2)}) copy-start(bf16[1,1024,1024]{2,1,0:T(8,128)(2,1)} %param.13) | copy-start | bytes 6291460
  1194.4 22.7 %copy-start.33 = (bf16[16,64,512]{2,1,0:T(8,128)(2,1)S(1)}, bf16[16,64,512]{2,1,0:T(8,128)(2,1)}, u32[]{:S(2)}) copy-start(bf16[16,64,512]{2,1,0:T(8,128)(2,1)} %copy-done.31) | copy-start | bytes 3145732
  1194.4 22.7 %copy-start.39 = (f32[1024]{0:T(1024)S(1)}, f32[1024]{0:T(1024)}, u32[]{:S(2)}) copy-start(f32[1024]{0:T(1024)} %copy-done.38) | copy-start | bytes 12292
  1194.4 22.7 %copy-start.45 = (f32[1,2,512]{2,0,1:T(1,128)S(1)}, f32[1,2,512]{2,0,1:T(1,128)}, u32[]{:S(2)}) copy-start(f32[1,2,512]{2,0,1:T(1,128)} %copy-done.44) | copy-start | bytes 12292
  1217.0 14.9 %copy-start.48 = (f32[1024]{0:T(1024)S(1)}, f32[1024]{0:T(1024)}, u32[]{:S(2)}) copy-start(f32[1024]{0:T(1024)} %copy-done.47) | copy-start | bytes 12292
  1217.1 16.9 %copy-start.43 = (f32[1024]{0:T(1024)S(1)}, f32[1024]{0:T(1024)}, u32[]{:S(2)}) copy-start(f32[1024]{0:T(1024)} %copy-done.42) | copy-start | bytes 12292
  1237.7 30.4 %all-to-all-start.8 = ((f32[32,1,2048]{2,1,0:T(1,128)}), f32[32,1,2048]{2,1,0:T(1,128)S(1)}, u32[]{:S(2)}, u32[]{:S(2)}) async-start(f32[32,1,2048]{2,1,0:T(1,128)} %reshape.309), calls=%async_computation.8 | async-start | bytes 524288 | tf_op jit(solution)/shard_map/all_to_all | solution.py:635
  (37 other events, 89.0 us)
Sparse Core Ops, SparseCore 0:
  23.8 170.4 all-gather.8
  195.8 33.0 all-gather.10
  230.4 103.9 all-gather.12
  335.8 104.0 all-gather.14
  620.3 352.9 all-reduce.2
  974.7 79.5 all-gather.16
  1111.1 79.5 all-gather.18

commit v2 on v1

--- a/solution.py
+++ b/solution.py
@@ -30,13 +30,13 @@
     return pullback(upstream)
 
 
-def gelu_tanh(values):
-    return jax.nn.gelu(values, approximate=True)
-
-
-def gelu_backward(values, upstream):
-    _, pullback = jax.vjp(gelu_tanh, values)
-    return pullback(upstream)[0]
+def gelu_and_slope(values):
+    squared = values * values
+    scale = math.sqrt(2.0 / math.pi)
+    bent = jnp.tanh(scale * (values * (1.0 + 0.044715 * squared)))
+    half = 0.5 * (1.0 + bent)
+    slope = half + (0.5 * scale) * values * (1.0 - bent * bent) * (1.0 + 0.134145 * squared)
+    return values * half, slope
 
 
 def dot(a, b, ca, cb):
@@ -51,34 +51,36 @@
     return pl.BlockSpec(shape, lambda *_: (0,) * len(shape), pipeline_mode=pl.Buffered(1))
 
 
-def project_kernel(table, a1_first, a1_second, weight, bias, q_t, k_n, v_t):
+def project_kernel(table, *refs):
+    blocks, (weight, bias, q_t, k_n, v_t) = refs[:-5], refs[-5:]
     width = k_n.shape[1]
-    blk = a1_first.shape[0]
-    for half, rows in enumerate((a1_first, a1_second)):
-        part = slice(half * blk, (half + 1) * blk)
-        heads = dot(rows[...], weight[...], 1, 0) + bias[...]
-        turned = jnp.transpose(heads)
-        q_t[:, part] = (turned[:width] * 0.125).astype(bf16)
-        v_t[:, part] = turned[2 * width :].astype(bf16)
-        k_n[part, :] = heads[:, width : 2 * width].astype(bf16)
+    for number, rows in enumerate(blocks):
+        blk = rows.shape[0]
+        part = slice(number * blk, (number + 1) * blk)
+        heads = (dot(rows[...], weight[...], 1, 0) + bias[...]).astype(bf16)
+        turned = jnp.transpose(heads[:, : 2 * width])
+        q_t[:, part] = turned[:width]
+        v_t[:, part] = turned[width:]
+        k_n[part, :] = heads[:, 2 * width :]
 
 
 def project(table, a1_full, weight, bias, blk, width):
     tokens, model = a1_full.shape
-    tile = 2 * blk
+    count = 4
+    tile = count * blk
     turned = pl.BlockSpec((width, tile), lambda i, t: (0, i))
     straight = pl.BlockSpec((tile, width), lambda i, t: (i, 0))
+
+    def block(number):
+        return pl.BlockSpec((blk, model), lambda i, t: (t[count * i + number], 0))
+
     return pl.pallas_call(
         project_kernel,
         grid_spec=pltpu.PrefetchScalarGridSpec(
             num_scalar_prefetch=1,
             grid=(tokens // tile,),
-            in_specs=[
-                pl.BlockSpec((blk, model), lambda i, t: (t[2 * i], 0)),
-                pl.BlockSpec((blk, model), lambda i, t: (t[2 * i + 1], 0)),
-                whole(weight.shape),
-                whole(bias.shape),
-            ],
+            in_specs=[block(number) for number in range(count)]
+            + [whole(weight.shape), whole(bias.shape)],
             out_specs=[turned, straight, turned],
         ),
         out_shape=[
@@ -91,7 +93,7 @@
             flops=8 * tokens * model * width, bytes_accessed=2 * tokens * model, transcendentals=0
         ),
         name="project",
-    )(table, a1_full, a1_full, weight, bias)
+    )(table, *([a1_full] * count), weight, bias)
 
 
 def forward_kernel(base, table, q_t, k_n, v_t, out_t, log_total, out_slots, scores):
@@ -108,9 +110,9 @@
         scores[slot] = tile_scores
         return jnp.max(tile_scores, axis=0, keepdims=True)
 
-    def absorb(index, slot, peak, total, summed, tile_peak):
+    def absorb(index, tile_scores, peak, total, summed, tile_peak):
         new_peak = jnp.maximum(peak, tile_peak)
-        weights = jnp.exp(scores[slot] - new_peak)
+        weights = jnp.exp(tile_scores - new_peak)
         keep = jnp.exp(peak - new_peak)
         total = total * keep + jnp.sum(weights, axis=0, keepdims=True)
         summed = summed * keep + dot(v_t[:, columns(index, blk)], weights.astype(bf16), 1, 0)
@@ -120,7 +122,9 @@
         peak, total, summed, tile_peak = carry
         for slot in range(2):
             next_peak = prepare(2 * pair + slot + 1, 1 - slot)
-            peak, total, summed = absorb(2 * pair + slot, slot, peak, total, summed, tile_peak)
+            peak, total, summed = absorb(
+                2 * pair + slot, scores[slot], peak, total, summed, tile_peak
+            )
             tile_peak = next_peak
         return peak, total, summed, tile_peak
 
@@ -132,13 +136,20 @@
     )
     peak, total, summed, _ = lax.fori_loop(0, step, body, carry)
     for half in range(2):
-        index = 2 * step + half
-        key_pos = half * blk + lax.broadcasted_iota(jnp.int32, (blk, tile), 0)
-        query_pos = lax.broadcasted_iota(jnp.int32, (blk, tile), 1)
-        tile_scores = jnp.where(query_pos >= key_pos, score(index), NEG)
-        scores[half] = tile_scores
+        part = query[:, half * blk :]
+        shape = (blk, tile - half * blk)
+        key_pos = lax.broadcasted_iota(jnp.int32, shape, 0)
+        query_pos = lax.broadcasted_iota(jnp.int32, shape, 1)
+        tile_scores = dot(k_n[columns(2 * step + half, blk), :], part, 1, 0)
+        tile_scores = jnp.where(query_pos >= key_pos, tile_scores, NEG)
         tile_peak = jnp.max(tile_scores, axis=0, keepdims=True)
-        peak, total, summed = absorb(index, half, peak, total, summed, tile_peak)
+        state = absorb(2 * step + half, tile_scores, peak, total, summed, tile_peak)
+        if half == 0:
+            left = tuple(array[:, :blk] for array in state)
+            peak, total, summed = (array[:, blk:] for array in state)
+    peak, total, summed = (
+        jnp.concatenate([first, second], axis=1) for first, second in zip(left, state)
+    )
     result = summed / total
     out_t[...] = result
     log_total[...] = peak + jnp.log(total)
@@ -234,8 +245,8 @@
     query_out = key_out = value_out = None
     if cross:
         (query_start, key_start, value_start), refs = refs[:3], refs[3:]
-    if kind == "second":
-        earlier, refs = refs[0], refs[1:]
+    if kind == "first":
+        low_query, refs = refs[0], refs[1:]
     refs = refs[after:]
     if kind in ("high", "first"):
         query_out, refs = refs[0], refs[1:]
@@ -243,8 +254,10 @@
         (key_out, value_out), refs = refs[:2], refs[2:]
     out_slots, refs = refs[0], refs[1:]
     scores, grads, query_sum, key_sum, value_sum = refs
-    slots, _, blk = out_slots.shape
-    tile, width = k_n.shape
+    _, tile, blk = scores.shape
+    slots = out_slots.shape[0]
+    width = q_t.shape[0]
+    piece = blk // 2
     step = pl.program_id(0)
 
     @pl.when(step == 0)
@@ -253,15 +266,21 @@
             query_sum[...] = query_start[...]
         else:
             query_sum[...] = jnp.zeros_like(query_sum)
-        if kind == "second":
-            out_slots[:, width:] = earlier[...]
-
-    keys = k_n[...]
+        if kind == "first":
+            out_slots[:, :width] = low_query[...]
+
+    keys = k_n[...].reshape(tile, width)
     keys_t = jnp.transpose(keys.astype(f32)).astype(bf16)
-    values = jnp.transpose(v_t[...].astype(f32)).astype(bf16)
     if cross:
-        key_sum[...] = key_start[...]
-        value_sum[...] = value_start[...]
+        start = piece if kind == "second" else 0
+        starts = range(start, v_t.shape[1], blk)
+        values = jnp.concatenate([v_t[:, at : at + piece] for at in starts], axis=1)
+    else:
+        values = v_t[...]
+    values = jnp.transpose(values.astype(f32)).astype(bf16)
+    if cross:
+        key_sum[...] = key_start[...].reshape(tile, width)
+        value_sum[...] = value_start[...].reshape(tile, width)
     else:
         key_sum[...] = jnp.zeros_like(key_sum)
         value_sum[...] = jnp.zeros_like(value_sum)
@@ -271,18 +290,24 @@
         scores[slot] = dot(keys, q_t[:, at], 1, 0)
         grads[slot] = dot(values, grad_t[:, at], 1, 0)
 
-    def absorb(index, slot, diagonal):
+    def absorb(index, tile_scores, prob_grads):
         at = columns(index, blk)
-        tile_scores = scores[slot]
-        if diagonal is not None:
-            key_pos = lax.broadcasted_iota(jnp.int32, (tile, blk), 0)
-            query_pos = diagonal * blk + lax.broadcasted_iota(jnp.int32, (tile, blk), 1)
-            tile_scores = jnp.where(query_pos >= key_pos, tile_scores, NEG)
+        rows = tile_scores.shape[0]
         probs = jnp.exp(tile_scores - log_total[:, at])
-        score_grads = (probs * (grads[slot] - delta[:, at])).astype(bf16)
-        value_sum[...] += dot(probs.astype(bf16), grad_n[at, :], 1, 0)
-        key_sum[...] += dot(score_grads, q_n[at, :], 1, 0)
-        query_sum[:, at] += dot(keys_t, score_grads, 1, 0)
+        score_grads = (probs * (prob_grads - delta[:, at])).astype(bf16)
+        value_sum[:rows] += dot(probs.astype(bf16), grad_n[at, :], 1, 0)
+        key_sum[:rows] += dot(score_grads, q_n[at, :], 1, 0)
+        query_sum[:, at] += dot(keys_t[:, :rows], score_grads, 1, 0)
+
+    def diagonal(half):
+        index = 2 * step + half
+        at = columns(index, blk)
+        shape = ((half + 1) * blk, blk)
+        key_pos = lax.broadcasted_iota(jnp.int32, shape, 0)
+        query_pos = half * blk + lax.broadcasted_iota(jnp.int32, shape, 1)
+        tile_scores = dot(keys[: shape[0]], q_t[:, at], 1, 0)
+        tile_scores = jnp.where(query_pos >= key_pos, tile_scores, NEG)
+        absorb(index, tile_scores, dot(values[: shape[0]], grad_t[:, at], 1, 0))
 
     def sweep(first, pairs):
         prepare(first, 0)
@@ -290,9 +315,9 @@
         def body(pair, carry):
             index = first + 2 * pair
             prepare(index + 1, 1)
-            absorb(index, 0, None)
+            absorb(index, scores[0], grads[0])
             prepare(jnp.minimum(index + 2, slots - 1), 0)
-            absorb(index + 1, 1, None)
+            absorb(index + 1, scores[1], grads[1])
             return carry
 
         lax.fori_loop(0, pairs, body, 0)
@@ -301,43 +326,43 @@
         sweep(0, slots // 2)
     else:
         for half in range(2):
-            prepare(2 * step + half, half)
-            absorb(2 * step + half, half, half)
+            diagonal(half)
 
         @pl.when(2 * step + 2 < slots)
         def _():
             sweep(2 * step + 2, slots // 2 - 1 - step)
 
-    def halves():
-        for half in range(2):
-            yield table[base + 2 * step + half], slice(half * blk, (half + 1) * blk), half
+    def query_grads(index):
+        return (query_sum[:, columns(index, blk)] * 0.125).astype(bf16)
 
     if kind == "low":
         key_out[...] = key_sum[...]
         value_out[...] = value_sum[...]
-        for slot, _, half in halves():
-            own = query_sum[:, columns(2 * step + half, blk)] * 0.125
-            out_slots[slot] = own.astype(bf16)
+        for half in range(2):
+            index = 2 * step + half
+            out_slots[table[base + index]] = query_grads(index)
     else:
-        start = width if kind == "second" else 0
         key_t = jnp.transpose(key_sum[...]).astype(bf16)
         value_t = jnp.transpose(value_sum[...]).astype(bf16)
-        for slot, part, _ in halves():
-            out_slots[slot, start : start + width] = key_t[:, part]
-            out_slots[slot, start + width : start + 2 * width] = value_t[:, part]
-    if query_out is not None:
-
-        @pl.when(step == pl.num_programs(0) - 1)
-        def _():
+        wide = blk if kind == "high" else piece
+        for number in range(tile // wide):
+            slot = table[base + tile // wide * step + number]
+            part = slice(number * wide, (number + 1) * wide)
+            if cross:
+                out_slots[slot, width:, :piece] = key_t[:, part]
+                out_slots[slot, width:, piece:] = value_t[:, part]
+            else:
+                out_slots[slot, :width] = key_t[:, part]
+                out_slots[slot, width:] = value_t[:, part]
+
+    @pl.when(step == pl.num_programs(0) - 1)
+    def _():
+        if query_out is not None:
             query_out[...] = query_sum[...]
-
-    if kind == "second":
-
-        @pl.when(step == pl.num_programs(0) - 1)
-        def _():
+        if kind == "second":
+
             def finish(index, carry):
-                own = query_sum[:, columns(index, blk)] * 0.125
-                out_slots[table[slots + index], 0:width] = own.astype(bf16)
+                out_slots[table[slots + index], :width] = query_grads(index)
                 return carry
 
             lax.fori_loop(0, slots, finish, 0)
@@ -347,23 +372,33 @@
     width, half = queries[0].shape
     slots = half // blk
     tile = 2 * blk
+    piece = blk // 2
     cross = kind in ("first", "second")
+    second = 1 if kind == "second" else 0
     steps = slots // 4 if cross else slots // 2
-    skip = {"high": slots // 2, "low": 0, "first": 0, "second": slots // 4}[kind]
-    start_skip = skip if cross else 0
-    straight = pl.BlockSpec((tile, width), lambda i, t: (start_skip + i, 0))
+    skip = slots // 2 if kind == "high" else 0
+    if cross:
+        straight = pl.BlockSpec((4, 1, piece, width), lambda i, t: (i, second, 0, 0))
+        k_n = k_n.reshape(-1, 2, piece, width)
+        starts = (
+            (starts[0],)
+            + tuple(array.reshape(-1, 2, piece, width) for array in starts[1:3])
+            + tuple(starts[3:])
+        )
+    else:
+        straight = pl.BlockSpec((tile, width), lambda i, t: (skip + i, 0))
     in_specs = [whole(array.shape) for array in queries] + [
-        pl.BlockSpec((tile, width), lambda i, t: (skip + i, 0)),
-        pl.BlockSpec((width, tile), lambda i, t: (0, skip + i)),
+        straight,
+        pl.BlockSpec((width, 4 * blk if cross else tile), lambda i, t: (0, skip + i)),
     ]
     if cross:
         in_specs += [whole((width, half)), straight, straight]
-    if kind == "second":
-        in_specs += [whole(starts[3].shape)]
+        in_specs += [whole(array.shape) for array in starts[3:]]
     in_specs += [pl.BlockSpec(memory_space=pl.ANY)] * len(after)
-    rows = {"high": 2, "low": 1, "first": 2, "second": 3}[kind] * width
-    out_specs = [whole((slots, rows, blk))]
-    out_shape = [jax.ShapeDtypeStruct((slots, rows, blk), bf16)]
+    rows = width if kind == "low" else 2 * width
+    held = (slots, rows, blk)
+    out_specs = [whole(held)]
+    out_shape = [jax.ShapeDtypeStruct(held, bf16)]
     if kind in ("high", "first"):
         out_specs = [whole((width, half))] + out_specs
         out_shape = [jax.ShapeDtypeStruct((width, half), f32)] + out_shape
@@ -396,39 +431,140 @@
     )(table, *queries, k_n, v_t, *starts, *after)
 
 
-def weight_kernel(high_pair, low_query, rest, a1, total):
-    blk = rest.shape[2]
-    width = low_query.shape[1]
-
-    @pl.when(pl.program_id(0) == 0)
+def weight_kernel(high_pair, first, second, a1, *refs):
+    out, total, sums = refs[-3:]
+    _, width, blk = second.shape
+    width //= 2
+    piece = blk // 2
+    parts, rows, length = out.shape
+    step = pl.program_id(0)
+
+    @pl.when(step == 0)
     def _():
         total[...] = jnp.zeros_like(total)
-
-    low = jnp.concatenate([low_query[0], rest[0, width:]], axis=0)
-    high = jnp.concatenate([rest[0, :width], high_pair[0]], axis=0)
+        sums[...] = jnp.zeros_like(sums)
+
+    low_key = jnp.concatenate([first[0, width:, :piece], second[0, width:, :piece]], axis=1)
+    low_value = jnp.concatenate([first[0, width:, piece:], second[0, width:, piece:]], axis=1)
+    low = jnp.concatenate([first[0, :width], low_key, low_value], axis=0)
+    high = jnp.concatenate([second[0, :width], high_pair[0]], axis=0)
     total[...] += dot(low, a1[:blk], 1, 0) + dot(high, a1[blk:], 1, 0)
-
-
-def weight_grad(high_pair, low_query, rest, a1_full):
-    slots, rows, blk = rest.shape
+    wide = low.astype(f32) + high.astype(f32)
+    for at in range(0, blk, 128):
+        sums[...] += wide[:, at : at + 128]
+
+    @pl.when(step == pl.num_programs(0) - 1)
+    def _():
+        row = jnp.sum(jnp.transpose(sums[...]), axis=0, keepdims=True)
+        tail = [row[:, number * width : (number + 1) * width] for number in range(3)]
+        tail = jnp.concatenate(tail, axis=0)
+        tail = jnp.concatenate([tail, jnp.zeros((3, length - width), f32)], axis=1)
+        tail = jnp.concatenate([tail, jnp.zeros((rows - 3 * width - 3, length), f32)], axis=0)
+        for part in range(parts):
+            own = total[:, part * length : (part + 1) * length]
+            out[part] = jnp.concatenate([own, tail], axis=0).astype(bf16)
+
+
+def weight_grad(high_pair, first, second, a1_full, parts, after):
+    slots, width, blk = second.shape
+    width //= 2
     tokens, model = a1_full.shape
+    rows = 3 * width
+    shape = (parts, rows + 16, model // parts)
+    given = (high_pair, first, second)
     return pl.pallas_call(
         weight_kernel,
         grid=(slots,),
-        in_specs=[
-            pl.BlockSpec((1,) + high_pair.shape[1:], lambda s: (s, 0, 0)),
-            pl.BlockSpec((1,) + low_query.shape[1:], lambda s: (s, 0, 0)),
-            pl.BlockSpec((1, rows, blk), lambda s: (s, 0, 0)),
-            pl.BlockSpec((2 * blk, model), lambda s: (s, 0)),
-        ],
-        out_specs=pl.BlockSpec((rows, model), lambda s: (0, 0)),
-        out_shape=jax.ShapeDtypeStruct((rows, model), f32),
+        in_specs=[pl.BlockSpec((1,) + array.shape[1:], lambda s: (s, 0, 0)) for array in given]
+        + [pl.BlockSpec((2 * blk, model), lambda s: (s, 0))]
+        + [pl.BlockSpec(memory_space=pl.ANY)] * len(after),
+        out_specs=whole(shape),
+        out_shape=jax.ShapeDtypeStruct(shape, bf16),
+        scratch_shapes=[pltpu.VMEM((rows, model), f32), pltpu.VMEM((rows, 128), f32)],
         compiler_params=pltpu.CompilerParams(vmem_limit_bytes=48 * MIB),
         cost_estimate=pl.CostEstimate(
             flops=2 * rows * tokens * model, bytes_accessed=2 * tokens * model, transcendentals=0
         ),
         name="weight_grad",
-    )(high_pair, low_query, rest, a1_full)
+    )(*given, a1_full, *after)
+
+
+def mlp_forward_kernel(normed, up, up_bias, down, hidden, slope, total):
+    @pl.when(pl.program_id(0) == 0)
+    def _():
+        total[...] = jnp.zeros_like(total)
+
+    value, bend = gelu_and_slope(dot(normed[...], up[...], 1, 1) + up_bias[...])
+    low = value.astype(bf16)
+    hidden[...] = low
+    slope[...] = bend.astype(bf16)
+    total[...] += dot(low, down[...], 1, 0)
+
+
+def mlp_backward_kernel(grad, down, slope, up, grad_pre, sums, total):
+    @pl.when(pl.program_id(0) == 0)
+    def _():
+        total[...] = jnp.zeros_like(total)
+
+    low = (dot(grad[...], down[...], 1, 1) * slope[...].astype(f32)).astype(bf16)
+    grad_pre[...] = low
+    sums[...] = jnp.sum(low.astype(f32), axis=0, keepdims=True)
+    total[...] += dot(low, up[...], 1, 0)
+
+
+def mlp_grads_kernel(hidden, grad, grad_pre, normed, down_out, up_out):
+    down_out[...] = dot(hidden[...], grad[...], 0, 0).astype(bf16)
+    up_out[...] = dot(grad_pre[...], normed[...], 0, 0).astype(bf16)
+
+
+def mlp_call(kernel, name, operands, kinds, results, result_kinds, rows, model, hidden):
+    chunk = 512
+    specs = {
+        "rows": whole((rows, model)),
+        "wide": pl.BlockSpec((rows, chunk), lambda j: (0, j)),
+        "tall": pl.BlockSpec((chunk, model), lambda j: (j, 0)),
+        "line": pl.BlockSpec((1, chunk), lambda j: (0, j)),
+    }
+    shapes = {
+        "rows": (rows, model),
+        "wide": (rows, hidden),
+        "tall": (hidden, model),
+        "line": (1, hidden),
+    }
+    return pl.pallas_call(
+        kernel,
+        grid=(hidden // chunk,),
+        in_specs=[specs[kind] for kind in kinds],
+        out_specs=[specs[kind] for kind in result_kinds],
+        out_shape=[
+            jax.ShapeDtypeStruct(shapes[kind], dtype) for kind, dtype in zip(result_kinds, results)
+        ],
+        compiler_params=pltpu.CompilerParams(vmem_limit_bytes=56 * MIB),
+        cost_estimate=pl.CostEstimate(
+            flops=4 * rows * model * hidden, bytes_accessed=8 * rows * hidden, transcendentals=0
+        ),
+        name=name,
+    )(*operands)
+
+
+def place_kernel(given, out):
+    count, width, length = given.shape
+    out[...] = jnp.transpose(given[...].reshape(count * width, length)).astype(f32)
+
+
+def place(gathered, width):
+    heads, _, length = gathered.shape
+    count = 4
+    groups = heads // count
+    return pl.pallas_call(
+        place_kernel,
+        grid=(3, groups),
+        in_specs=[pl.BlockSpec((count, width, length), lambda c, i: (i, c, 0))],
+        out_specs=pl.BlockSpec((length, count * width), lambda c, i: (0, c * groups + i)),
+        out_shape=jax.ShapeDtypeStruct((length, 3 * heads * width), f32),
+        compiler_params=pltpu.CompilerParams(vmem_limit_bytes=32 * MIB),
+        name="place",
+    )(gathered)
 
 
 def local(
@@ -481,9 +617,13 @@
         qkv_weight.reshape(-1, 3, HEADS, width), head, axis=2, keepdims=False
     )
     mine = lax.all_gather(mine.reshape(-1, 3 * width), "wt", axis=0, tiled=True)
+    scale = 1.0 / math.sqrt(width)
+    mine = jnp.concatenate(
+        [mine[:, :width] * bf16(scale), mine[:, 2 * width :], mine[:, width : 2 * width]], axis=1
+    )
     q_bias = lax.dynamic_slice(qvbias, (head * width,), (width,))
     v_bias = lax.dynamic_slice(qvbias, (model + head * width,), (width,))
-    bias = jnp.concatenate([q_bias, jnp.zeros_like(q_bias), v_bias])
+    bias = jnp.concatenate([q_bias * scale, v_bias, jnp.zeros_like(q_bias)])
 
     lows = block_order.reshape(devices, 2)[:, 0]
     numbers = jnp.arange(devices, dtype=jnp.int32)
@@ -517,16 +657,30 @@
     proj_pre = dot(attended_t, full_proj, 0, 0) + projbias
     residual = inputs + layer_norm(proj_pre, gains[1], shifts[1])
     normed_mid = layer_norm(residual, gains[2], shifts[2]).astype(bf16)
-    pre_act = dot(normed_mid, up_full, 1, 1) + upbias
-    hidden = gelu_tanh(pre_act).astype(bf16)
-    branch = dot(hidden, down_full, 1, 0) + downbias
+    sizes = (rows, model, up_full.shape[0])
+    hidden, slope, branch = mlp_call(
+        mlp_forward_kernel,
+        "mlp_forward",
+        (normed_mid, up_full, upbias[None, :], down_full),
+        ("rows", "tall", "line", "tall"),
+        (bf16, bf16, f32),
+        ("wide", "wide", "rows"),
+        *sizes,
+    )
+    branch = branch + downbias
     layer_output = (residual + layer_norm(branch, gains[3], shifts[3])).astype(bf16)
 
     grad_branch, gain_three, shift_three = norm_backward(branch, gains[3], shifts[3], upstream)
     grad_branch = grad_branch.astype(bf16)
-    grad_hidden = dot(grad_branch, down_full, 1, 1)
-    grad_pre = gelu_backward(pre_act, grad_hidden).astype(bf16)
-    grad_mid = dot(grad_pre, up_full, 1, 0)
+    grad_pre, up_sums, grad_mid = mlp_call(
+        mlp_backward_kernel,
+        "mlp_backward",
+        (grad_branch, down_full, slope, up_full),
+        ("rows", "tall", "wide", "tall"),
+        (bf16, f32, f32),
+        ("wide", "line", "rows"),
+        *sizes,
+    )
     grad_residual, gain_two, shift_two = norm_backward(residual, gains[2], shifts[2], grad_mid)
     grad_residual = upstream + grad_residual
     grad_proj_pre, gain_one, shift_one = norm_backward(
@@ -537,8 +691,15 @@
     given_high = to_heads(grad_attended_t[:, blk:])
     given_low = to_heads(grad_attended_t[:, :blk])
 
-    grad_downward = dot(hidden, grad_branch, 0, 0).astype(bf16)
-    grad_upward = dot(grad_pre, normed_mid, 0, 0).astype(bf16)
+    grad_downward, grad_upward = mlp_call(
+        mlp_grads_kernel,
+        "mlp_grads",
+        (hidden, grad_branch, grad_pre, normed_mid),
+        ("wide", "rows", "wide", "rows"),
+        (bf16, bf16),
+        ("tall", "tall"),
+        *sizes,
+    )
     grad_proj = dot(attended_t, grad_proj_pre, 1, 0).astype(bf16)
 
     def own_rows(array):
@@ -547,7 +708,7 @@
 
     early = jnp.concatenate(
         [
-            jnp.sum(grad_pre.astype(f32), axis=0),
+            up_sums[0],
             jnp.sum(grad_branch.astype(f32), axis=0),
             jnp.sum(grad_proj_pre.astype(f32), axis=0),
             gain_one,
@@ -559,8 +720,8 @@
         ]
     ).astype(bf16)
     grad_proj = jnp.concatenate([grad_proj, early.reshape(-1, model)], axis=0)
-    given_high, given_low, grad_downward, grad_upward, grad_proj = lax.optimization_barrier(
-        (given_high, given_low, grad_downward, grad_upward, grad_proj)
+    given_high, grad_downward, grad_upward, grad_proj = lax.optimization_barrier(
+        (given_high, grad_downward, grad_upward, grad_proj)
     )
     summed = lax.psum((grad_downward, grad_upward, grad_proj), everywhere)
     grad_downward, grad_upward, grad_proj = summed
@@ -577,8 +738,9 @@
 
     def token_grads(array):
         own = lax.dynamic_slice_in_dim(array, group * HEADS, HEADS, 0)
-        own = lax.all_to_all(own, "h", 0, 0, tiled=True).reshape(HEADS, -1, width, blk)
-        return jnp.transpose(own, (1, 0, 2, 3)).reshape(-1, blk)
+        own = lax.all_to_all(own, "h", 0, 0, tiled=True)
+        own = own.reshape(HEADS, -1, width, array.shape[2])
+        return jnp.transpose(own, (1, 0, 2, 3)).reshape(-1, array.shape[2])
 
     grad_t, grad_n, delta, q_n = delta_rows(True, owner, given_high, out_high, q_t)
     high = (q_t[:, half:], q_n, grad_t, grad_n, log_high, delta)
@@ -587,58 +749,54 @@
     grad_t, grad_n, delta, q_n = delta_rows(False, owner, given_low, out_low, q_t)
     low = (q_t[:, :half], q_n, grad_t, grad_n, log_low, delta)
     key_sum, value_sum, low_query = backward("low", owner, low, k_n, v_t, (), (), blk)
-    low_tokens = token_grads(low_query)
+    starts = (query_sum, key_sum, value_sum, low_query)
+    query_sum, first = backward("first", owner, high, k_n, v_t, starts, (high_tokens,), blk)
+    first_tokens = token_grads(first)
     starts = (query_sum, key_sum, value_sum)
-    query_sum, earlier = backward(
-        "first", owner, high, k_n, v_t, starts, (high_tokens,), blk
-    )
-    starts = (query_sum, key_sum, value_sum, earlier)
-    after = (low_tokens,) + tuple(summed)
-    (rest,) = backward("second", owner, high, k_n, v_t, starts, after, blk)
-    rest_tokens = token_grads(rest)
-
-    columns_grad = weight_grad(high_pair, low_query, rest, a1_full).T.astype(bf16)
-    columns_grad = columns_grad.reshape(weight_parts, -1, 3 * width)
+    (second,) = backward("second", owner, high, k_n, v_t, starts, (), blk)
+    second_tokens = token_grads(second)
+
+    def own_columns(array):
+        length = array.shape[1] // weight_parts
+        return lax.dynamic_slice_in_dim(array, part * length, length, 1)
+
+    after = (first_tokens,) + tuple(summed)
+    columns_grad = weight_grad(high_pair, first, second, a1_full, weight_parts, after)
     columns_grad = lax.all_to_all(columns_grad, "wt", 0, 0, tiled=True)
     columns_grad = jnp.sum(columns_grad.astype(f32), axis=0).astype(bf16)
     all_columns = lax.all_gather(columns_grad, "h", axis=0)
-    all_columns = all_columns.reshape(HEADS, -1, 3, width)
-    grad_qkv = jnp.transpose(all_columns, (1, 2, 0, 3)).reshape(-1, 3 * model).astype(f32)
-
+    grad_qkv = place(all_columns, width)
+    sums = all_columns[:, 3 * width : 3 * width + 3, :width].astype(f32)
+    sums = jnp.transpose(sums, (1, 0, 2)).reshape(3, model)
+    grad_qvbias = own_rows(jnp.concatenate([sums[0], sums[2]]))
+
+    own_weight = qkv_weight.astype(f32)
+    shift_zero = jnp.sum(own_weight * sums.reshape(1, -1), axis=1)
+    gain_zero = jnp.sum(own_weight * grad_qkv, axis=1)
+    first_norm = own_columns(jnp.stack([gains[0], shifts[0]]))
+    gain_zero = (gain_zero - first_norm[1] * shift_zero) / first_norm[0]
+
+    second_tokens, grad_downward, grad_upward, grad_proj = lax.optimization_barrier(
+        (second_tokens, grad_downward, grad_upward, grad_proj)
+    )
+    piece = blk // 2
+    low_key = [first_tokens[model:, :piece], second_tokens[model:, :piece]]
+    low_value = [first_tokens[model:, piece:], second_tokens[model:, piece:]]
+    low_rows = [
+        first_tokens[:model],
+        jnp.concatenate(low_key, axis=1),
+        jnp.concatenate(low_value, axis=1),
+    ]
+    high_rows = [second_tokens[:model], high_tokens]
     grads_t = jnp.concatenate(
-        [
-            jnp.concatenate([low_tokens, rest_tokens[model:]], axis=0),
-            jnp.concatenate([rest_tokens[:model], high_tokens], axis=0),
-        ],
-        axis=1,
+        [jnp.concatenate(low_rows, axis=0), jnp.concatenate(high_rows, axis=0)], axis=1
     )
     grad_normed = dot(grads_t, full_qkv, 0, 1)
-    grad_inputs, gain_zero, shift_zero = norm_backward(inputs, gains[0], shifts[0], grad_normed)
+    grad_inputs, _, _ = norm_backward(inputs, gains[0], shifts[0], grad_normed)
     input_grad = (grad_residual + grad_inputs).reshape(1, rows, model)
-    bias_sums = jnp.sum(grads_t.astype(f32), axis=1)
-
-    def own_columns(array):
-        length = array.shape[1] // weight_parts
-        return lax.dynamic_slice_in_dim(array, part * length, length, 1)
-
-    late = jnp.concatenate([bias_sums[:model], bias_sums[2 * model :], gain_zero, shift_zero])
-    late = jnp.concatenate(
-        [
-            late[: 2 * model].reshape(weight_parts, -1),
-            late[2 * model : 3 * model].reshape(weight_parts, -1),
-            late[3 * model :].reshape(weight_parts, -1),
-        ],
-        axis=1,
-    )
-    late = jnp.broadcast_to(late[None], (devices,) + late.shape)
-    late = late.reshape(devices * weight_parts, 1, -1)
-    late = jnp.sum(lax.all_to_all(late, everywhere, 0, 0, tiled=True), axis=0)[0]
-    length = model // weight_parts
-    grad_qvbias = late[: 2 * length]
-    late = late[2 * length :].reshape(2, length)
     early = own_columns(early)
-    grad_gains = jnp.concatenate([late[0:1], early[2:5]], axis=0)
-    grad_biases = jnp.concatenate([late[1:2], early[5:8]], axis=0)
+    grad_gains = jnp.concatenate([gain_zero[None], early[2:5]], axis=0)
+    grad_biases = jnp.concatenate([shift_zero[None], early[5:8]], axis=0)
     return (
         layer_output.reshape(1, rows, model),
         input_grad,

time: 1290 us -> 1200 us (0.930)
  matrix products: 135 us -> 28.2 us
  Pallas kernels: 652 us -> 716 us
  waiting for transfers between devices: 265 us -> 249 us
  local copies, waits for them, and re-layouts: 68.9 us -> 55.6 us
    dot_general x10 -> x4, matrix products: 135 us -> 28.2 us  [dot(): lax.dot_general(a, b, (((ca,), (cb,)), ((), ())), preferred_element_type=...]
    pallas_call x0 -> x4, Pallas kernels: none -> 84.3 us  [the longest x3 78.5 us: mlp_call(): pl.pallas_call(kernel, grid=(hidden // chunk,), in_specs=[specs[kind] for...]
    all_to_all x2, waiting for transfers between devices: 16.3 us -> 0.03 us  [to_heads(): lax.all_to_all(array.reshape(HEADS, width, blk), 'h', 0, 0, tiled=True)]
    reduce_sum x2 -> x1, other arithmetic: 20.1 us -> 4.19 us  [local(): shift_zero = jnp.sum(own_weight * sums.reshape(1, -1), axis=1)]
    unnamed x132 -> x148, local copies, waits for them, and re-layouts: 44.8 us -> 33.9 us
    all_to_all x4 -> x3, waiting for transfers between devices: 64.5 us -> 67.1 us  [token_grads(): own = lax.all_to_all(own, 'h', 0, 0, tiled=True)]
  transfers between devices with their start and end apart: 15 -> 14, of which waited for: 6 -> 3; matrix products, arithmetic and copies ran while one was open for 13% -> 6% of each run, Pallas kernels for 51% -> 55%
where the time goes in v2:
time: 1200 us; the launch traced here: 1190 us
  Pallas kernels  716 us (60%)
  waiting for transfers between devices  249 us (21%)
  other arithmetic  64.6 us (5%)
  local copies, waits for them, and re-layouts  55.6 us (5%)
  starting transfers between devices  42.6 us (4%)
  matrix products  28.2 us (2%)
  blocking collectives  19 us (2%)
  between operations  15.5 us (1%)
    pallas_call x4, Pallas kernels, backward(): pl.pallas_call(functools.partial(backward_kernel, kind, 2 * skip, len(aft...  398 us
    pallas_call x2, Pallas kernels, forward(): pl.pallas_call(functools.partial(forward_kernel, base), grid_spec=pltpu.P...  183 us
    all_gather x1, waiting for transfers between devices, local(): a1_full = lax.all_gather(a1, ctx, axis=0, tiled=True)  156 us
    pallas_call x3, Pallas kernels, mlp_call(): pl.pallas_call(kernel, grid=(hidden // chunk,), in_specs=[specs[kind] for...  78.5 us
    all_to_all x3, waiting for transfers between devices, token_grads(): own = lax.all_to_all(own, 'h', 0, 0, tiled=True)  67.1 us
    unnamed x148, local copies, waits for them, and re-layouts  33.9 us
    dot_general x4, matrix products, dot(): lax.dot_general(a, b, (((ca,), (cb,)), ((), ())), preferred_element_type=...  28.2 us
  transfers between devices with their start and end apart: 14, of which 3 were waited for; matrix products, arithmetic and copies ran while one was open for 6% of the time, Pallas kernels for 55%

profile of v2, /device:TPU:13, one launch (start us, length us, event | category | flops | bytes accessed | tf_op | source)
XLA Modules:
  0.0 1191.1 jit_solution(2305595473979910132)
XLA Ops:
  30.6 6.8 all_gather.33
  38.0 156.2 %all-gather.9.cloned.1.call-done.refs_0_.refs_1_.refs_2_.refs_3_.a1 = bf16[16384,1024]{1,0:T(8,128)(2,1)} async-done(((bf16[1024,1024]{1,0:T(8,128)(2,1)}), bf16[16384,1024]{1,0:T(8,128)(2,1)}) %all-gather.9.cloned.1.call-update) | async-done | bytes 33554448 | tf_op jit(solution)/shard_map/all_gather | solution.py:614
  194.2 18.5 %project.1 = (bf16[64,16384]{1,0:T(8,128)(2,1)S(1)}, bf16[16384,64]{1,0:T(8,128)(2,1)}, bf16[64,16384]{1,0:T(8,128)(2,1)S(1)}) custom-call(s32[32]{0:T(128)S(1)} %get-tuple-element.120.table, bf16[16384,1024]{1,0:T(8,128)(2,1)} %all-gather.9.cloned.1.call-done.refs_0_.refs_1_.refs_2_.refs_3_.a1, ...), custom_call_target="tpu_custom_call" | custom-call | flops 8589934592 | bytes 33554432 | tf_op jit(solution)/shard_map/project/pallas_call | solution.py:77
  215.4 130.9 %forward_high.1 = (f32[64,8192]{1,0:T(8,128)}, f32[1,8192]{1,0:T(1,128)}, bf16[16,64,512]{2,1,0:T(8,128)(2,1)}) custom-call(s32[32]{0:T(128)} %get-tuple-element.121.table.refs_0_, bf16[64,16384]{1,0:T(8,128)(2,1)} %copy-done, bf16[16384,64]{1,0:T(8,128)(2,1)} %get-tuple-element.53.k_n.refs_7_, bf16[64,16384]{1,0:T(8,128)(2,1)} %copy-done.9), custom_call_target="tpu_custom_call" | custom-call | flops 103079215104 | bytes 12582912 | tf_op jit(solution)/shard_map/forward_high/pallas_call | solution.py:168
  346.4 5.4 all-to-all-start.1
  351.9 52.0 %forward_low.1 = (f32[64,8192]{1,0:T(8,128)}, f32[1,8192]{1,0:T(1,128)}, bf16[16,64,512]{2,1,0:T(8,128)(2,1)}) custom-call(s32[32]{0:T(128)} %get-tuple-element.121.table.refs_0_, bf16[64,16384]{1,0:T(8,128)(2,1)} %copy-done, bf16[16384,64]{1,0:T(8,128)(2,1)} %get-tuple-element.53.k_n.refs_7_, bf16[64,16384]{1,0:T(8,128)(2,1)} %copy-done.9), custom_call_target="tpu_custom_call" | custom-call | flops 34359738368 | bytes 12582912 | tf_op jit(solution)/shard_map/forward_low/pallas_call | solution.py:168
  403.9 6.3 all-to-all-start
  412.1 23.3 %all-to-all-done = bf16[16,64,512]{2,1,0:T(8,128)(2,1)} async-done(((bf16[16,64,512]{2,1,0:T(8,128)(2,1)}), bf16[16,64,512]{2,1,0:T(8,128)(2,1)}, u32[]{:S(2)}, u32[]{:S(2)}) %all-to-all-start) | async-done | bytes 1048608 | tf_op jit(solution)/shard_map/all_to_all | solution.py:642
  435.3 4.4 add_reduce_fusion.1
  448.8 30.5 %mlp_forward.1 = (bf16[1024,4096]{1,0:T(8,128)(2,1)}, bf16[1024,4096]{1,0:T(8,128)(2,1)}, f32[1024,1024]{1,0:T(8,128)}) custom-call(bf16[1024,1024]{1,0:T(8,128)(2,1)} %add_convert_fusion.3.normed, bf16[4096,1024]{1,0:T(8,128)(2,1)} %all-gather.13.cloned.1.call-done.up, f32[1,4096]{1,0:T(1,128)} %bitcast.190, ...), custom_call_target="tpu_custom_call" | custom-call | flops 17179869184 | bytes 33554432 | tf_op jit(solution)/shard_map/mlp_forward/pallas_call | solution.py:534
  485.7 3.7 fusion.49
  491.1 24.8 %mlp_backward.1 = (bf16[1024,4096]{1,0:T(8,128)(2,1)}, f32[1,4096]{1,0:T(1,128)}, f32[1024,1024]{1,0:T(8,128)}) custom-call(bf16[1024,1024]{1,0:T(8,128)(2,1)} %get-tuple-element.110.grad, bf16[4096,1024]{1,0:T(8,128)(2,1)} %all-gather.15.cloned.1.call-done.down, bf16[1024,4096]{1,0:T(8,128)(2,1)} %get-tuple-element.58.slope, ...), custom_call_target="tpu_custom_call" | custom-call | flops 17179869184 | bytes 33554432 | tf_op jit(solution)/shard_map/mlp_backward/pallas_call | solution.py:534
  527.4 3.7 convolution_convert_fusion
  534.9 5.0 all-to-all-start.2
  541.8 23.1 %mlp_grads.1 = (bf16[4096,1024]{1,0:T(8,128)(2,1)}, bf16[4096,1024]{1,0:T(8,128)(2,1)}) custom-call(bf16[1024,4096]{1,0:T(8,128)(2,1)} %get-tuple-element.60.hidden, bf16[1024,1024]{1,0:T(8,128)(2,1)} %get-tuple-element.110.grad, bf16[1024,4096]{1,0:T(8,128)(2,1)} %get-tuple-element.61.grad_pre, bf16[1024,1024]{1,0:T(8,128)(2,1)} %add_convert_fusion.3.normed), custom_call_target="tpu_custom_call" | custom-call | flops 17179869184 | bytes 33554432 | tf_op jit(solution)/shard_map/mlp_grads/pallas_call | solution.py:534
  564.8 6.0 all-to-all-start.3
  582.5 105.0 %backward_high.1 = (f32[64,8192]{1,0:T(8,128)}, bf16[16,128,512]{2,1,0:T(8,128)(2,1)}) custom-call(s32[32]{0:T(128)} %get-tuple-element.121.table.refs_0_, bf16[64,8192]{1,0:T(8,128)(2,1)} %get-tuple-element.132.refs_1_, bf16[8192,64]{1,0:T(8,128)(2,1)} %copy-done.11, bf16[64,8192]{1,0:T(8,128)(2,1)} %copy-done.14, bf16[8192,64]{1,0:T(8,128)(2,1)} %copy-done.10, ...), custom_call_target="tpu_custom_call" | custom-call | flops 17179869184 | bytes 16777216 | tf_op jit(solution)/shard_map/backward_high/pallas_call | solution.py:408
  687.4 6.3 all-to-all-start.4
  695.3 8.8 delta_low.1
  708.4 102.2 %backward_low.1 = (f32[8192,64]{1,0:T(8,128)}, f32[8192,64]{1,0:T(8,128)}, bf16[16,64,512]{2,1,0:T(8,128)(2,1)}) custom-call(s32[32]{0:T(128)} %get-tuple-element.121.table.refs_0_, bf16[64,8192]{1,0:T(8,128)(2,1)} %get-tuple-element.131.refs_1_, bf16[8192,64]{1,0:T(8,128)(2,1)} %copy-done.13, bf16[64,8192]{1,0:T(8,128)(2,1)} %copy-done.15, ...), custom_call_target="tpu_custom_call" | custom-call | flops 17179869184 | bytes 16777216 | tf_op jit(solution)/shard_map/backward_low/pallas_call | solution.py:408
  813.7 96.2 %backward_first.1 = (f32[64,8192]{1,0:T(8,128)}, bf16[16,128,512]{2,1,0:T(8,128)(2,1)}) custom-call(s32[32]{0:T(128)} %get-tuple-element.121.table.refs_0_, bf16[64,8192]{1,0:T(8,128)(2,1)} %get-tuple-element.132.refs_1_, bf16[8192,64]{1,0:T(8,128)(2,1)} %copy-done.11, bf16[64,8192]{1,0:T(8,128)(2,1)} %copy-done.14, bf16[8192,64]{1,0:T(8,128)(2,1)} %copy-done.10, ...), custom_call_target="tpu_custom_call" | custom-call | flops 17179869184 | bytes 16777216 | tf_op jit(solution)/shard_map/backward_first/pallas_call | solution.py:408
  909.9 6.0 all-to-all-start.5
  916.5 95.1 %backward_second.1.second = bf16[16,128,512]{2,1,0:T(8,128)(2,1)} custom-call(s32[32]{0:T(128)} %get-tuple-element.121.table.refs_0_, bf16[64,8192]{1,0:T(8,128)(2,1)} %get-tuple-element.132.refs_1_, bf16[8192,64]{1,0:T(8,128)(2,1)} %copy-done.11, bf16[64,8192]{1,0:T(8,128)(2,1)} %copy-done.14, bf16[8192,64]{1,0:T(8,128)(2,1)} %copy-done.10, ...), custom_call_target="tpu_custom_call" | custom-call | flops 17179869184 | bytes 16777216 | tf_op jit(solution)/shard_map/backward_second/pallas_call | solution.py:408
  1016.5 19.9 %weight_grad.1 = bf16[2,208,512]{2,1,0:T(8,128)(2,1)S(1)} custom-call(bf16[16,128,512]{2,1,0:T(8,128)(2,1)S(1)} %copy-done.2, bf16[16,128,512]{2,1,0:T(8,128)(2,1)S(1)} %copy-done.3, bf16[16,128,512]{2,1,0:T(8,128)(2,1)} %backward_second.1.second, bf16[16384,1024]{1,0:T(8,128)(2,1)} %all-gather.9.cloned.1.call-done.refs_0_.refs_1_.refs_2_.refs_3_.a1, ...), custom_call_target="tpu_custom_call" | custom-call | flops 6442450944 | bytes 33554432 | tf_op jit(solution)/shard_map/weight_grad/pallas_call | solution.py:475
  1036.3 9.0 all_to_all.40
  1045.3 7.0 all-to-all-start.6
  1053.3 67.1 %all-to-all-done.6 = bf16[16,128,512]{2,1,0:T(8,128)(2,1)} async-done(((bf16[16,128,512]{2,1,0:T(8,128)(2,1)}), bf16[16,128,512]{2,1,0:T(8,128)(2,1)}, u32[]{:S(2)}, u32[]{:S(2)}) %all-to-all-start.6) | async-done | bytes 2097184 | tf_op jit(solution)/shard_map/all_to_all | solution.py:741
  1126.6 11.8 dynamic-slice_convert_fusion
  1144.5 17.7 %fusion.29 = (f32[1024]{0:T(1024)S(1)}, f32[1024,1024]{1,0:T(8,128)}) fusion(bf16[1,1024,1024]{2,1,0:T(8,128)(2,1)S(1)} %copy-done.22, f32[1024]{0:T(1024)S(1)} %bitcast.175, f32[1024]{0:T(1024)S(1)} %copy-done.38, bf16[1024,3072]{1,0:T(8,128)(2,1)} %all-gather.17.cloned.1.call-done, bf16[2048,512]{1,0:T(8,128)(2,1)} %bitcast.154, ...), kind=kOutput, calls=%fused_computation.40 | convolution fusion | flops 6491732992 | bytes 18886656 | tf_op jit(solution)/shard_map/dot_general | solution.py:43
  1165.8 4.5 add_bitcast_fusion
  1172.3 5.8 place.1
  1178.4 4.2 fusion.1
  (261 shorter events, 108.3 us)
Async XLA Ops:
  7.2 14.3 %copy-start.20 = (bf16[1,1024,1024]{2,1,0:T(8,128)(2,1)S(1)}, bf16[1,1024,1024]{2,1,0:T(8,128)(2,1)}, u32[]{:S(2)}) copy-start(bf16[1,1024,1024]{2,1,0:T(8,128)(2,1)} %param.13) | copy-start | bytes 6291460
  7.2 187.0 %all-gather.9.cloned.1.call-start = ((), (), s32[]{:S(2)}) async-start(), calls=%async_computation.8 | async-start | bytes 35651584 | tf_op jit(solution)/shard_map/all_gather | solution.py:614
  15.3 10.4 copy-start.36
  17.2 6.4 copy-start.40
  23.6 388.4 %all-gather.11.cloned.1.call-start = ((), (), s32[]{:S(2)}) async-start(), calls=%async_computation.9 | async-start | bytes 3145728 | tf_op jit(solution)/shard_map/all_gather | solution.py:652
  24.4 424.4 %all-gather.13.cloned.1.call-start = ((), (), s32[]{:S(2)}) async-start(), calls=%async_computation.10 | async-start | bytes 12582912 | tf_op jit(solution)/shard_map/all_gather | solution.py:653
  25.1 423.6 %all-gather.15.cloned.1.call-start = ((), (), s32[]{:S(2)}) async-start(), calls=%async_computation.11 | async-start | bytes 12582912 | tf_op jit(solution)/shard_map/all_gather | solution.py:654
  346.4 57.5 %all-to-all-start.1 = ((bf16[16,64,512]{2,1,0:T(8,128)(2,1)}), bf16[16,64,512]{2,1,0:T(8,128)(2,1)S(1)}, u32[]{:S(2)}, u32[]{:S(2)}) async-start(bf16[16,64,512]{2,1,0:T(8,128)(2,1)} %get-tuple-element.56), calls=%async_computation.1 | async-start | bytes 2097152 | tf_op jit(solution)/shard_map/all_to_all | solution.py:642
  351.8 58.4 %copy-start.52 = (f32[1,4,2,128]{3,2,1,0:T(2,128)S(1)}, f32[1,4,2,128]{3,2,1,0:T(2,128)}, u32[]{:S(2)}) copy-start(f32[1,4,2,128]{3,2,1,0:T(2,128)} %get-tuple-element.148) | copy-start | bytes 12292
  351.8 58.5 %copy-start.53 = (f32[1,4,2,128]{3,2,1,0:T(2,128)S(1)}, f32[1,4,2,128]{3,2,1,0:T(2,128)}, u32[]{:S(2)}) copy-start(f32[1,4,2,128]{3,2,1,0:T(2,128)} %get-tuple-element.153) | copy-start | bytes 12292
  351.8 59.2 %copy-start.49 = (f32[1,4,2,128]{3,2,1,0:T(2,128)S(1)}, f32[1,4,2,128]{3,2,1,0:T(2,128)}, u32[]{:S(2)}) copy-start(f32[1,4,2,128]{3,2,1,0:T(2,128)} %get-tuple-element.147) | copy-start | bytes 12292
  351.8 59.2 %copy-start.51 = (f32[1,4,2,128]{3,2,1,0:T(2,128)S(1)}, f32[1,4,2,128]{3,2,1,0:T(2,128)}, u32[]{:S(2)}) copy-start(f32[1,4,2,128]{3,2,1,0:T(2,128)} %get-tuple-element.152) | copy-start | bytes 12292
  351.8 59.2 %copy-start.39 = (f32[1,1,2,2048]{3,2,1,0:T(2,128)S(1)}, f32[1,1,2,2048]{3,2,1,0:T(2,128)}, u32[]{:S(2)}) copy-start(f32[1,1,2,2048]{3,2,1,0:T(2,128)} %get-tuple-element.142) | copy-start | bytes 49156
  351.8 59.8 %copy-start.50 = (f32[1,4,2,128]{3,2,1,0:T(2,128)S(1)}, f32[1,4,2,128]{3,2,1,0:T(2,128)}, u32[]{:S(2)}) copy-start(f32[1,4,2,128]{3,2,1,0:T(2,128)} %get-tuple-element.151) | copy-start | bytes 12292
  351.9 59.8 %copy-start.48 = (f32[1,4,2,128]{3,2,1,0:T(2,128)S(1)}, f32[1,4,2,128]{3,2,1,0:T(2,128)}, u32[]{:S(2)}) copy-start(f32[1,4,2,128]{3,2,1,0:T(2,128)} %get-tuple-element.146) | copy-start | bytes 12292
  351.9 59.8 %copy-start.28 = (bf16[1,1024,1024]{2,1,0:T(8,128)(2,1)S(1)}, bf16[1,1024,1024]{2,1,0:T(8,128)(2,1)}, u32[]{:S(2)}) copy-start(bf16[1,1024,1024]{2,1,0:T(8,128)(2,1)} %param.25) | copy-start | bytes 6291460
  403.9 35.9 %copy-start.34 = (bf16[16,64,512]{2,1,0:T(8,128)(2,1)}, bf16[16,64,512]{2,1,0:T(8,128)(2,1)S(1)}, u32[]{:S(2)}) copy-start(bf16[16,64,512]{2,1,0:T(8,128)(2,1)S(1)} %all-to-all-done.1) | copy-start | bytes 3145732
  403.9 31.5 %all-to-all-start = ((bf16[16,64,512]{2,1,0:T(8,128)(2,1)}), bf16[16,64,512]{2,1,0:T(8,128)(2,1)}, u32[]{:S(2)}, u32[]{:S(2)}) async-start(bf16[16,64,512]{2,1,0:T(8,128)(2,1)} %get-tuple-element.55), calls=%async_computation | async-start | bytes 2097152 | tf_op jit(solution)/shard_map/all_to_all | solution.py:642
  533.5 6.5 copy-start.54
  534.9 29.9 %all-to-all-start.2 = ((bf16[16,64,512]{2,1,0:T(8,128)(2,1)}), bf16[16,64,512]{2,1,0:T(8,128)(2,1)S(1)}, u32[]{:S(2)}, u32[]{:S(2)}) async-start(bf16[16,64,512]{2,1,0:T(8,128)(2,1)} %bitcast.16), calls=%async_computation.2 | async-start | bytes 2097152 | tf_op jit(solution)/shard_map/all_to_all | solution.py:645
  564.8 122.6 %all-to-all-start.3 = ((bf16[16,64,512]{2,1,0:T(8,128)(2,1)}), bf16[16,64,512]{2,1,0:T(8,128)(2,1)}, u32[]{:S(2)}, u32[]{:S(2)}) async-start(bf16[16,64,512]{2,1,0:T(8,128)(2,1)} %bitcast.18), calls=%async_computation.3 | async-start | bytes 2097152 | tf_op jit(solution)/shard_map/all_to_all | solution.py:645
  570.8 444.0 %all-reduce.3.cloned.1.call-start = ((), (), s32[]{:S(2)}) async-start(), calls=%async_computation.14 | async-start | bytes 37814272 | tf_op jit(solution)/shard_map/psum | solution.py:726
  687.4 123.2 %all-to-all-start.4 = ((bf16[16,128,512]{2,1,0:T(8,128)(2,1)}), bf16[16,128,512]{2,1,0:T(8,128)(2,1)}, u32[]{:S(2)}, u32[]{:S(2)}) async-start(bf16[16,128,512]{2,1,0:T(8,128)(2,1)} %get-tuple-element.82.high_pair), calls=%async_computation.4 | async-start | bytes 4194304 | tf_op jit(solution)/shard_map/all_to_all | solution.py:741
  909.9 101.7 %all-to-all-start.5 = ((bf16[16,128,512]{2,1,0:T(8,128)(2,1)}), bf16[16,128,512]{2,1,0:T(8,128)(2,1)}, u32[]{:S(2)}, u32[]{:S(2)}) async-start(bf16[16,128,512]{2,1,0:T(8,128)(2,1)} %get-tuple-element.83.first), calls=%async_computation.5 | async-start | bytes 4194304 | tf_op jit(solution)/shard_map/all_to_all | solution.py:741
  915.9 228.6 %all-gather.17.cloned.1.call-start = ((), (), s32[]{:S(2)}) async-start(), calls=%async_computation.12 | async-start | bytes 9437184 | tf_op jit(solution)/shard_map/all_gather | solution.py:655
  1036.3 16.9 %copy-start.47 = (f32[1,1,2,512]{3,2,1,0:T(2,128)S(1)}, f32[1,1,2,512]{3,2,1,0:T(2,128)}, u32[]{:S(2)}) copy-start(f32[1,1,2,512]{3,2,1,0:T(2,128)} %get-tuple-element.150) | copy-start | bytes 12292
  1036.3 16.9 %copy-start.46 = (f32[1,1,2,512]{3,2,1,0:T(2,128)S(1)}, f32[1,1,2,512]{3,2,1,0:T(2,128)}, u32[]{:S(2)}) copy-start(f32[1,1,2,512]{3,2,1,0:T(2,128)} %get-tuple-element.145) | copy-start | bytes 12292
  1045.3 78.5 %copy-start.31 = (bf16[16,2,64,512]{3,2,0,1:T(8,128)(2,1)S(1)}, bf16[16,2,64,512]{3,2,0,1:T(8,128)(2,1)}, u32[]{:S(2)}) copy-start(bf16[16,2,64,512]{3,2,0,1:T(8,128)(2,1)} %copy.80) | copy-start | bytes 6291460
  1045.3 75.2 %all-to-all-start.6 = ((bf16[16,128,512]{2,1,0:T(8,128)(2,1)}), bf16[16,128,512]{2,1,0:T(8,128)(2,1)}, u32[]{:S(2)}, u32[]{:S(2)}) async-start(bf16[16,128,512]{2,1,0:T(8,128)(2,1)} %backward_second.1.second), calls=%async_computation.6 | async-start | bytes 4194304 | tf_op jit(solution)/shard_map/all_to_all | solution.py:741
  1052.3 118.0 %all-gather.19.cloned.1.call-start = ((), (), s32[]{:S(2)}) async-start(), calls=%async_computation.13 | async-start | bytes 3620864 | tf_op jit(solution)/shard_map/all_gather | solution.py:767
  1144.5 17.7 %copy-start.45 = (f32[1024]{0:T(1024)S(1)}, f32[1024]{0:T(1024)}, u32[]{:S(2)}) copy-start(f32[1024]{0:T(1024)} %copy-done.44) | copy-start | bytes 12292
  1144.5 17.8 %copy-start.43 = (f32[1024]{0:T(1024)S(1)}, f32[1024]{0:T(1024)}, u32[]{:S(2)}) copy-start(f32[1024]{0:T(1024)} %copy-done.42) | copy-start | bytes 12292
  (39 other events, 105.6 us)
Sparse Core Ops, SparseCore 0:
  23.7 170.4 all-gather.8
  195.7 33.0 all-gather.10
  230.3 104.0 all-gather.12
  335.8 103.9 all-gather.14
  578.4 361.4 all-reduce.2
  941.2 94.1 all-gather.16
  1055.5 64.8 all-gather.18

commit v3 on v2

--- a/solution.py
+++ b/solution.py
@@ -110,31 +110,29 @@
         scores[slot] = tile_scores
         return jnp.max(tile_scores, axis=0, keepdims=True)
 
-    def absorb(index, tile_scores, peak, total, summed, tile_peak):
+    ones = jnp.ones((16, blk), bf16)
+
+    def absorb(index, tile_scores, peak, summed, tile_peak):
         new_peak = jnp.maximum(peak, tile_peak)
-        weights = jnp.exp(tile_scores - new_peak)
+        weights = jnp.exp(tile_scores - new_peak).astype(bf16)
         keep = jnp.exp(peak - new_peak)
-        total = total * keep + jnp.sum(weights, axis=0, keepdims=True)
-        summed = summed * keep + dot(v_t[:, columns(index, blk)], weights.astype(bf16), 1, 0)
-        return new_peak, total, summed
+        values = jnp.concatenate([v_t[:, columns(index, blk)], ones], axis=0)
+        return new_peak, summed * keep + dot(values, weights, 1, 0)
 
     def body(pair, carry):
-        peak, total, summed, tile_peak = carry
+        peak, summed, tile_peak = carry
         for slot in range(2):
             next_peak = prepare(2 * pair + slot + 1, 1 - slot)
-            peak, total, summed = absorb(
-                2 * pair + slot, scores[slot], peak, total, summed, tile_peak
-            )
+            peak, summed = absorb(2 * pair + slot, scores[slot], peak, summed, tile_peak)
             tile_peak = next_peak
-        return peak, total, summed, tile_peak
+        return peak, summed, tile_peak
 
     carry = (
         jnp.full((1, tile), -jnp.inf, f32),
-        jnp.zeros((1, tile), f32),
-        jnp.zeros((width, tile), f32),
+        jnp.zeros((width + 16, tile), f32),
         prepare(0, 0),
     )
-    peak, total, summed, _ = lax.fori_loop(0, step, body, carry)
+    peak, summed, _ = lax.fori_loop(0, step, body, carry)
     for half in range(2):
         part = query[:, half * blk :]
         shape = (blk, tile - half * blk)
@@ -143,14 +141,15 @@
         tile_scores = dot(k_n[columns(2 * step + half, blk), :], part, 1, 0)
         tile_scores = jnp.where(query_pos >= key_pos, tile_scores, NEG)
         tile_peak = jnp.max(tile_scores, axis=0, keepdims=True)
-        state = absorb(2 * step + half, tile_scores, peak, total, summed, tile_peak)
+        state = absorb(2 * step + half, tile_scores, peak, summed, tile_peak)
         if half == 0:
             left = tuple(array[:, :blk] for array in state)
-            peak, total, summed = (array[:, blk:] for array in state)
-    peak, total, summed = (
+            peak, summed = (array[:, blk:] for array in state)
+    peak, summed = (
         jnp.concatenate([first, second], axis=1) for first, second in zip(left, state)
     )
-    result = summed / total
+    total = summed[width : width + 1]
+    result = summed[:width] / total
     out_t[...] = result
     log_total[...] = peak + jnp.log(total)
     low = result.astype(bf16)
@@ -248,6 +247,8 @@
     if kind == "first":
         low_query, refs = refs[0], refs[1:]
     refs = refs[after:]
+    if kind == "second":
+        query_slots, refs = refs[0], refs[1:]
     if kind in ("high", "first"):
         query_out, refs = refs[0], refs[1:]
     elif kind == "low":
@@ -348,7 +349,7 @@
         for number in range(tile // wide):
             slot = table[base + tile // wide * step + number]
             part = slice(number * wide, (number + 1) * wide)
-            if cross:
+            if kind == "first":
                 out_slots[slot, width:, :piece] = key_t[:, part]
                 out_slots[slot, width:, piece:] = value_t[:, part]
             else:
@@ -362,7 +363,7 @@
         if kind == "second":
 
             def finish(index, carry):
-                out_slots[table[slots + index], :width] = query_grads(index)
+                query_slots[table[slots + index]] = query_grads(index)
                 return carry
 
             lax.fori_loop(0, slots, finish, 0)
@@ -396,12 +397,15 @@
         in_specs += [whole(array.shape) for array in starts[3:]]
     in_specs += [pl.BlockSpec(memory_space=pl.ANY)] * len(after)
     rows = width if kind == "low" else 2 * width
-    held = (slots, rows, blk)
+    held = (slots, rows, piece if kind == "second" else blk)
     out_specs = [whole(held)]
     out_shape = [jax.ShapeDtypeStruct(held, bf16)]
     if kind in ("high", "first"):
         out_specs = [whole((width, half))] + out_specs
         out_shape = [jax.ShapeDtypeStruct((width, half), f32)] + out_shape
+    elif kind == "second":
+        out_specs = [whole((slots, width, blk))] + out_specs
+        out_shape = [jax.ShapeDtypeStruct((slots, width, blk), bf16)] + out_shape
     elif kind == "low":
         out_specs = [straight, straight] + out_specs
         out_shape = [jax.ShapeDtypeStruct((half, width), f32)] * 2 + out_shape
@@ -431,10 +435,11 @@
     )(table, *queries, k_n, v_t, *starts, *after)
 
 
-def weight_kernel(high_pair, first, second, a1, *refs):
-    out, total, sums = refs[-3:]
-    _, width, blk = second.shape
-    width //= 2
+def weight_kernel(part, high_pair, first, query, second, a1, down, up, *refs):
+    out, down_out, up_out, total, sums = refs[-5:]
+    _, width, blk = query.shape
+    down_out[...] = down[...].astype(f32)
+    up_out[...] = up[...].astype(f32)
     piece = blk // 2
     parts, rows, length = out.shape
     step = pl.program_id(0)
@@ -444,10 +449,10 @@
         total[...] = jnp.zeros_like(total)
         sums[...] = jnp.zeros_like(sums)
 
-    low_key = jnp.concatenate([first[0, width:, :piece], second[0, width:, :piece]], axis=1)
-    low_value = jnp.concatenate([first[0, width:, piece:], second[0, width:, piece:]], axis=1)
+    low_key = jnp.concatenate([first[0, width:, :piece], second[0, :width]], axis=1)
+    low_value = jnp.concatenate([first[0, width:, piece:], second[0, width:]], axis=1)
     low = jnp.concatenate([first[0, :width], low_key, low_value], axis=0)
-    high = jnp.concatenate([second[0, :width], high_pair[0]], axis=0)
+    high = jnp.concatenate([query[0], high_pair[0]], axis=0)
     total[...] += dot(low, a1[:blk], 1, 0) + dot(high, a1[blk:], 1, 0)
     wide = low.astype(f32) + high.astype(f32)
     for at in range(0, blk, 128):
@@ -460,33 +465,42 @@
         tail = jnp.concatenate(tail, axis=0)
         tail = jnp.concatenate([tail, jnp.zeros((3, length - width), f32)], axis=1)
         tail = jnp.concatenate([tail, jnp.zeros((rows - 3 * width - 3, length), f32)], axis=0)
-        for part in range(parts):
-            own = total[:, part * length : (part + 1) * length]
-            out[part] = jnp.concatenate([own, tail], axis=0).astype(bf16)
-
-
-def weight_grad(high_pair, first, second, a1_full, parts, after):
-    slots, width, blk = second.shape
-    width //= 2
+        for number in range(parts):
+            own = total[:, number * length : (number + 1) * length]
+            out[number] = jnp.concatenate([own, tail], axis=0).astype(bf16)
+
+
+def weight_grad(part, high_pair, first, query, second, a1_full, down, up, parts, after):
+    slots, width, blk = query.shape
     tokens, model = a1_full.shape
     rows = 3 * width
     shape = (parts, rows + 16, model // parts)
-    given = (high_pair, first, second)
+    given = (high_pair, first, query, second)
+    own = down.shape[0] // parts
+    strip = own // slots
+    summed = pl.BlockSpec((strip, model), lambda s, t: (t[0] * slots + s, 0))
+    kept = pl.BlockSpec((strip, model), lambda s, t: (s, 0))
     return pl.pallas_call(
         weight_kernel,
-        grid=(slots,),
-        in_specs=[pl.BlockSpec((1,) + array.shape[1:], lambda s: (s, 0, 0)) for array in given]
-        + [pl.BlockSpec((2 * blk, model), lambda s: (s, 0))]
-        + [pl.BlockSpec(memory_space=pl.ANY)] * len(after),
-        out_specs=whole(shape),
-        out_shape=jax.ShapeDtypeStruct(shape, bf16),
-        scratch_shapes=[pltpu.VMEM((rows, model), f32), pltpu.VMEM((rows, 128), f32)],
+        grid_spec=pltpu.PrefetchScalarGridSpec(
+            num_scalar_prefetch=1,
+            grid=(slots,),
+            in_specs=[
+                pl.BlockSpec((1,) + array.shape[1:], lambda s, t: (s, 0, 0)) for array in given
+            ]
+            + [pl.BlockSpec((2 * blk, model), lambda s, t: (s, 0)), summed, summed]
+            + [pl.BlockSpec(memory_space=pl.ANY)] * len(after),
+            out_specs=[whole(shape), kept, kept],
+            scratch_shapes=[pltpu.VMEM((rows, model), f32), pltpu.VMEM((rows, 128), f32)],
+        ),
+        out_shape=[jax.ShapeDtypeStruct(shape, bf16)]
+        + [jax.ShapeDtypeStruct((own, model), f32)] * 2,
         compiler_params=pltpu.CompilerParams(vmem_limit_bytes=48 * MIB),
         cost_estimate=pl.CostEstimate(
             flops=2 * rows * tokens * model, bytes_accessed=2 * tokens * model, transcendentals=0
         ),
         name="weight_grad",
-    )(*given, a1_full, *after)
+    )(part.reshape(1), *given, a1_full, down, up, *after)
 
 
 def mlp_forward_kernel(normed, up, up_bias, down, hidden, slope, total):
@@ -727,8 +741,6 @@
     grad_downward, grad_upward, grad_proj = summed
     early = grad_proj[model:].astype(f32).reshape(-1)
     grad_proj = grad_proj[:model]
-    grad_downward = own_rows(grad_downward).astype(f32)
-    grad_upward = own_rows(grad_upward).astype(f32)
     grad_proj = own_rows(grad_proj).astype(f32)
     hidden_width = up_full.shape[0]
     grad_upbias = own_rows(early[:hidden_width])
@@ -753,17 +765,31 @@
     query_sum, first = backward("first", owner, high, k_n, v_t, starts, (high_tokens,), blk)
     first_tokens = token_grads(first)
     starts = (query_sum, key_sum, value_sum)
-    (second,) = backward("second", owner, high, k_n, v_t, starts, (), blk)
-    second_tokens = token_grads(second)
+    query, second = backward("second", owner, high, k_n, v_t, starts, (), blk)
+    query, first_tokens = lax.optimization_barrier((query, first_tokens))
+    query_tokens = token_grads(query)
 
     def own_columns(array):
         length = array.shape[1] // weight_parts
         return lax.dynamic_slice_in_dim(array, part * length, length, 1)
 
-    after = (first_tokens,) + tuple(summed)
-    columns_grad = weight_grad(high_pair, first, second, a1_full, weight_parts, after)
+    columns_grad, grad_downward, grad_upward = weight_grad(
+        part.astype(jnp.int32),
+        high_pair,
+        first,
+        query,
+        second,
+        a1_full,
+        grad_downward,
+        grad_upward,
+        weight_parts,
+        (first_tokens,),
+    )
+    columns_grad, query_tokens = lax.optimization_barrier((columns_grad, query_tokens))
     columns_grad = lax.all_to_all(columns_grad, "wt", 0, 0, tiled=True)
     columns_grad = jnp.sum(columns_grad.astype(f32), axis=0).astype(bf16)
+    columns_grad, second = lax.optimization_barrier((columns_grad, second))
+    second_tokens = token_grads(second)
     all_columns = lax.all_gather(columns_grad, "h", axis=0)
     grad_qkv = place(all_columns, width)
     sums = all_columns[:, 3 * width : 3 * width + 3, :width].astype(f32)
@@ -776,18 +802,15 @@
     first_norm = own_columns(jnp.stack([gains[0], shifts[0]]))
     gain_zero = (gain_zero - first_norm[1] * shift_zero) / first_norm[0]
 
-    second_tokens, grad_downward, grad_upward, grad_proj = lax.optimization_barrier(
-        (second_tokens, grad_downward, grad_upward, grad_proj)
-    )
     piece = blk // 2
-    low_key = [first_tokens[model:, :piece], second_tokens[model:, :piece]]
-    low_value = [first_tokens[model:, piece:], second_tokens[model:, piece:]]
+    low_key = [first_tokens[model:, :piece], second_tokens[:model]]
+    low_value = [first_tokens[model:, piece:], second_tokens[model:]]
     low_rows = [
         first_tokens[:model],
         jnp.concatenate(low_key, axis=1),
         jnp.concatenate(low_value, axis=1),
     ]
-    high_rows = [second_tokens[:model], high_tokens]
+    high_rows = [query_tokens, high_tokens]
     grads_t = jnp.concatenate(
         [jnp.concatenate(low_rows, axis=0), jnp.concatenate(high_rows, axis=0)], axis=1
     )

time: 1200 us -> 1150 us (0.958)
  waiting for transfers between devices: 249 us -> 208 us
    all_to_all x3 -> x4, waiting for transfers between devices: 67.1 us -> 26.3 us  [token_grads(): own = lax.all_to_all(own, 'h', 0, 0, tiled=True)]
    all_to_all x3 -> x4, starting transfers between devices: 19.3 us -> 25.6 us  [token_grads(): own = lax.all_to_all(own, 'h', 0, 0, tiled=True)]
    unnamed x148 -> x146, local copies, waits for them, and re-layouts: 33.9 us -> 32.1 us
  transfers between devices with their start and end apart: 14 -> 15, of which waited for: 3 -> 3; matrix products, arithmetic and copies ran while one was open for 6% -> 5% of each run, Pallas kernels for 55% -> 58%
where the time goes in v3:
time: 1150 us; the launch traced here: 1140 us
  Pallas kernels  715 us (62%)
  waiting for transfers between devices  208 us (18%)
  other arithmetic  52.9 us (5%)
  starting transfers between devices  48.8 us (4%)
  local copies, waits for them, and re-layouts  47.1 us (4%)
  matrix products  29.8 us (3%)
  blocking collectives  19 us (2%)
  between operations  15.6 us (1%)
    pallas_call x4, Pallas kernels, backward(): pl.pallas_call(functools.partial(backward_kernel, kind, 2 * skip, len(aft...  397 us
    pallas_call x2, Pallas kernels, forward(): pl.pallas_call(functools.partial(forward_kernel, base), grid_spec=pltpu.P...  176 us
    all_gather x1, waiting for transfers between devices, local(): a1_full = lax.all_gather(a1, ctx, axis=0, tiled=True)  156 us
    pallas_call x3, Pallas kernels, mlp_call(): pl.pallas_call(kernel, grid=(hidden // chunk,), in_specs=[specs[kind] for...  78.4 us
    unnamed x146, local copies, waits for them, and re-layouts  32.1 us
    dot_general x4, matrix products, dot(): lax.dot_general(a, b, (((ca,), (cb,)), ((), ())), preferred_element_type=...  29.8 us
    pallas_call x1, Pallas kernels, weight_grad(): pl.pallas_call(weight_kernel, grid_spec=pltpu.PrefetchScalarGridSpec(num_...  26.9 us
    all_to_all x4, waiting for transfers between devices, token_grads(): own = lax.all_to_all(own, 'h', 0, 0, tiled=True)  26.3 us
  transfers between devices with their start and end apart: 15, of which 3 were waited for; matrix products, arithmetic and copies ran while one was open for 5% of the time, Pallas kernels for 58%

profile of v3, /device:TPU:13, one launch (start us, length us, event | category | flops | bytes accessed | tf_op | source)
XLA Modules:
  0.0 1136.5 jit_solution(16336736726316703832)
XLA Ops:
  30.6 6.8 all_gather.33
  38.0 156.2 %all-gather.9.cloned.1.call-done.refs_0_.refs_1_.refs_2_.refs_3_.a1 = bf16[16384,1024]{1,0:T(8,128)(2,1)} async-done(((bf16[1024,1024]{1,0:T(8,128)(2,1)}), bf16[16384,1024]{1,0:T(8,128)(2,1)}) %all-gather.9.cloned.1.call-update) | async-done | bytes 33554448 | tf_op jit(solution)/shard_map/all_gather | solution.py:628
  194.2 18.6 %project.1 = (bf16[64,16384]{1,0:T(8,128)(2,1)S(1)}, bf16[16384,64]{1,0:T(8,128)(2,1)}, bf16[64,16384]{1,0:T(8,128)(2,1)S(1)}) custom-call(s32[32]{0:T(128)S(1)} %get-tuple-element.134.table, bf16[16384,1024]{1,0:T(8,128)(2,1)} %all-gather.9.cloned.1.call-done.refs_0_.refs_1_.refs_2_.refs_3_.a1, ...), custom_call_target="tpu_custom_call" | custom-call | flops 8589934592 | bytes 33554432 | tf_op jit(solution)/shard_map/project/pallas_call | solution.py:77
  215.4 125.7 %forward_high.1 = (f32[64,8192]{1,0:T(8,128)}, f32[1,8192]{1,0:T(1,128)}, bf16[16,64,512]{2,1,0:T(8,128)(2,1)}) custom-call(s32[32]{0:T(128)} %get-tuple-element.135.table.refs_0_, bf16[64,16384]{1,0:T(8,128)(2,1)} %copy-done, bf16[16384,64]{1,0:T(8,128)(2,1)} %get-tuple-element.60.k_n.refs_7_, bf16[64,16384]{1,0:T(8,128)(2,1)} %copy-done.8), custom_call_target="tpu_custom_call" | custom-call | flops 103079215104 | bytes 12582912 | tf_op jit(solution)/shard_map/forward_high/pallas_call | solution.py:167
  341.1 5.4 all-to-all-start.1
  346.6 50.5 %forward_low.1 = (f32[64,8192]{1,0:T(8,128)}, f32[1,8192]{1,0:T(1,128)}, bf16[16,64,512]{2,1,0:T(8,128)(2,1)}) custom-call(s32[32]{0:T(128)} %get-tuple-element.135.table.refs_0_, bf16[64,16384]{1,0:T(8,128)(2,1)} %copy-done, bf16[16384,64]{1,0:T(8,128)(2,1)} %get-tuple-element.60.k_n.refs_7_, bf16[64,16384]{1,0:T(8,128)(2,1)} %copy-done.8), custom_call_target="tpu_custom_call" | custom-call | flops 34359738368 | bytes 12582912 | tf_op jit(solution)/shard_map/forward_low/pallas_call | solution.py:167
  397.1 6.4 all-to-all-start
  405.4 23.3 %all-to-all-done = bf16[16,64,512]{2,1,0:T(8,128)(2,1)} async-done(((bf16[16,64,512]{2,1,0:T(8,128)(2,1)}), bf16[16,64,512]{2,1,0:T(8,128)(2,1)}, u32[]{:S(2)}, u32[]{:S(2)}) %all-to-all-start) | async-done | bytes 1048608 | tf_op jit(solution)/shard_map/all_to_all | solution.py:656
  428.6 4.4 add_reduce_fusion.1
  442.0 30.5 %mlp_forward.1 = (bf16[1024,4096]{1,0:T(8,128)(2,1)}, bf16[1024,4096]{1,0:T(8,128)(2,1)}, f32[1024,1024]{1,0:T(8,128)}) custom-call(bf16[1024,1024]{1,0:T(8,128)(2,1)} %add_convert_fusion.3.normed, bf16[4096,1024]{1,0:T(8,128)(2,1)} %all-gather.13.cloned.1.call-done.up, f32[1,4096]{1,0:T(1,128)} %bitcast.193, ...), custom_call_target="tpu_custom_call" | custom-call | flops 17179869184 | bytes 33554432 | tf_op jit(solution)/shard_map/mlp_forward/pallas_call | solution.py:548
  478.9 3.9 fusion.49
  484.5 24.8 %mlp_backward.1 = (bf16[1024,4096]{1,0:T(8,128)(2,1)}, f32[1,4096]{1,0:T(1,128)}, f32[1024,1024]{1,0:T(8,128)}) custom-call(bf16[1024,1024]{1,0:T(8,128)(2,1)} %get-tuple-element.124.grad, bf16[4096,1024]{1,0:T(8,128)(2,1)} %all-gather.15.cloned.1.call-done.down, bf16[1024,4096]{1,0:T(8,128)(2,1)} %get-tuple-element.65.slope, ...), custom_call_target="tpu_custom_call" | custom-call | flops 17179869184 | bytes 33554432 | tf_op jit(solution)/shard_map/mlp_backward/pallas_call | solution.py:548
  520.7 3.7 convolution_convert_fusion
  528.4 4.8 all-to-all-start.2
  535.0 23.0 %mlp_grads.1 = (bf16[4096,1024]{1,0:T(8,128)(2,1)}, bf16[4096,1024]{1,0:T(8,128)(2,1)}) custom-call(bf16[1024,4096]{1,0:T(8,128)(2,1)} %get-tuple-element.67.hidden, bf16[1024,1024]{1,0:T(8,128)(2,1)} %get-tuple-element.124.grad, bf16[1024,4096]{1,0:T(8,128)(2,1)} %get-tuple-element.68.grad_pre, bf16[1024,1024]{1,0:T(8,128)(2,1)} %add_convert_fusion.3.normed), custom_call_target="tpu_custom_call" | custom-call | flops 17179869184 | bytes 33554432 | tf_op jit(solution)/shard_map/mlp_grads/pallas_call | solution.py:548
  558.1 6.1 all-to-all-start.3
  574.6 103.9 %backward_high.1 = (f32[64,8192]{1,0:T(8,128)}, bf16[16,128,512]{2,1,0:T(8,128)(2,1)}) custom-call(s32[32]{0:T(128)} %get-tuple-element.135.table.refs_0_, bf16[64,8192]{1,0:T(8,128)(2,1)} %get-tuple-element.142.refs_1_, bf16[8192,64]{1,0:T(8,128)(2,1)} %copy-done.10, bf16[64,8192]{1,0:T(8,128)(2,1)} %copy-done.13, bf16[8192,64]{1,0:T(8,128)(2,1)} %copy-done.9, ...), custom_call_target="tpu_custom_call" | custom-call | flops 17179869184 | bytes 16777216 | tf_op jit(solution)/shard_map/backward_high/pallas_call | solution.py:412
  678.5 6.1 all-to-all-start.4
  687.0 8.8 delta_low.1
  700.2 102.3 %backward_low.1 = (f32[8192,64]{1,0:T(8,128)}, f32[8192,64]{1,0:T(8,128)}, bf16[16,64,512]{2,1,0:T(8,128)(2,1)}) custom-call(s32[32]{0:T(128)} %get-tuple-element.135.table.refs_0_, bf16[64,8192]{1,0:T(8,128)(2,1)} %get-tuple-element.141.refs_1_, bf16[8192,64]{1,0:T(8,128)(2,1)} %copy-done.12, bf16[64,8192]{1,0:T(8,128)(2,1)} %copy-done.14, ...), custom_call_target="tpu_custom_call" | custom-call | flops 17179869184 | bytes 16777216 | tf_op jit(solution)/shard_map/backward_low/pallas_call | solution.py:412
  805.7 96.1 %backward_first.1 = (f32[64,8192]{1,0:T(8,128)}, bf16[16,128,512]{2,1,0:T(8,128)(2,1)}) custom-call(s32[32]{0:T(128)} %get-tuple-element.135.table.refs_0_, bf16[64,8192]{1,0:T(8,128)(2,1)} %get-tuple-element.142.refs_1_, bf16[8192,64]{1,0:T(8,128)(2,1)} %copy-done.10, bf16[64,8192]{1,0:T(8,128)(2,1)} %copy-done.13, bf16[8192,64]{1,0:T(8,128)(2,1)} %copy-done.9, ...), custom_call_target="tpu_custom_call" | custom-call | flops 17179869184 | bytes 16777216 | tf_op jit(solution)/shard_map/backward_first/pallas_call | solution.py:412
  901.8 6.0 all-to-all-start.5
  907.8 95.1 %backward_second.1 = (bf16[16,64,512]{2,1,0:T(8,128)(2,1)}, bf16[16,128,256]{2,1,0:T(8,128)(2,1)}) custom-call(s32[32]{0:T(128)} %get-tuple-element.135.table.refs_0_, bf16[64,8192]{1,0:T(8,128)(2,1)} %get-tuple-element.142.refs_1_, bf16[8192,64]{1,0:T(8,128)(2,1)} %copy-done.10, bf16[64,8192]{1,0:T(8,128)(2,1)} %copy-done.13, bf16[8192,64]{1,0:T(8,128)(2,1)} %copy-done.9, ...), custom_call_target="tpu_custom_call" | custom-call | flops 17179869184 | bytes 16777216 | tf_op jit(solution)/shard_map/backward_second/pallas_call | solution.py:412
  1006.2 6.0 all-to-all-start.6
  1012.3 26.9 %weight_grad.1 = (bf16[2,208,512]{2,1,0:T(8,128)(2,1)S(1)}, f32[2048,1024]{1,0:T(8,128)}, f32[2048,1024]{1,0:T(8,128)}) custom-call(s32[1]{0:T(128)} %bitcast.27.part, bf16[16,128,512]{2,1,0:T(8,128)(2,1)S(1)} %copy-done.2, bf16[16,128,512]{2,1,0:T(8,128)(2,1)} %get-tuple-element.92.first, bf16[16,64,512]{2,1,0:T(8,128)(2,1)} %get-tuple-element.94.query, ...), custom_call_target="tpu_custom_call" | custom-call | flops 6442450944 | bytes 33554432 | tf_op jit(solution)/shard_map/weight_grad/pallas_call | solution.py:483
  1039.2 8.9 all_to_all.45
  1049.0 7.5 all-to-all-start.8
  1061.8 26.3 %all-to-all-done.8 = bf16[16,128,256]{2,1,0:T(8,128)(2,1)S(1)} async-done(((bf16[16,128,256]{2,1,0:T(8,128)(2,1)}), bf16[16,128,256]{2,1,0:T(8,128)(2,1)S(1)}, u32[]{:S(2)}, u32[]{:S(2)}) %all-to-all-start.8) | async-done | bytes 1048608 | tf_op jit(solution)/shard_map/all_to_all | solution.py:753
  1088.4 19.3 %fusion.29 = (f32[1024]{0:T(1024)S(1)}, f32[1024,1024]{1,0:T(8,128)}) fusion(bf16[1,1024,1024]{2,1,0:T(8,128)(2,1)S(1)} %copy-done.21, f32[1024]{0:T(1024)S(1)} %bitcast.178, f32[1024]{0:T(1024)S(1)} %copy-done.37, bf16[1024,3072]{1,0:T(8,128)(2,1)} %all-gather.17.cloned.1.call-done, bf16[2048,512]{1,0:T(8,128)(2,1)} %bitcast.156, ...), kind=kOutput, calls=%fused_computation.40 | convolution fusion | flops 6491732992 | bytes 18886656 | tf_op jit(solution)/shard_map/dot_general | solution.py:43
  1111.2 4.5 add_bitcast_fusion
  1117.7 5.8 place.1
  1123.8 4.2 fusion.1
  (259 shorter events, 99.2 us)
Async XLA Ops:
  7.2 187.0 %all-gather.9.cloned.1.call-start = ((), (), s32[]{:S(2)}) async-start(), calls=%async_computation.9 | async-start | bytes 35651584 | tf_op jit(solution)/shard_map/all_gather | solution.py:628
  23.6 381.7 %all-gather.11.cloned.1.call-start = ((), (), s32[]{:S(2)}) async-start(), calls=%async_computation.10 | async-start | bytes 3145728 | tf_op jit(solution)/shard_map/all_gather | solution.py:666
  24.4 417.6 %all-gather.13.cloned.1.call-start = ((), (), s32[]{:S(2)}) async-start(), calls=%async_computation.11 | async-start | bytes 12582912 | tf_op jit(solution)/shard_map/all_gather | solution.py:667
  25.1 416.9 %all-gather.15.cloned.1.call-start = ((), (), s32[]{:S(2)}) async-start(), calls=%async_computation.12 | async-start | bytes 12582912 | tf_op jit(solution)/shard_map/all_gather | solution.py:668
  341.1 56.0 %all-to-all-start.1 = ((bf16[16,64,512]{2,1,0:T(8,128)(2,1)}), bf16[16,64,512]{2,1,0:T(8,128)(2,1)S(1)}, u32[]{:S(2)}, u32[]{:S(2)}) async-start(bf16[16,64,512]{2,1,0:T(8,128)(2,1)} %get-tuple-element.63), calls=%async_computation.1 | async-start | bytes 2097152 | tf_op jit(solution)/shard_map/all_to_all | solution.py:656
  346.5 57.0 %copy-start.51 = (f32[1,4,2,128]{3,2,1,0:T(2,128)S(1)}, f32[1,4,2,128]{3,2,1,0:T(2,128)}, u32[]{:S(2)}) copy-start(f32[1,4,2,128]{3,2,1,0:T(2,128)} %get-tuple-element.160) | copy-start | bytes 12292
  346.5 57.0 %copy-start.52 = (f32[1,4,2,128]{3,2,1,0:T(2,128)S(1)}, f32[1,4,2,128]{3,2,1,0:T(2,128)}, u32[]{:S(2)}) copy-start(f32[1,4,2,128]{3,2,1,0:T(2,128)} %get-tuple-element.165) | copy-start | bytes 12292
  346.5 57.8 %copy-start.48 = (f32[1,4,2,128]{3,2,1,0:T(2,128)S(1)}, f32[1,4,2,128]{3,2,1,0:T(2,128)}, u32[]{:S(2)}) copy-start(f32[1,4,2,128]{3,2,1,0:T(2,128)} %get-tuple-element.159) | copy-start | bytes 12292
  346.5 57.8 %copy-start.50 = (f32[1,4,2,128]{3,2,1,0:T(2,128)S(1)}, f32[1,4,2,128]{3,2,1,0:T(2,128)}, u32[]{:S(2)}) copy-start(f32[1,4,2,128]{3,2,1,0:T(2,128)} %get-tuple-element.164) | copy-start | bytes 12292
  346.5 57.8 %copy-start.38 = (f32[1,1,2,2048]{3,2,1,0:T(2,128)S(1)}, f32[1,1,2,2048]{3,2,1,0:T(2,128)}, u32[]{:S(2)}) copy-start(f32[1,1,2,2048]{3,2,1,0:T(2,128)} %get-tuple-element.154) | copy-start | bytes 49156
  346.5 58.4 %copy-start.49 = (f32[1,4,2,128]{3,2,1,0:T(2,128)S(1)}, f32[1,4,2,128]{3,2,1,0:T(2,128)}, u32[]{:S(2)}) copy-start(f32[1,4,2,128]{3,2,1,0:T(2,128)} %get-tuple-element.163) | copy-start | bytes 12292
  346.5 58.4 %copy-start.47 = (f32[1,4,2,128]{3,2,1,0:T(2,128)S(1)}, f32[1,4,2,128]{3,2,1,0:T(2,128)}, u32[]{:S(2)}) copy-start(f32[1,4,2,128]{3,2,1,0:T(2,128)} %get-tuple-element.158) | copy-start | bytes 12292
  346.6 58.4 %copy-start.27 = (bf16[1,1024,1024]{2,1,0:T(8,128)(2,1)S(1)}, bf16[1,1024,1024]{2,1,0:T(8,128)(2,1)}, u32[]{:S(2)}) copy-start(bf16[1,1024,1024]{2,1,0:T(8,128)(2,1)} %param.25) | copy-start | bytes 6291460
  397.1 36.0 %copy-start.33 = (bf16[16,64,512]{2,1,0:T(8,128)(2,1)}, bf16[16,64,512]{2,1,0:T(8,128)(2,1)S(1)}, u32[]{:S(2)}) copy-start(bf16[16,64,512]{2,1,0:T(8,128)(2,1)S(1)} %all-to-all-done.1) | copy-start | bytes 3145732
  397.1 31.5 %all-to-all-start = ((bf16[16,64,512]{2,1,0:T(8,128)(2,1)}), bf16[16,64,512]{2,1,0:T(8,128)(2,1)}, u32[]{:S(2)}, u32[]{:S(2)}) async-start(bf16[16,64,512]{2,1,0:T(8,128)(2,1)} %get-tuple-element.62), calls=%async_computation | async-start | bytes 2097152 | tf_op jit(solution)/shard_map/all_to_all | solution.py:656
  528.4 29.7 %all-to-all-start.2 = ((bf16[16,64,512]{2,1,0:T(8,128)(2,1)}), bf16[16,64,512]{2,1,0:T(8,128)(2,1)S(1)}, u32[]{:S(2)}, u32[]{:S(2)}) async-start(bf16[16,64,512]{2,1,0:T(8,128)(2,1)} %bitcast.16), calls=%async_computation.2 | async-start | bytes 2097152 | tf_op jit(solution)/shard_map/all_to_all | solution.py:659
  533.2 479.1 %all-reduce.3.cloned.1.call-start = ((), (), s32[]{:S(2)}) async-start(), calls=%async_computation.15 | async-start | bytes 37814272 | tf_op jit(solution)/shard_map/psum | solution.py:740
  558.1 120.4 %all-to-all-start.3 = ((bf16[16,64,512]{2,1,0:T(8,128)(2,1)}), bf16[16,64,512]{2,1,0:T(8,128)(2,1)}, u32[]{:S(2)}, u32[]{:S(2)}) async-start(bf16[16,64,512]{2,1,0:T(8,128)(2,1)} %bitcast.153), calls=%async_computation.3 | async-start | bytes 2097152 | tf_op jit(solution)/shard_map/all_to_all | solution.py:659
  678.5 124.0 %all-to-all-start.4 = ((bf16[16,128,512]{2,1,0:T(8,128)(2,1)}), bf16[16,128,512]{2,1,0:T(8,128)(2,1)}, u32[]{:S(2)}, u32[]{:S(2)}) async-start(bf16[16,128,512]{2,1,0:T(8,128)(2,1)} %get-tuple-element.89.high_pair), calls=%async_computation.4 | async-start | bytes 4194304 | tf_op jit(solution)/shard_map/all_to_all | solution.py:753
  684.5 403.8 %all-gather.17.cloned.1.call-start = ((), (), s32[]{:S(2)}) async-start(), calls=%async_computation.13 | async-start | bytes 9437184 | tf_op jit(solution)/shard_map/all_gather | solution.py:669
  901.8 101.1 %all-to-all-start.5 = ((bf16[16,128,512]{2,1,0:T(8,128)(2,1)}), bf16[16,128,512]{2,1,0:T(8,128)(2,1)}, u32[]{:S(2)}, u32[]{:S(2)}) async-start(bf16[16,128,512]{2,1,0:T(8,128)(2,1)} %get-tuple-element.92.first), calls=%async_computation.5 | async-start | bytes 4194304 | tf_op jit(solution)/shard_map/all_to_all | solution.py:753
  1006.2 33.1 %all-to-all-start.6 = ((bf16[16,64,512]{2,1,0:T(8,128)(2,1)}), bf16[16,64,512]{2,1,0:T(8,128)(2,1)}, u32[]{:S(2)}, u32[]{:S(2)}) async-start(bf16[16,64,512]{2,1,0:T(8,128)(2,1)} %get-tuple-element.94.query), calls=%async_computation.6 | async-start | bytes 2097152 | tf_op jit(solution)/shard_map/all_to_all | solution.py:753
  1012.2 103.6 %all-gather.19.cloned.1.call-start = ((), (), s32[]{:S(2)}) async-start(), calls=%async_computation.14 | async-start | bytes 3620864 | tf_op jit(solution)/shard_map/all_gather | solution.py:793
  1012.3 44.2 %copy-start.46 = (f32[1,1,2,512]{3,2,1,0:T(2,128)S(1)}, f32[1,1,2,512]{3,2,1,0:T(2,128)}, u32[]{:S(2)}) copy-start(f32[1,1,2,512]{3,2,1,0:T(2,128)} %get-tuple-element.162) | copy-start | bytes 12292
  1012.3 44.2 %copy-start.45 = (f32[1,1,2,512]{3,2,1,0:T(2,128)S(1)}, f32[1,1,2,512]{3,2,1,0:T(2,128)}, u32[]{:S(2)}) copy-start(f32[1,1,2,512]{3,2,1,0:T(2,128)} %get-tuple-element.157) | copy-start | bytes 12292
  1039.2 17.4 %copy-start.30 = (bf16[16,2,64,512]{3,2,0,1:T(8,128)(2,1)S(1)}, bf16[16,2,64,512]{3,2,0,1:T(8,128)(2,1)}, u32[]{:S(2)}) copy-start(bf16[16,2,64,512]{3,2,0,1:T(8,128)(2,1)} %copy.59) | copy-start | bytes 6291460
  1049.0 39.1 %all-to-all-start.8 = ((bf16[16,128,256]{2,1,0:T(8,128)(2,1)}), bf16[16,128,256]{2,1,0:T(8,128)(2,1)S(1)}, u32[]{:S(2)}, u32[]{:S(2)}) async-start(bf16[16,128,256]{2,1,0:T(8,128)(2,1)} %get-tuple-element.100.second), calls=%async_computation.8 | async-start | bytes 2097152 | tf_op jit(solution)/shard_map/all_to_all | solution.py:753
  1058.9 29.5 %copy-start.21 = (bf16[1,1024,1024]{2,1,0:T(8,128)(2,1)S(1)}, bf16[1,1024,1024]{2,1,0:T(8,128)(2,1)}, u32[]{:S(2)}) copy-start(bf16[1,1024,1024]{2,1,0:T(8,128)(2,1)} %param.13) | copy-start | bytes 6291460
  1058.9 29.4 %copy-start.37 = (f32[1024]{0:T(1024)S(1)}, f32[1024]{0:T(1024)}, u32[]{:S(2)}) copy-start(f32[1024]{0:T(1024)} %copy-done.36) | copy-start | bytes 12292
  1058.9 29.4 %copy-start.40 = (f32[1,4,2,128]{3,1,2,0:T(4,128)S(1)}, f32[1,4,2,128]{3,1,2,0:T(4,128)}, u32[]{:S(2)}) copy-start(f32[1,4,2,128]{3,1,2,0:T(4,128)} %copy-done.39) | copy-start | bytes 12292
  1088.3 19.3 %copy-start.44 = (f32[1024]{0:T(1024)S(1)}, f32[1024]{0:T(1024)}, u32[]{:S(2)}) copy-start(f32[1024]{0:T(1024)} %copy-done.43) | copy-start | bytes 12292
  1088.3 19.4 %copy-start.42 = (f32[1024]{0:T(1024)S(1)}, f32[1024]{0:T(1024)}, u32[]{:S(2)}) copy-start(f32[1024]{0:T(1024)} %copy-done.41) | copy-start | bytes 12292
  (39 other events, 138.3 us)
Sparse Core Ops, SparseCore 0:
  23.7 170.4 all-gather.8
  195.7 33.0 all-gather.10
  230.3 103.9 all-gather.12
  335.8 103.9 all-gather.14
  558.2 380.2 all-reduce.2
  939.9 89.6 all-gather.16
  1049.1 57.8 all-gather.18

commit v4 on v3

--- a/solution.py
+++ b/solution.py
@@ -23,11 +23,6 @@
     centered = values - average
     variance = jnp.mean(centered * centered, axis=-1, keepdims=True)
     return centered * lax.rsqrt(variance + EPS) * norm_gain + norm_shift
-
-
-def norm_backward(values, norm_gain, norm_shift, upstream):
-    _, pullback = jax.vjp(layer_norm, values, norm_gain, norm_shift)
-    return pullback(upstream)
 
 
 def gelu_and_slope(values):
@@ -503,8 +498,39 @@
     )(part.reshape(1), *given, a1_full, down, up, *after)
 
 
-def mlp_forward_kernel(normed, up, up_bias, down, hidden, slope, total):
-    @pl.when(pl.program_id(0) == 0)
+def normalize(values):
+    centered = values - jnp.mean(values, axis=-1, keepdims=True)
+    factor = lax.rsqrt(jnp.mean(centered * centered, axis=-1, keepdims=True) + EPS)
+    return centered * factor, factor
+
+
+def normalize_backward(normal, factor, gain, upstream):
+    scaled = upstream * gain
+    along = jnp.mean(scaled * normal, axis=-1, keepdims=True)
+    return factor * (scaled - jnp.mean(scaled, axis=-1, keepdims=True) - normal * along)
+
+
+def over_rows(rows, body, count, width):
+    strip = 128
+
+    def one(index, sums):
+        return body(pl.ds(pl.multiple_of(index * strip, strip), strip), sums)
+
+    zero = tuple(jnp.zeros((1, width), f32) for _ in range(count))
+    return lax.fori_loop(0, rows // strip, one, zero)
+
+
+def column_sum(values):
+    return jnp.sum(values, axis=0, keepdims=True)
+
+
+def mlp_forward_kernel(
+    normed, up, up_bias, down, down_bias, residual, upstream, gain, shift,
+    hidden, slope, layer_output, grad_branch, sums, total,
+):
+    step = pl.program_id(0)
+
+    @pl.when(step == 0)
     def _():
         total[...] = jnp.zeros_like(total)
 
@@ -514,16 +540,55 @@
     slope[...] = bend.astype(bf16)
     total[...] += dot(low, down[...], 1, 0)
 
-
-def mlp_backward_kernel(grad, down, slope, up, grad_pre, sums, total):
-    @pl.when(pl.program_id(0) == 0)
+    @pl.when(step == pl.num_programs(0) - 1)
+    def _():
+        def strip(at, carry):
+            normal, factor = normalize(total[at, :] + down_bias[...])
+            output = residual[at, :] + normal * gain[...] + shift[...]
+            layer_output[at, :] = output.astype(bf16)
+            given = upstream[at, :].astype(f32)
+            grad = normalize_backward(normal, factor, gain[...], given).astype(bf16)
+            grad_branch[at, :] = grad
+            new = (given * normal, given, grad.astype(f32))
+            return tuple(old + column_sum(part) for old, part in zip(carry, new))
+
+        result = over_rows(*[total.shape[0], strip, 3, total.shape[1]])
+        for number in range(3):
+            sums[number : number + 1] = result[number]
+
+
+def mlp_backward_kernel(
+    grad, down, slope, up, residual, proj_pre, upstream, gain_one, gain_two,
+    grad_pre, up_sums, grad_residual, grad_proj_pre, sums, total,
+):
+    step = pl.program_id(0)
+
+    @pl.when(step == 0)
     def _():
         total[...] = jnp.zeros_like(total)
 
     low = (dot(grad[...], down[...], 1, 1) * slope[...].astype(f32)).astype(bf16)
     grad_pre[...] = low
-    sums[...] = jnp.sum(low.astype(f32), axis=0, keepdims=True)
+    up_sums[...] = column_sum(low.astype(f32))
     total[...] += dot(low, up[...], 1, 0)
+
+    @pl.when(step == pl.num_programs(0) - 1)
+    def _():
+        def strip(at, carry):
+            grad_mid = total[at, :]
+            normal_two, factor = normalize(residual[at, :])
+            back = normalize_backward(normal_two, factor, gain_two[...], grad_mid)
+            back = upstream[at, :].astype(f32) + back
+            grad_residual[at, :] = back
+            normal_one, factor = normalize(proj_pre[at, :])
+            low = normalize_backward(normal_one, factor, gain_one[...], back).astype(bf16)
+            grad_proj_pre[at, :] = low
+            new = (back * normal_one, back, grad_mid * normal_two, grad_mid, low.astype(f32))
+            return tuple(old + column_sum(part) for old, part in zip(carry, new))
+
+        result = over_rows(*[total.shape[0], strip, 5, total.shape[1]])
+        for number in range(5):
+            sums[number : number + 1] = result[number]
 
 
 def mlp_grads_kernel(hidden, grad, grad_pre, normed, down_out, up_out):
@@ -531,19 +596,22 @@
     up_out[...] = dot(grad_pre[...], normed[...], 0, 0).astype(bf16)
 
 
-def mlp_call(kernel, name, operands, kinds, results, result_kinds, rows, model, hidden):
+def mlp_call(kernel, name, operands, kinds, results, result_kinds, rows, model, hidden, kept):
     chunk = 512
     specs = {
         "rows": whole((rows, model)),
         "wide": pl.BlockSpec((rows, chunk), lambda j: (0, j)),
         "tall": pl.BlockSpec((chunk, model), lambda j: (j, 0)),
         "line": pl.BlockSpec((1, chunk), lambda j: (0, j)),
+        "row": whole((1, model)),
+        "sums": whole((8, model)),
     }
     shapes = {
         "rows": (rows, model),
         "wide": (rows, hidden),
         "tall": (hidden, model),
         "line": (1, hidden),
+        "sums": (8, model),
     }
     return pl.pallas_call(
         kernel,
@@ -553,12 +621,79 @@
         out_shape=[
             jax.ShapeDtypeStruct(shapes[kind], dtype) for kind, dtype in zip(result_kinds, results)
         ],
+        scratch_shapes=[pltpu.VMEM((rows, model), f32)] if kept else [],
         compiler_params=pltpu.CompilerParams(vmem_limit_bytes=56 * MIB),
         cost_estimate=pl.CostEstimate(
             flops=4 * rows * model * hidden, bytes_accessed=8 * rows * hidden, transcendentals=0
         ),
         name=name,
     )(*operands)
+
+
+def input_kernel(
+    first, second, query, high, weight_q, weight_k, weight_v, inputs, grad_residual, gain,
+    out, total,
+):
+    step = pl.program_id(0)
+    heads, _, blk = first.shape
+    width = query.shape[1]
+    piece = blk // 2
+    rows = heads * width
+
+    def part(array, start):
+        return array[:, start : start + width].reshape(rows, array.shape[2])
+
+    @pl.when(step == 0)
+    def _():
+        total[...] = jnp.zeros_like(total)
+
+    weight = jnp.concatenate([weight_q[...], weight_k[...], weight_v[...]], axis=1)
+    pair = part(first, width)
+    key = jnp.concatenate([pair[:, :piece], part(second, 0)], axis=1)
+    value = jnp.concatenate([pair[:, piece:], part(second, width)], axis=1)
+    low = jnp.concatenate([part(first, 0), key, value], axis=0)
+    top = jnp.concatenate([part(query, 0), part(high, 0), part(high, width)], axis=0)
+    total[:, :blk] += dot(weight, low, 1, 0)
+    total[:, blk:] += dot(weight, top, 1, 0)
+
+    @pl.when(step == pl.num_programs(0) - 1)
+    def _():
+        def strip(index, carry):
+            at = columns(index, 128)
+            grad = jnp.transpose(total[:, at])
+            normal, factor = normalize(inputs[at, :].astype(f32))
+            back = normalize_backward(normal, factor, gain[...], grad)
+            out[at, :] = grad_residual[at, :] + back
+            return carry
+
+        lax.fori_loop(0, out.shape[0] // 128, strip, 0)
+
+
+def input_grads(first, second, query, high, weight, inputs, grad_residual, gain):
+    heads, width, blk = query.shape
+    rows, model = inputs.shape
+    count = 4
+    steps = heads // count
+    given = (first, second, query, high)
+
+    def columns_of(number):
+        return pl.BlockSpec((model, count * width), lambda j: (0, number * steps + j))
+
+    return pl.pallas_call(
+        input_kernel,
+        grid=(steps,),
+        in_specs=[pl.BlockSpec((count,) + array.shape[1:], lambda j: (j, 0, 0)) for array in given]
+        + [columns_of(number) for number in range(3)]
+        + [whole((rows, model)), whole((rows, model)), whole((1, model))],
+        out_specs=whole((rows, model)),
+        out_shape=jax.ShapeDtypeStruct((rows, model), f32),
+        scratch_shapes=[pltpu.VMEM((model, rows), f32)],
+        compiler_params=pltpu.CompilerParams(vmem_limit_bytes=56 * MIB),
+        cost_estimate=pl.CostEstimate(
+            flops=6 * rows * model * model, bytes_accessed=24 * rows * model, transcendentals=0
+        ),
+        name="input_grads",
+    )(*given, weight, weight, weight, inputs, grad_residual, gain)
 
 
 def place_kernel(given, out):
@@ -623,7 +758,6 @@
     qvbias, projbias, upbias, downbias, gains, shifts = pieces
 
     inputs = activations.reshape(rows, model).astype(f32)
-    upstream = cotangent.reshape(rows, model).astype(f32)
     a1 = layer_norm(inputs, gains[0], shifts[0]).astype(bf16)
     a1_full = lax.all_gather(a1, ctx, axis=0, tiled=True)
 
@@ -672,35 +806,29 @@
     residual = inputs + layer_norm(proj_pre, gains[1], shifts[1])
     normed_mid = layer_norm(residual, gains[2], shifts[2]).astype(bf16)
     sizes = (rows, model, up_full.shape[0])
-    hidden, slope, branch = mlp_call(
+    given = cotangent.reshape(rows, model)
+    hidden, slope, layer_output, grad_branch, sums_three = mlp_call(
         mlp_forward_kernel,
         "mlp_forward",
-        (normed_mid, up_full, upbias[None, :], down_full),
-        ("rows", "tall", "line", "tall"),
-        (bf16, bf16, f32),
-        ("wide", "wide", "rows"),
+        (normed_mid, up_full, upbias[None, :], down_full, downbias[None, :], residual, given)
+        + (gains[3:4], shifts[3:4]),
+        ("rows", "tall", "line", "tall", "row", "rows", "rows", "row", "row"),
+        (bf16, bf16, bf16, bf16, f32),
+        ("wide", "wide", "rows", "rows", "sums"),
         *sizes,
-    )
-    branch = branch + downbias
-    layer_output = (residual + layer_norm(branch, gains[3], shifts[3])).astype(bf16)
-
-    grad_branch, gain_three, shift_three = norm_backward(branch, gains[3], shifts[3], upstream)
-    grad_branch = grad_branch.astype(bf16)
-    grad_pre, up_sums, grad_mid = mlp_call(
+        True,
+    )
+    grad_pre, up_sums, grad_residual, grad_proj_pre, sums_two = mlp_call(
         mlp_backward_kernel,
         "mlp_backward",
-        (grad_branch, down_full, slope, up_full),
-        ("rows", "tall", "wide", "tall"),
-        (bf16, f32, f32),
-        ("wide", "line", "rows"),
+        (grad_branch, down_full, slope, up_full, residual, proj_pre, given)
+        + (gains[1:2], gains[2:3]),
+        ("rows", "tall", "wide", "tall", "rows", "rows", "rows", "row", "row"),
+        (bf16, f32, f32, bf16, f32),
+        ("wide", "line", "rows", "rows", "sums"),
         *sizes,
-    )
-    grad_residual, gain_two, shift_two = norm_backward(residual, gains[2], shifts[2], grad_mid)
-    grad_residual = upstream + grad_residual
-    grad_proj_pre, gain_one, shift_one = norm_backward(
-        proj_pre, gains[1], shifts[1], grad_residual
-    )
-    grad_proj_pre = grad_proj_pre.astype(bf16)
+        True,
+    )
     grad_attended_t = dot(full_proj, grad_proj_pre, 1, 1).astype(bf16)
     given_high = to_heads(grad_attended_t[:, blk:])
     given_low = to_heads(grad_attended_t[:, :blk])
@@ -713,6 +841,7 @@
         (bf16, bf16),
         ("tall", "tall"),
         *sizes,
+        False,
     )
     grad_proj = dot(attended_t, grad_proj_pre, 1, 0).astype(bf16)
 
@@ -723,14 +852,14 @@
     early = jnp.concatenate(
         [
             up_sums[0],
-            jnp.sum(grad_branch.astype(f32), axis=0),
-            jnp.sum(grad_proj_pre.astype(f32), axis=0),
-            gain_one,
-            gain_two,
-            gain_three,
-            shift_one,
-            shift_two,
-            shift_three,
+            sums_three[2],
+            sums_two[4],
+            sums_two[0],
+            sums_two[2],
+            sums_three[0],
+            sums_two[1],
+            sums_two[3],
+            sums_three[1],
         ]
     ).astype(bf16)
     grad_proj = jnp.concatenate([grad_proj, early.reshape(-1, model)], axis=0)
@@ -750,9 +879,7 @@
 
     def token_grads(array):
         own = lax.dynamic_slice_in_dim(array, group * HEADS, HEADS, 0)
-        own = lax.all_to_all(own, "h", 0, 0, tiled=True)
-        own = own.reshape(HEADS, -1, width, array.shape[2])
-        return jnp.transpose(own, (1, 0, 2, 3)).reshape(-1, array.shape[2])
+        return lax.all_to_all(own, "h", 0, 0, tiled=True)
 
     grad_t, grad_n, delta, q_n = delta_rows(True, owner, given_high, out_high, q_t)
     high = (q_t[:, half:], q_n, grad_t, grad_n, log_high, delta)
@@ -802,21 +929,16 @@
     first_norm = own_columns(jnp.stack([gains[0], shifts[0]]))
     gain_zero = (gain_zero - first_norm[1] * shift_zero) / first_norm[0]
 
-    piece = blk // 2
-    low_key = [first_tokens[model:, :piece], second_tokens[:model]]
-    low_value = [first_tokens[model:, piece:], second_tokens[model:]]
-    low_rows = [
-        first_tokens[:model],
-        jnp.concatenate(low_key, axis=1),
-        jnp.concatenate(low_value, axis=1),
-    ]
-    high_rows = [query_tokens, high_tokens]
-    grads_t = jnp.concatenate(
-        [jnp.concatenate(low_rows, axis=0), jnp.concatenate(high_rows, axis=0)], axis=1
-    )
-    grad_normed = dot(grads_t, full_qkv, 0, 1)
-    grad_inputs, _, _ = norm_backward(inputs, gains[0], shifts[0], grad_normed)
-    input_grad = (grad_residual + grad_inputs).reshape(1, rows, model)
+    input_grad = input_grads(
+        first_tokens,
+        second_tokens,
+        query_tokens,
+        high_tokens,
+        full_qkv,
+        activations.reshape(rows, model),
+        grad_residual,
+        gains[0:1],
+    ).reshape(1, rows, model)
     early = own_columns(early)
     grad_gains = jnp.concatenate([gain_zero[None], early[2:5]], axis=0)
     grad_biases = jnp.concatenate([shift_zero[None], early[5:8]], axis=0)

time: 1150 us -> 1130 us (0.983)
  Pallas kernels: 715 us -> 752 us
  other arithmetic: 52.9 us -> 24.2 us
  matrix products: 29.8 us -> 10.9 us
    reduce_sum x10 -> x0, other arithmetic: 21.4 us -> none  [the longest x4 10.8 us: layer_norm(): centered = values - average]
    dot_general x4 -> x3, matrix products: 29.8 us -> 10.9 us  [dot(): lax.dot_general(a, b, (((ca,), (cb,)), ((), ())), preferred_element_type=...]
    pallas_call x0 -> x1, Pallas kernels: none -> 18.4 us  [input_grads(): pl.pallas_call(input_kernel, grid=(steps,), in_specs=[pl.BlockSpec((count...]
    pallas_call x3, Pallas kernels: 78.4 us -> 96.7 us  [mlp_call(): pl.pallas_call(kernel, grid=(hidden // chunk,), in_specs=[specs[kind] for...]
    unnamed x146 -> x128, local copies, waits for them, and re-layouts: 32.1 us -> 35.6 us
  transfers between devices with their start and end apart: 15 -> 15, of which waited for: 3 -> 4; matrix products, arithmetic and copies ran while one was open for 5% -> 3% of each run, Pallas kernels for 58% -> 60%
where the time goes in v4:
time: 1130 us; the launch traced here: 1120 us
  Pallas kernels  752 us (67%)
  waiting for transfers between devices  205 us (18%)
  starting transfers between devices  48.4 us (4%)
  local copies, waits for them, and re-layouts  43.4 us (4%)
  other arithmetic  24.2 us (2%)
  blocking collectives  18.9 us (2%)
  between operations  15.4 us (1%)
    pallas_call x4, Pallas kernels, backward(): pl.pallas_call(functools.partial(backward_kernel, kind, 2 * skip, len(aft...  397 us
    pallas_call x2, Pallas kernels, forward(): pl.pallas_call(functools.partial(forward_kernel, base), grid_spec=pltpu.P...  175 us
    all_gather x1, waiting for transfers between devices, local(): a1_full = lax.all_gather(a1, ctx, axis=0, tiled=True)  156 us
    pallas_call x3, Pallas kernels, mlp_call(): pl.pallas_call(kernel, grid=(hidden // chunk,), in_specs=[specs[kind] for...  96.7 us
    unnamed x128, local copies, waits for them, and re-layouts  35.6 us
    pallas_call x1, Pallas kernels, weight_grad(): pl.pallas_call(weight_kernel, grid_spec=pltpu.PrefetchScalarGridSpec(num_...  27 us
    all_to_all x4, waiting for transfers between devices, token_grads(): return lax.all_to_all(own, 'h', 0, 0, tiled=True)  26.1 us
    all_to_all x4, starting transfers between devices, token_grads(): return lax.all_to_all(own, 'h', 0, 0, tiled=True)  25.5 us
  transfers between devices with their start and end apart: 15, of which 4 were waited for; matrix products, arithmetic and copies ran while one was open for 3% of the time, Pallas kernels for 60%

profile of v4, /device:TPU:13, one launch (start us, length us, event | category | flops | bytes accessed | tf_op | source)
XLA Modules:
  0.0 1118.2 jit_solution(2692615667047900023)
XLA Ops:
  12.0 3.3 all-gather
  30.1 6.8 all_gather.33
  38.5 155.7 %all-gather.9.cloned.1.call-done.refs_0_.refs_1_.refs_2_.refs_3_.a1 = bf16[16384,1024]{1,0:T(8,128)(2,1)} async-done(((bf16[1024,1024]{1,0:T(8,128)(2,1)}), bf16[16384,1024]{1,0:T(8,128)(2,1)}) %all-gather.9.cloned.1.call-update) | async-done | bytes 33554448 | tf_op jit(solution)/shard_map/all_gather | solution.py:762
  194.2 18.6 %project.1 = (bf16[64,16384]{1,0:T(8,128)(2,1)S(1)}, bf16[16384,64]{1,0:T(8,128)(2,1)}, bf16[64,16384]{1,0:T(8,128)(2,1)S(1)}) custom-call(s32[32]{0:T(128)S(1)} %get-tuple-element.131.table, bf16[16384,1024]{1,0:T(8,128)(2,1)} %all-gather.9.cloned.1.call-done.refs_0_.refs_1_.refs_2_.refs_3_.a1, ...), custom_call_target="tpu_custom_call" | custom-call | flops 8589934592 | bytes 33554432 | tf_op jit(solution)/shard_map/project/pallas_call | solution.py:72
  215.4 49.8 %forward_low.1 = (f32[64,8192]{1,0:T(8,128)}, f32[1,8192]{1,0:T(1,128)}, bf16[16,64,512]{2,1,0:T(8,128)(2,1)}) custom-call(s32[32]{0:T(128)} %get-tuple-element.132.table.refs_0_, bf16[64,16384]{1,0:T(8,128)(2,1)} %copy-done, bf16[16384,64]{1,0:T(8,128)(2,1)} %get-tuple-element.64.k_n.refs_7_, bf16[64,16384]{1,0:T(8,128)(2,1)} %copy-done.9), custom_call_target="tpu_custom_call" | custom-call | flops 34359738368 | bytes 12582912 | tf_op jit(solution)/shard_map/forward_low/pallas_call | solution.py:162
  265.2 5.4 all-to-all-start
  270.7 125.7 %forward_high.1 = (f32[64,8192]{1,0:T(8,128)}, f32[1,8192]{1,0:T(1,128)}, bf16[16,64,512]{2,1,0:T(8,128)(2,1)}) custom-call(s32[32]{0:T(128)} %get-tuple-element.132.table.refs_0_, bf16[64,16384]{1,0:T(8,128)(2,1)} %copy-done, bf16[16384,64]{1,0:T(8,128)(2,1)} %get-tuple-element.64.k_n.refs_7_, bf16[64,16384]{1,0:T(8,128)(2,1)} %copy-done.9), custom_call_target="tpu_custom_call" | custom-call | flops 103079215104 | bytes 12582912 | tf_op jit(solution)/shard_map/forward_high/pallas_call | solution.py:162
  396.4 6.6 all-to-all-start.1
  407.4 20.8 %all-to-all-done.1 = bf16[16,64,512]{2,1,0:T(8,128)(2,1)S(1)} async-done(((bf16[16,64,512]{2,1,0:T(8,128)(2,1)}), bf16[16,64,512]{2,1,0:T(8,128)(2,1)S(1)}, u32[]{:S(2)}, u32[]{:S(2)}) %all-to-all-start.1) | async-done | bytes 1048608 | tf_op jit(solution)/shard_map/all_to_all | solution.py:790
  428.2 4.5 fusion.19
  441.6 37.7 %mlp_forward.1 = (bf16[1024,4096]{1,0:T(8,128)(2,1)}, bf16[1024,4096]{1,0:T(8,128)(2,1)}, bf16[1024,1024]{1,0:T(8,128)(2,1)}, bf16[1024,1024]{1,0:T(8,128)(2,1)}, f32[8,1024]{1,0:T(8,128)}) custom-call(bf16[1024,1024]{1,0:T(8,128)(2,1)} %add_convert_fusion.normed, bf16[4096,1024]{1,0:T(8,128)(2,1)} %all-gather.13.cloned.1.call-done.up, f32[1,4096]{1,0:T(1,128)} %bitcast.126, ...), custom_call_target="tpu_custom_call" | custom-call | flops 17179869184 | bytes 33554432 | tf_op jit(solution)/shard_map/mlp_forward/pallas_call | solution.py:616
  479.3 36.0 %mlp_backward.1 = (bf16[1024,4096]{1,0:T(8,128)(2,1)}, f32[1,4096]{1,0:T(1,128)}, f32[1024,1024]{1,0:T(8,128)}, bf16[1024,1024]{1,0:T(8,128)(2,1)}, f32[8,1024]{1,0:T(8,128)}) custom-call(bf16[1024,1024]{1,0:T(8,128)(2,1)} %get-tuple-element.69.grad, bf16[4096,1024]{1,0:T(8,128)(2,1)} %all-gather.15.cloned.1.call-done.down, ...), custom_call_target="tpu_custom_call" | custom-call | flops 17179869184 | bytes 33554432 | tf_op jit(solution)/shard_map/mlp_backward/pallas_call | solution.py:616
  515.4 4.1 convolution_convert_fusion
  523.6 4.6 all-to-all-start.2
  529.9 23.0 %mlp_grads.1 = (bf16[4096,1024]{1,0:T(8,128)(2,1)}, bf16[4096,1024]{1,0:T(8,128)(2,1)}) custom-call(bf16[1024,4096]{1,0:T(8,128)(2,1)} %get-tuple-element.72.hidden, bf16[1024,1024]{1,0:T(8,128)(2,1)} %get-tuple-element.69.grad, bf16[1024,4096]{1,0:T(8,128)(2,1)} %get-tuple-element.73.grad_pre, bf16[1024,1024]{1,0:T(8,128)(2,1)} %add_convert_fusion.normed), custom_call_target="tpu_custom_call" | custom-call | flops 17179869184 | bytes 33554432 | tf_op jit(solution)/shard_map/mlp_grads/pallas_call | solution.py:616
  553.1 6.1 all-to-all-start.3
  561.9 3.3 delta_high.1
  569.5 103.9 %backward_high.1 = (f32[64,8192]{1,0:T(8,128)}, bf16[16,128,512]{2,1,0:T(8,128)(2,1)}) custom-call(s32[32]{0:T(128)} %get-tuple-element.132.table.refs_0_, bf16[64,8192]{1,0:T(8,128)(2,1)} %get-tuple-element.136.refs_1_, bf16[8192,64]{1,0:T(8,128)(2,1)} %copy-done.11, bf16[64,8192]{1,0:T(8,128)(2,1)} %copy-done.14, bf16[8192,64]{1,0:T(8,128)(2,1)} %copy-done.10, ...), custom_call_target="tpu_custom_call" | custom-call | flops 17179869184 | bytes 16777216 | tf_op jit(solution)/shard_map/backward_high/pallas_call | solution.py:407
  673.4 6.1 all-to-all-start.4
  681.9 9.0 delta_low.1
  695.2 102.3 %backward_low.1 = (f32[8192,64]{1,0:T(8,128)}, f32[8192,64]{1,0:T(8,128)}, bf16[16,64,512]{2,1,0:T(8,128)(2,1)}) custom-call(s32[32]{0:T(128)} %get-tuple-element.132.table.refs_0_, bf16[64,8192]{1,0:T(8,128)(2,1)} %get-tuple-element.135.refs_1_, bf16[8192,64]{1,0:T(8,128)(2,1)} %copy-done.13, bf16[64,8192]{1,0:T(8,128)(2,1)} %copy-done.15, ...), custom_call_target="tpu_custom_call" | custom-call | flops 17179869184 | bytes 16777216 | tf_op jit(solution)/shard_map/backward_low/pallas_call | solution.py:407
  797.4 96.0 %backward_first.1 = (f32[64,8192]{1,0:T(8,128)}, bf16[16,128,512]{2,1,0:T(8,128)(2,1)}) custom-call(s32[32]{0:T(128)} %get-tuple-element.132.table.refs_0_, bf16[64,8192]{1,0:T(8,128)(2,1)} %get-tuple-element.136.refs_1_, bf16[8192,64]{1,0:T(8,128)(2,1)} %copy-done.11, bf16[64,8192]{1,0:T(8,128)(2,1)} %copy-done.14, bf16[8192,64]{1,0:T(8,128)(2,1)} %copy-done.10, ...), custom_call_target="tpu_custom_call" | custom-call | flops 17179869184 | bytes 16777216 | tf_op jit(solution)/shard_map/backward_first/pallas_call | solution.py:407
  893.5 6.4 all-to-all-start.5
  899.9 95.3 %backward_second.1 = (bf16[16,64,512]{2,1,0:T(8,128)(2,1)}, bf16[16,128,256]{2,1,0:T(8,128)(2,1)}) custom-call(s32[32]{0:T(128)} %get-tuple-element.132.table.refs_0_, bf16[64,8192]{1,0:T(8,128)(2,1)} %get-tuple-element.136.refs_1_, bf16[8192,64]{1,0:T(8,128)(2,1)} %copy-done.11, bf16[64,8192]{1,0:T(8,128)(2,1)} %copy-done.14, bf16[8192,64]{1,0:T(8,128)(2,1)} %copy-done.10, ...), custom_call_target="tpu_custom_call" | custom-call | flops 17179869184 | bytes 16777216 | tf_op jit(solution)/shard_map/backward_second/pallas_call | solution.py:407
  995.2 6.0 all-to-all-start.6
  1002.5 27.0 %weight_grad.1 = (bf16[2,208,512]{2,1,0:T(8,128)(2,1)S(1)}, f32[2048,1024]{1,0:T(8,128)}, f32[2048,1024]{1,0:T(8,128)}) custom-call(s32[1]{0:T(128)} %bitcast.20.part, bf16[16,128,512]{2,1,0:T(8,128)(2,1)S(1)} %copy-done.2, bf16[16,128,512]{2,1,0:T(8,128)(2,1)} %get-tuple-element.99.first, bf16[16,64,512]{2,1,0:T(8,128)(2,1)S(1)} %copy-done.3, ...), custom_call_target="tpu_custom_call" | custom-call | flops 6442450944 | bytes 33554432 | tf_op jit(solution)/shard_map/weight_grad/pallas_call | solution.py:478
  1029.5 8.9 all_to_all.45
  1039.2 7.0 all-to-all-start.8
  1051.8 26.1 %all-to-all-done.8.second = bf16[16,128,256]{2,1,0:T(8,128)(2,1)S(1)} async-done(((bf16[16,128,256]{2,1,0:T(8,128)(2,1)}), bf16[16,128,256]{2,1,0:T(8,128)(2,1)S(1)}, u32[]{:S(2)}, u32[]{:S(2)}) %all-to-all-start.8) | async-done | bytes 1048608 | tf_op jit(solution)/shard_map/all_to_all | solution.py:882
  1078.9 18.4 %input_grads.1 = f32[1024,1024]{1,0:T(8,128)} custom-call(bf16[16,128,512]{2,1,0:T(8,128)(2,1)} %all-to-all-done.5.refs_0_.first, bf16[16,128,256]{2,1,0:T(8,128)(2,1)} %copy-done.24, bf16[16,64,512]{2,1,0:T(8,128)(2,1)} %all-to-all-done.6.query, bf16[16,128,512]{2,1,0:T(8,128)(2,1)} %all-to-all-done.4.refs_13_.high, ...), custom_call_target="tpu_custom_call" | custom-call | flops 6442450944 | bytes 25165824 | tf_op jit(solution)/shard_map/input_grads/pallas_call | solution.py:682
  1099.3 5.8 place.1
  1105.5 4.2 fusion.1
  (216 shorter events, 68.7 us)
Async XLA Ops:
  7.2 14.2 %copy-start.18 = (bf16[1,1024,1024]{2,1,0:T(8,128)(2,1)S(1)}, bf16[1,1024,1024]{2,1,0:T(8,128)(2,1)}, u32[]{:S(2)}) copy-start(bf16[1,1024,1024]{2,1,0:T(8,128)(2,1)} %param.13) | copy-start | bytes 6291460
  7.2 187.0 %all-gather.9.cloned.1.call-start = ((), (), s32[]{:S(2)}) async-start(), calls=%async_computation.9 | async-start | bytes 35651584 | tf_op jit(solution)/shard_map/all_gather | solution.py:762
  15.3 10.4 copy-start.27
  23.6 383.8 %all-gather.11.cloned.1.call-start = ((), (), s32[]{:S(2)}) async-start(), calls=%async_computation.10 | async-start | bytes 3145728 | tf_op jit(solution)/shard_map/all_gather | solution.py:800
  24.4 417.2 %all-gather.13.cloned.1.call-start = ((), (), s32[]{:S(2)}) async-start(), calls=%async_computation.11 | async-start | bytes 12582912 | tf_op jit(solution)/shard_map/all_gather | solution.py:801
  25.1 416.5 %all-gather.15.cloned.1.call-start = ((), (), s32[]{:S(2)}) async-start(), calls=%async_computation.12 | async-start | bytes 12582912 | tf_op jit(solution)/shard_map/all_gather | solution.py:802
  26.3 10.8 copy-start.43
  265.2 131.2 %all-to-all-start = ((bf16[16,64,512]{2,1,0:T(8,128)(2,1)}), bf16[16,64,512]{2,1,0:T(8,128)(2,1)S(1)}, u32[]{:S(2)}, u32[]{:S(2)}) async-start(bf16[16,64,512]{2,1,0:T(8,128)(2,1)} %get-tuple-element.66), calls=%async_computation | async-start | bytes 2097152 | tf_op jit(solution)/shard_map/all_to_all | solution.py:790
  270.6 133.1 %copy-start.42 = (f32[1,4,2,128]{3,2,1,0:T(2,128)S(1)}, f32[1,4,2,128]{3,2,1,0:T(2,128)}, u32[]{:S(2)}) copy-start(f32[1,4,2,128]{3,2,1,0:T(2,128)} %get-tuple-element.159) | copy-start | bytes 12292
  270.6 133.1 %copy-start.35 = (f32[1,4,2,128]{3,2,1,0:T(2,128)S(1)}, f32[1,4,2,128]{3,2,1,0:T(2,128)}, u32[]{:S(2)}) copy-start(f32[1,4,2,128]{3,2,1,0:T(2,128)} %get-tuple-element.152) | copy-start | bytes 12292
  270.6 133.1 %copy-start.41 = (f32[1,4,2,128]{3,2,1,0:T(2,128)S(1)}, f32[1,4,2,128]{3,2,1,0:T(2,128)}, u32[]{:S(2)}) copy-start(f32[1,4,2,128]{3,2,1,0:T(2,128)} %get-tuple-element.158) | copy-start | bytes 12292
  270.6 133.1 %copy-start.34 = (f32[1,4,2,128]{3,2,1,0:T(2,128)S(1)}, f32[1,4,2,128]{3,2,1,0:T(2,128)}, u32[]{:S(2)}) copy-start(f32[1,4,2,128]{3,2,1,0:T(2,128)} %get-tuple-element.151) | copy-start | bytes 12292
  270.6 133.1 %copy-start.40 = (f32[1,1,2,512]{3,2,1,0:T(2,128)S(1)}, f32[1,1,2,512]{3,2,1,0:T(2,128)}, u32[]{:S(2)}) copy-start(f32[1,1,2,512]{3,2,1,0:T(2,128)} %get-tuple-element.157) | copy-start | bytes 12292
  270.6 133.7 %copy-start.33 = (f32[1,1,2,512]{3,2,1,0:T(2,128)S(1)}, f32[1,1,2,512]{3,2,1,0:T(2,128)}, u32[]{:S(2)}) copy-start(f32[1,1,2,512]{3,2,1,0:T(2,128)} %get-tuple-element.150) | copy-start | bytes 12292
  270.7 134.3 %copy-start.28 = (f32[1,1,2,2048]{3,2,1,0:T(2,128)S(1)}, f32[1,1,2,2048]{3,2,1,0:T(2,128)}, u32[]{:S(2)}) copy-start(f32[1,1,2,2048]{3,2,1,0:T(2,128)} %get-tuple-element.146) | copy-start | bytes 49156
  270.7 135.5 %copy-start.39 = (f32[1,1,2,512]{3,2,1,0:T(2,128)S(1)}, f32[1,1,2,512]{3,2,1,0:T(2,128)}, u32[]{:S(2)}) copy-start(f32[1,1,2,512]{3,2,1,0:T(2,128)} %get-tuple-element.155) | copy-start | bytes 12292
  270.7 136.1 %copy-start.38 = (f32[1,1,2,512]{3,2,1,0:T(2,128)S(1)}, f32[1,1,2,512]{3,2,1,0:T(2,128)}, u32[]{:S(2)}) copy-start(f32[1,1,2,512]{3,2,1,0:T(2,128)} %get-tuple-element.156) | copy-start | bytes 12292
  396.4 31.8 %all-to-all-start.1 = ((bf16[16,64,512]{2,1,0:T(8,128)(2,1)}), bf16[16,64,512]{2,1,0:T(8,128)(2,1)S(1)}, u32[]{:S(2)}, u32[]{:S(2)}) async-start(bf16[16,64,512]{2,1,0:T(8,128)(2,1)} %get-tuple-element.67), calls=%async_computation.1 | async-start | bytes 2097152 | tf_op jit(solution)/shard_map/all_to_all | solution.py:790
  479.3 36.0 %copy-start.26 = (bf16[16,64,512]{2,1,0:T(8,128)(2,1)S(1)}, bf16[16,64,512]{2,1,0:T(8,128)(2,1)}, u32[]{:S(2)}) copy-start(bf16[16,64,512]{2,1,0:T(8,128)(2,1)} %copy-done.25) | copy-start | bytes 3145732
  523.6 29.5 %all-to-all-start.2 = ((bf16[16,64,512]{2,1,0:T(8,128)(2,1)}), bf16[16,64,512]{2,1,0:T(8,128)(2,1)S(1)}, u32[]{:S(2)}, u32[]{:S(2)}) async-start(bf16[16,64,512]{2,1,0:T(8,128)(2,1)} %bitcast.15), calls=%async_computation.2 | async-start | bytes 2097152 | tf_op jit(solution)/shard_map/all_to_all | solution.py:793
  528.2 473.0 %all-reduce.3.cloned.1.call-start = ((), (), s32[]{:S(2)}) async-start(), calls=%async_computation.15 | async-start | bytes 37814272 | tf_op jit(solution)/shard_map/psum | solution.py:869
  553.1 120.3 %all-to-all-start.3 = ((bf16[16,64,512]{2,1,0:T(8,128)(2,1)}), bf16[16,64,512]{2,1,0:T(8,128)(2,1)}, u32[]{:S(2)}, u32[]{:S(2)}) async-start(bf16[16,64,512]{2,1,0:T(8,128)(2,1)} %bitcast.107), calls=%async_computation.3 | async-start | bytes 2097152 | tf_op jit(solution)/shard_map/all_to_all | solution.py:793
  673.4 124.1 %all-to-all-start.4 = ((bf16[16,128,512]{2,1,0:T(8,128)(2,1)}), bf16[16,128,512]{2,1,0:T(8,128)(2,1)}, u32[]{:S(2)}, u32[]{:S(2)}) async-start(bf16[16,128,512]{2,1,0:T(8,128)(2,1)} %get-tuple-element.96.high_pair), calls=%async_computation.4 | async-start | bytes 4194304 | tf_op jit(solution)/shard_map/all_to_all | solution.py:882
  679.4 372.4 %all-gather.17.cloned.1.call-start = ((), (), s32[]{:S(2)}) async-start(), calls=%async_computation.13 | async-start | bytes 9437184 | tf_op jit(solution)/shard_map/all_gather | solution.py:803
  893.5 101.7 %all-to-all-start.5 = ((bf16[16,128,512]{2,1,0:T(8,128)(2,1)}), bf16[16,128,512]{2,1,0:T(8,128)(2,1)}, u32[]{:S(2)}, u32[]{:S(2)}) async-start(bf16[16,128,512]{2,1,0:T(8,128)(2,1)} %get-tuple-element.99.first), calls=%async_computation.5 | async-start | bytes 4194304 | tf_op jit(solution)/shard_map/all_to_all | solution.py:882
  899.9 101.3 %copy-start.2 = (bf16[16,128,512]{2,1,0:T(8,128)(2,1)S(1)}, bf16[16,128,512]{2,1,0:T(8,128)(2,1)}, u32[]{:S(2)}) copy-start(bf16[16,128,512]{2,1,0:T(8,128)(2,1)} %get-tuple-element.96.high_pair) | copy-start | bytes 6291460
  995.2 34.3 %all-to-all-start.6 = ((bf16[16,64,512]{2,1,0:T(8,128)(2,1)}), bf16[16,64,512]{2,1,0:T(8,128)(2,1)}, u32[]{:S(2)}, u32[]{:S(2)}) async-start(bf16[16,64,512]{2,1,0:T(8,128)(2,1)} %get-tuple-element.101.query), calls=%async_computation.6 | async-start | bytes 2097152 | tf_op jit(solution)/shard_map/all_to_all | solution.py:882
  1001.2 96.2 %all-gather.19.cloned.1.call-start = ((), (), s32[]{:S(2)}) async-start(), calls=%async_computation.14 | async-start | bytes 3620864 | tf_op jit(solution)/shard_map/all_gather | solution.py:920
  1002.5 43.8 %copy-start.37 = (f32[1,1,2,512]{3,2,1,0:T(2,128)S(1)}, f32[1,1,2,512]{3,2,1,0:T(2,128)}, u32[]{:S(2)}) copy-start(f32[1,1,2,512]{3,2,1,0:T(2,128)} %get-tuple-element.154) | copy-start | bytes 12292
  1002.5 43.8 %copy-start.32 = (f32[1,1,2,512]{3,2,1,0:T(2,128)S(1)}, f32[1,1,2,512]{3,2,1,0:T(2,128)}, u32[]{:S(2)}) copy-start(f32[1,1,2,512]{3,2,1,0:T(2,128)} %get-tuple-element.149) | copy-start | bytes 12292
  1039.2 38.7 %all-to-all-start.8 = ((bf16[16,128,256]{2,1,0:T(8,128)(2,1)}), bf16[16,128,256]{2,1,0:T(8,128)(2,1)S(1)}, u32[]{:S(2)}, u32[]{:S(2)}) async-start(bf16[16,128,256]{2,1,0:T(8,128)(2,1)} %get-tuple-element.107.second), calls=%async_computation.8 | async-start | bytes 2097152 | tf_op jit(solution)/shard_map/all_to_all | solution.py:882
  1046.3 31.7 %copy-start.29 = (f32[1,1,2,512]{3,1,2,0:T(1,128)}, f32[1,1,2,512]{3,1,2,0:T(1,128)S(1)}, u32[]{:S(2)}) copy-start(f32[1,1,2,512]{3,1,2,0:T(1,128)S(1)} %copy.56) | copy-start | bytes 12292
  (29 other events, 83.9 us)
Sparse Core Ops, SparseCore 0:
  23.7 170.4 all-gather.8
  195.7 33.0 all-gather.10
  230.3 104.0 all-gather.12
  335.8 103.9 all-gather.14
  553.2 389.7 all-reduce.2
  944.4 84.1 all-gather.16
  1039.4 57.4 all-gather.18

commit v5 on v4

--- a/solution.py
+++ b/solution.py
@@ -286,8 +286,7 @@
         scores[slot] = dot(keys, q_t[:, at], 1, 0)
         grads[slot] = dot(values, grad_t[:, at], 1, 0)
 
-    def absorb(index, tile_scores, prob_grads):
-        at = columns(index, blk)
+    def absorb(at, tile_scores, prob_grads):
         rows = tile_scores.shape[0]
         probs = jnp.exp(tile_scores - log_total[:, at])
         score_grads = (probs * (prob_grads - delta[:, at])).astype(bf16)
@@ -295,15 +294,14 @@
         key_sum[:rows] += dot(score_grads, q_n[at, :], 1, 0)
         query_sum[:, at] += dot(keys_t[:, :rows], score_grads, 1, 0)
 
-    def diagonal(half):
-        index = 2 * step + half
-        at = columns(index, blk)
-        shape = ((half + 1) * blk, blk)
+    def diagonal(number):
+        at = columns(4 * step + number, piece)
+        shape = ((number + 1) * piece, piece)
         key_pos = lax.broadcasted_iota(jnp.int32, shape, 0)
-        query_pos = half * blk + lax.broadcasted_iota(jnp.int32, shape, 1)
+        query_pos = number * piece + lax.broadcasted_iota(jnp.int32, shape, 1)
         tile_scores = dot(keys[: shape[0]], q_t[:, at], 1, 0)
         tile_scores = jnp.where(query_pos >= key_pos, tile_scores, NEG)
-        absorb(index, tile_scores, dot(values[: shape[0]], grad_t[:, at], 1, 0))
+        absorb(at, tile_scores, dot(values[: shape[0]], grad_t[:, at], 1, 0))
 
     def sweep(first, pairs):
         prepare(first, 0)
@@ -311,9 +309,9 @@
         def body(pair, carry):
             index = first + 2 * pair
             prepare(index + 1, 1)
-            absorb(index, scores[0], grads[0])
+            absorb(columns(index, blk), scores[0], grads[0])
             prepare(jnp.minimum(index + 2, slots - 1), 0)
-            absorb(index + 1, scores[1], grads[1])
+            absorb(columns(index + 1, blk), scores[1], grads[1])
             return carry
 
         lax.fori_loop(0, pairs, body, 0)
@@ -321,8 +319,8 @@
     if cross:
         sweep(0, slots // 2)
     else:
-        for half in range(2):
-            diagonal(half)
+        for number in range(4):
+            diagonal(number)
 
         @pl.when(2 * step + 2 < slots)
         def _():
@@ -430,11 +428,9 @@
     )(table, *queries, k_n, v_t, *starts, *after)
 
 
-def weight_kernel(part, high_pair, first, query, second, a1, down, up, *refs):
-    out, down_out, up_out, total, sums = refs[-5:]
+def weight_kernel(high_pair, first, query, second, a1, *refs):
+    out, total, sums = refs[-3:]
     _, width, blk = query.shape
-    down_out[...] = down[...].astype(f32)
-    up_out[...] = up[...].astype(f32)
     piece = blk // 2
     parts, rows, length = out.shape
     step = pl.program_id(0)
@@ -465,37 +461,27 @@
             out[number] = jnp.concatenate([own, tail], axis=0).astype(bf16)
 
 
-def weight_grad(part, high_pair, first, query, second, a1_full, down, up, parts, after):
+def weight_grad(high_pair, first, query, second, a1_full, parts, after):
     slots, width, blk = query.shape
     tokens, model = a1_full.shape
     rows = 3 * width
     shape = (parts, rows + 16, model // parts)
     given = (high_pair, first, query, second)
-    own = down.shape[0] // parts
-    strip = own // slots
-    summed = pl.BlockSpec((strip, model), lambda s, t: (t[0] * slots + s, 0))
-    kept = pl.BlockSpec((strip, model), lambda s, t: (s, 0))
     return pl.pallas_call(
         weight_kernel,
-        grid_spec=pltpu.PrefetchScalarGridSpec(
-            num_scalar_prefetch=1,
-            grid=(slots,),
-            in_specs=[
-                pl.BlockSpec((1,) + array.shape[1:], lambda s, t: (s, 0, 0)) for array in given
-            ]
-            + [pl.BlockSpec((2 * blk, model), lambda s, t: (s, 0)), summed, summed]
-            + [pl.BlockSpec(memory_space=pl.ANY)] * len(after),
-            out_specs=[whole(shape), kept, kept],
-            scratch_shapes=[pltpu.VMEM((rows, model), f32), pltpu.VMEM((rows, 128), f32)],
-        ),
-        out_shape=[jax.ShapeDtypeStruct(shape, bf16)]
-        + [jax.ShapeDtypeStruct((own, model), f32)] * 2,
+        grid=(slots,),
+        in_specs=[pl.BlockSpec((1,) + array.shape[1:], lambda s: (s, 0, 0)) for array in given]
+        + [pl.BlockSpec((2 * blk, model), lambda s: (s, 0))]
+        + [pl.BlockSpec(memory_space=pl.ANY)] * len(after),
+        out_specs=whole(shape),
+        out_shape=jax.ShapeDtypeStruct(shape, bf16),
+        scratch_shapes=[pltpu.VMEM((rows, model), f32), pltpu.VMEM((rows, 128), f32)],
         compiler_params=pltpu.CompilerParams(vmem_limit_bytes=48 * MIB),
         cost_estimate=pl.CostEstimate(
             flops=2 * rows * tokens * model, bytes_accessed=2 * tokens * model, transcendentals=0
         ),
         name="weight_grad",
-    )(part.reshape(1), *given, a1_full, down, up, *after)
+    )(*given, a1_full, *after)
 
 
 def normalize(values):
@@ -900,18 +886,11 @@
         length = array.shape[1] // weight_parts
         return lax.dynamic_slice_in_dim(array, part * length, length, 1)
 
-    columns_grad, grad_downward, grad_upward = weight_grad(
-        part.astype(jnp.int32),
-        high_pair,
-        first,
-        query,
-        second,
-        a1_full,
-        grad_downward,
-        grad_upward,
-        weight_parts,
-        (first_tokens,),
-    )
+    columns_grad = weight_grad(
+        high_pair, first, query, second, a1_full, weight_parts, (first_tokens,) + tuple(summed)
+    )
+    grad_downward = own_rows(grad_downward).astype(f32)
+    grad_upward = own_rows(grad_upward).astype(f32)
     columns_grad, query_tokens = lax.optimization_barrier((columns_grad, query_tokens))
     columns_grad = lax.all_to_all(columns_grad, "wt", 0, 0, tiled=True)
     columns_grad = jnp.sum(columns_grad.astype(f32), axis=0).astype(bf16)

time: 1130 us -> 1120 us (level)
  Pallas kernels: 752 us -> 740 us
  other arithmetic: 24.2 us -> 35.8 us
    convert_element_type x0 -> x1, other arithmetic: none -> 11.8 us  [local(): grad_downward = own_rows(grad_downward).astype(f32)]
  transfers between devices with their start and end apart: 15 -> 15, of which waited for: 4 -> 5; matrix products, arithmetic and copies ran while one was open for 3% -> 4% of each run, Pallas kernels for 60% -> 59%
where the time goes in v5:
time: 1120 us; the launch traced here: 1110 us
  Pallas kernels  740 us (66%)
  waiting for transfers between devices  197 us (18%)
  starting transfers between devices  47 us (4%)
  local copies, waits for them, and re-layouts  43.1 us (4%)
  other arithmetic  35.8 us (3%)
  blocking collectives  24.2 us (2%)
  between operations  15.4 us (1%)
    pallas_call x4, Pallas kernels, backward(): pl.pallas_call(functools.partial(backward_kernel, kind, 2 * skip, len(aft...  392 us
    pallas_call x2, Pallas kernels, forward(): pl.pallas_call(functools.partial(forward_kernel, base), grid_spec=pltpu.P...  175 us
    all_gather x1, waiting for transfers between devices, local(): a1_full = lax.all_gather(a1, ctx, axis=0, tiled=True)  156 us
    pallas_call x3, Pallas kernels, mlp_call(): pl.pallas_call(kernel, grid=(hidden // chunk,), in_specs=[specs[kind] for...  96.8 us
    unnamed x128, local copies, waits for them, and re-layouts  35.3 us
    all_to_all x4, starting transfers between devices, token_grads(): return lax.all_to_all(own, 'h', 0, 0, tiled=True)  24 us
  transfers between devices with their start and end apart: 15, of which 5 were waited for; matrix products, arithmetic and copies ran while one was open for 4% of the time, Pallas kernels for 59%

profile of v5, /device:TPU:13, one launch (start us, length us, event | category | flops | bytes accessed | tf_op | source)
XLA Modules:
  0.0 1113.3 jit_solution(16858036783153208693)
XLA Ops:
  30.1 6.8 all_gather.33
  38.5 155.7 %all-gather.9.cloned.1.call-done.refs_0_.refs_1_.refs_2_.refs_3_.a1 = bf16[16384,1024]{1,0:T(8,128)(2,1)} async-done(((bf16[1024,1024]{1,0:T(8,128)(2,1)}), bf16[16384,1024]{1,0:T(8,128)(2,1)}) %all-gather.9.cloned.1.call-update) | async-done | bytes 33554448 | tf_op jit(solution)/shard_map/all_gather | solution.py:748
  194.2 18.6 %project.1 = (bf16[64,16384]{1,0:T(8,128)(2,1)S(1)}, bf16[16384,64]{1,0:T(8,128)(2,1)}, bf16[64,16384]{1,0:T(8,128)(2,1)S(1)}) custom-call(s32[32]{0:T(128)S(1)} %get-tuple-element.125.table, bf16[16384,1024]{1,0:T(8,128)(2,1)} %all-gather.9.cloned.1.call-done.refs_0_.refs_1_.refs_2_.refs_3_.a1, ...), custom_call_target="tpu_custom_call" | custom-call | flops 8589934592 | bytes 33554432 | tf_op jit(solution)/shard_map/project/pallas_call | solution.py:72
  215.4 49.8 %forward_low.1 = (f32[64,8192]{1,0:T(8,128)}, f32[1,8192]{1,0:T(1,128)}, bf16[16,64,512]{2,1,0:T(8,128)(2,1)}) custom-call(s32[32]{0:T(128)} %get-tuple-element.126.table.refs_0_, bf16[64,16384]{1,0:T(8,128)(2,1)} %copy-done, bf16[16384,64]{1,0:T(8,128)(2,1)} %get-tuple-element.61.k_n.refs_7_, bf16[64,16384]{1,0:T(8,128)(2,1)} %copy-done.9), custom_call_target="tpu_custom_call" | custom-call | flops 34359738368 | bytes 12582912 | tf_op jit(solution)/shard_map/forward_low/pallas_call | solution.py:162
  265.2 5.3 all-to-all-start
  270.6 125.7 %forward_high.1 = (f32[64,8192]{1,0:T(8,128)}, f32[1,8192]{1,0:T(1,128)}, bf16[16,64,512]{2,1,0:T(8,128)(2,1)}) custom-call(s32[32]{0:T(128)} %get-tuple-element.126.table.refs_0_, bf16[64,16384]{1,0:T(8,128)(2,1)} %copy-done, bf16[16384,64]{1,0:T(8,128)(2,1)} %get-tuple-element.61.k_n.refs_7_, bf16[64,16384]{1,0:T(8,128)(2,1)} %copy-done.9), custom_call_target="tpu_custom_call" | custom-call | flops 103079215104 | bytes 12582912 | tf_op jit(solution)/shard_map/forward_high/pallas_call | solution.py:162
  396.3 6.6 all-to-all-start.1
  407.3 20.8 %all-to-all-done.1 = bf16[16,64,512]{2,1,0:T(8,128)(2,1)S(1)} async-done(((bf16[16,64,512]{2,1,0:T(8,128)(2,1)}), bf16[16,64,512]{2,1,0:T(8,128)(2,1)S(1)}, u32[]{:S(2)}, u32[]{:S(2)}) %all-to-all-start.1) | async-done | bytes 1048608 | tf_op jit(solution)/shard_map/all_to_all | solution.py:776
  428.1 4.4 fusion.19
  441.3 37.7 %mlp_forward.1 = (bf16[1024,4096]{1,0:T(8,128)(2,1)}, bf16[1024,4096]{1,0:T(8,128)(2,1)}, bf16[1024,1024]{1,0:T(8,128)(2,1)}, bf16[1024,1024]{1,0:T(8,128)(2,1)}, f32[8,1024]{1,0:T(8,128)}) custom-call(bf16[1024,1024]{1,0:T(8,128)(2,1)} %add_convert_fusion.normed, bf16[4096,1024]{1,0:T(8,128)(2,1)} %all-gather.13.cloned.1.call-done.up, f32[1,4096]{1,0:T(1,128)} %bitcast.125, ...), custom_call_target="tpu_custom_call" | custom-call | flops 17179869184 | bytes 33554432 | tf_op jit(solution)/shard_map/mlp_forward/pallas_call | solution.py:602
  479.1 36.0 %mlp_backward.1 = (bf16[1024,4096]{1,0:T(8,128)(2,1)}, f32[1,4096]{1,0:T(1,128)}, f32[1024,1024]{1,0:T(8,128)}, bf16[1024,1024]{1,0:T(8,128)(2,1)}, f32[8,1024]{1,0:T(8,128)}) custom-call(bf16[1024,1024]{1,0:T(8,128)(2,1)} %get-tuple-element.66.grad, bf16[4096,1024]{1,0:T(8,128)(2,1)} %all-gather.15.cloned.1.call-done.down, ...), custom_call_target="tpu_custom_call" | custom-call | flops 17179869184 | bytes 33554432 | tf_op jit(solution)/shard_map/mlp_backward/pallas_call | solution.py:602
  515.2 4.1 convolution_convert_fusion
  523.4 4.8 all-to-all-start.2
  529.9 23.0 %mlp_grads.1 = (bf16[4096,1024]{1,0:T(8,128)(2,1)}, bf16[4096,1024]{1,0:T(8,128)(2,1)}) custom-call(bf16[1024,4096]{1,0:T(8,128)(2,1)} %get-tuple-element.69.hidden, bf16[1024,1024]{1,0:T(8,128)(2,1)} %get-tuple-element.66.grad, bf16[1024,4096]{1,0:T(8,128)(2,1)} %get-tuple-element.70.grad_pre, bf16[1024,1024]{1,0:T(8,128)(2,1)} %add_convert_fusion.normed), custom_call_target="tpu_custom_call" | custom-call | flops 17179869184 | bytes 33554432 | tf_op jit(solution)/shard_map/mlp_grads/pallas_call | solution.py:602
  553.1 6.0 all-to-all-start.3
  569.4 101.3 %backward_high.1 = (f32[64,8192]{1,0:T(8,128)}, bf16[16,128,512]{2,1,0:T(8,128)(2,1)}) custom-call(s32[32]{0:T(128)} %get-tuple-element.126.table.refs_0_, bf16[64,8192]{1,0:T(8,128)(2,1)} %get-tuple-element.130.refs_1_, bf16[8192,64]{1,0:T(8,128)(2,1)} %copy-done.11, bf16[64,8192]{1,0:T(8,128)(2,1)} %copy-done.14, bf16[8192,64]{1,0:T(8,128)(2,1)} %copy-done.10, ...), custom_call_target="tpu_custom_call" | custom-call | flops 17179869184 | bytes 16777216 | tf_op jit(solution)/shard_map/backward_high/pallas_call | solution.py:405
  670.7 6.0 all-to-all-start.4
  678.9 8.8 delta_low.1
  692.2 99.7 %backward_low.1 = (f32[8192,64]{1,0:T(8,128)}, f32[8192,64]{1,0:T(8,128)}, bf16[16,64,512]{2,1,0:T(8,128)(2,1)}) custom-call(s32[32]{0:T(128)} %get-tuple-element.126.table.refs_0_, bf16[64,8192]{1,0:T(8,128)(2,1)} %get-tuple-element.129.refs_1_, bf16[8192,64]{1,0:T(8,128)(2,1)} %copy-done.13, bf16[64,8192]{1,0:T(8,128)(2,1)} %copy-done.15, ...), custom_call_target="tpu_custom_call" | custom-call | flops 17179869184 | bytes 16777216 | tf_op jit(solution)/shard_map/backward_low/pallas_call | solution.py:405
  791.8 96.1 %backward_first.1 = (f32[64,8192]{1,0:T(8,128)}, bf16[16,128,512]{2,1,0:T(8,128)(2,1)}) custom-call(s32[32]{0:T(128)} %get-tuple-element.126.table.refs_0_, bf16[64,8192]{1,0:T(8,128)(2,1)} %get-tuple-element.130.refs_1_, bf16[8192,64]{1,0:T(8,128)(2,1)} %copy-done.11, bf16[64,8192]{1,0:T(8,128)(2,1)} %copy-done.14, bf16[8192,64]{1,0:T(8,128)(2,1)} %copy-done.10, ...), custom_call_target="tpu_custom_call" | custom-call | flops 17179869184 | bytes 16777216 | tf_op jit(solution)/shard_map/backward_first/pallas_call | solution.py:405
  887.9 6.4 all-to-all-start.5
  894.3 95.2 %backward_second.1 = (bf16[16,64,512]{2,1,0:T(8,128)(2,1)}, bf16[16,128,256]{2,1,0:T(8,128)(2,1)}) custom-call(s32[32]{0:T(128)} %get-tuple-element.126.table.refs_0_, bf16[64,8192]{1,0:T(8,128)(2,1)} %get-tuple-element.130.refs_1_, bf16[8192,64]{1,0:T(8,128)(2,1)} %copy-done.11, bf16[64,8192]{1,0:T(8,128)(2,1)} %copy-done.14, bf16[8192,64]{1,0:T(8,128)(2,1)} %copy-done.10, ...), custom_call_target="tpu_custom_call" | custom-call | flops 17179869184 | bytes 16777216 | tf_op jit(solution)/shard_map/backward_second/pallas_call | solution.py:405
  989.6 6.0 all-to-all-start.6
  996.9 20.1 %weight_grad.1 = bf16[2,208,512]{2,1,0:T(8,128)(2,1)S(1)} custom-call(bf16[16,128,512]{2,1,0:T(8,128)(2,1)S(1)} %copy-done.2, bf16[16,128,512]{2,1,0:T(8,128)(2,1)} %get-tuple-element.96.first, bf16[16,64,512]{2,1,0:T(8,128)(2,1)S(1)} %copy-done.3, bf16[16,128,256]{2,1,0:T(8,128)(2,1)} %get-tuple-element.104.second, ...), custom_call_target="tpu_custom_call" | custom-call | flops 6442450944 | bytes 33554432 | tf_op jit(solution)/shard_map/weight_grad/pallas_call | solution.py:470
  1017.0 3.9 all-to-all-done.6.query
  1020.9 14.2 %all_to_all.45 = bf16[2,208,512]{2,1,0:T(8,128)(2,1)S(1)} all-to-all(bf16[2,208,512]{2,1,0:T(8,128)(2,1)S(1)} %weight_grad.1), channel_id=1, replica_groups=mesh['ctx'=16,'wt'=2] {'wt'}, dimensions={0} | all-to-all | bytes 851968 | tf_op jit(solution)/shard_map/all_to_all | solution.py:895
  1035.9 5.5 all-to-all-start.8
  1046.9 11.8 %dynamic-slice_convert_fusion = (f32[2048,1024]{1,0:T(8,128)}, f32[2048,1024]{1,0:T(8,128)}) fusion(bf16[4096,1024]{1,0:T(8,128)(2,1)} %get-tuple-element.120.refs_1_, s32[]{:T(128)S(6)} %select_n.41, bf16[4096,1024]{1,0:T(8,128)(2,1)} %get-tuple-element.121.refs_2_), kind=kLoop, calls=%fused_computation.13 | loop fusion | flops 4194304 | bytes 25165828 | tf_op jit(solution)/shard_map/convert_element_type | solution.py:892
  1058.7 14.4 %all-to-all-done.8.second = bf16[16,128,256]{2,1,0:T(8,128)(2,1)S(1)} async-done(((bf16[16,128,256]{2,1,0:T(8,128)(2,1)}), bf16[16,128,256]{2,1,0:T(8,128)(2,1)S(1)}, u32[]{:S(2)}, u32[]{:S(2)}) %all-to-all-start.8) | async-done | bytes 1048608 | tf_op jit(solution)/shard_map/all_to_all | solution.py:868
  1074.1 18.4 %input_grads.1 = f32[1024,1024]{1,0:T(8,128)} custom-call(bf16[16,128,512]{2,1,0:T(8,128)(2,1)} %all-to-all-done.5.refs_0_.first, bf16[16,128,256]{2,1,0:T(8,128)(2,1)} %copy-done.24, bf16[16,64,512]{2,1,0:T(8,128)(2,1)} %all-to-all-done.6.query, bf16[16,128,512]{2,1,0:T(8,128)(2,1)} %all-to-all-done.4.refs_13_.high, ...), custom_call_target="tpu_custom_call" | custom-call | flops 6442450944 | bytes 25165824 | tf_op jit(solution)/shard_map/input_grads/pallas_call | solution.py:668
  1094.4 5.8 place.1
  1100.6 4.2 fusion.1
  (217 shorter events, 74.8 us)
Async XLA Ops:
  7.2 14.2 %copy-start.18 = (bf16[1,1024,1024]{2,1,0:T(8,128)(2,1)S(1)}, bf16[1,1024,1024]{2,1,0:T(8,128)(2,1)}, u32[]{:S(2)}) copy-start(bf16[1,1024,1024]{2,1,0:T(8,128)(2,1)} %param.13) | copy-start | bytes 6291460
  7.2 187.0 %all-gather.9.cloned.1.call-start = ((), (), s32[]{:S(2)}) async-start(), calls=%async_computation.9 | async-start | bytes 35651584 | tf_op jit(solution)/shard_map/all_gather | solution.py:748
  15.3 10.4 copy-start.27
  23.6 383.7 %all-gather.11.cloned.1.call-start = ((), (), s32[]{:S(2)}) async-start(), calls=%async_computation.10 | async-start | bytes 3145728 | tf_op jit(solution)/shard_map/all_gather | solution.py:786
  24.4 417.0 %all-gather.13.cloned.1.call-start = ((), (), s32[]{:S(2)}) async-start(), calls=%async_computation.11 | async-start | bytes 12582912 | tf_op jit(solution)/shard_map/all_gather | solution.py:787
  25.1 416.2 %all-gather.15.cloned.1.call-start = ((), (), s32[]{:S(2)}) async-start(), calls=%async_computation.12 | async-start | bytes 12582912 | tf_op jit(solution)/shard_map/all_gather | solution.py:788
  26.3 10.8 copy-start.43
  265.2 131.1 %all-to-all-start = ((bf16[16,64,512]{2,1,0:T(8,128)(2,1)}), bf16[16,64,512]{2,1,0:T(8,128)(2,1)S(1)}, u32[]{:S(2)}, u32[]{:S(2)}) async-start(bf16[16,64,512]{2,1,0:T(8,128)(2,1)} %get-tuple-element.63), calls=%async_computation | async-start | bytes 2097152 | tf_op jit(solution)/shard_map/all_to_all | solution.py:776
  270.5 133.1 %copy-start.42 = (f32[1,4,2,128]{3,2,1,0:T(2,128)S(1)}, f32[1,4,2,128]{3,2,1,0:T(2,128)}, u32[]{:S(2)}) copy-start(f32[1,4,2,128]{3,2,1,0:T(2,128)} %get-tuple-element.153) | copy-start | bytes 12292
  270.5 133.1 %copy-start.35 = (f32[1,4,2,128]{3,2,1,0:T(2,128)S(1)}, f32[1,4,2,128]{3,2,1,0:T(2,128)}, u32[]{:S(2)}) copy-start(f32[1,4,2,128]{3,2,1,0:T(2,128)} %get-tuple-element.146) | copy-start | bytes 12292
  270.5 133.1 %copy-start.41 = (f32[1,4,2,128]{3,2,1,0:T(2,128)S(1)}, f32[1,4,2,128]{3,2,1,0:T(2,128)}, u32[]{:S(2)}) copy-start(f32[1,4,2,128]{3,2,1,0:T(2,128)} %get-tuple-element.152) | copy-start | bytes 12292
  270.6 133.1 %copy-start.34 = (f32[1,4,2,128]{3,2,1,0:T(2,128)S(1)}, f32[1,4,2,128]{3,2,1,0:T(2,128)}, u32[]{:S(2)}) copy-start(f32[1,4,2,128]{3,2,1,0:T(2,128)} %get-tuple-element.145) | copy-start | bytes 12292
  270.6 133.1 %copy-start.40 = (f32[1,1,2,512]{3,2,1,0:T(2,128)S(1)}, f32[1,1,2,512]{3,2,1,0:T(2,128)}, u32[]{:S(2)}) copy-start(f32[1,1,2,512]{3,2,1,0:T(2,128)} %get-tuple-element.151) | copy-start | bytes 12292
  270.6 133.7 %copy-start.33 = (f32[1,1,2,512]{3,2,1,0:T(2,128)S(1)}, f32[1,1,2,512]{3,2,1,0:T(2,128)}, u32[]{:S(2)}) copy-start(f32[1,1,2,512]{3,2,1,0:T(2,128)} %get-tuple-element.144) | copy-start | bytes 12292
  270.6 134.3 %copy-start.28 = (f32[1,1,2,2048]{3,2,1,0:T(2,128)S(1)}, f32[1,1,2,2048]{3,2,1,0:T(2,128)}, u32[]{:S(2)}) copy-start(f32[1,1,2,2048]{3,2,1,0:T(2,128)} %get-tuple-element.140) | copy-start | bytes 49156
  270.6 135.5 %copy-start.39 = (f32[1,1,2,512]{3,2,1,0:T(2,128)S(1)}, f32[1,1,2,512]{3,2,1,0:T(2,128)}, u32[]{:S(2)}) copy-start(f32[1,1,2,512]{3,2,1,0:T(2,128)} %get-tuple-element.149) | copy-start | bytes 12292
  270.6 136.1 %copy-start.38 = (f32[1,1,2,512]{3,2,1,0:T(2,128)S(1)}, f32[1,1,2,512]{3,2,1,0:T(2,128)}, u32[]{:S(2)}) copy-start(f32[1,1,2,512]{3,2,1,0:T(2,128)} %get-tuple-element.150) | copy-start | bytes 12292
  396.3 31.8 %all-to-all-start.1 = ((bf16[16,64,512]{2,1,0:T(8,128)(2,1)}), bf16[16,64,512]{2,1,0:T(8,128)(2,1)S(1)}, u32[]{:S(2)}, u32[]{:S(2)}) async-start(bf16[16,64,512]{2,1,0:T(8,128)(2,1)} %get-tuple-element.64), calls=%async_computation.1 | async-start | bytes 2097152 | tf_op jit(solution)/shard_map/all_to_all | solution.py:776
  479.1 36.0 %copy-start.26 = (bf16[16,64,512]{2,1,0:T(8,128)(2,1)S(1)}, bf16[16,64,512]{2,1,0:T(8,128)(2,1)}, u32[]{:S(2)}) copy-start(bf16[16,64,512]{2,1,0:T(8,128)(2,1)} %copy-done.25) | copy-start | bytes 3145732
  523.4 29.7 %all-to-all-start.2 = ((bf16[16,64,512]{2,1,0:T(8,128)(2,1)}), bf16[16,64,512]{2,1,0:T(8,128)(2,1)S(1)}, u32[]{:S(2)}, u32[]{:S(2)}) async-start(bf16[16,64,512]{2,1,0:T(8,128)(2,1)} %bitcast.15), calls=%async_computation.2 | async-start | bytes 2097152 | tf_op jit(solution)/shard_map/all_to_all | solution.py:779
  528.2 467.5 %all-reduce.3.cloned.1.call-start = ((), (), s32[]{:S(2)}) async-start(), calls=%async_computation.15 | async-start | bytes 37814272 | tf_op jit(solution)/shard_map/psum | solution.py:855
  553.1 117.6 %all-to-all-start.3 = ((bf16[16,64,512]{2,1,0:T(8,128)(2,1)}), bf16[16,64,512]{2,1,0:T(8,128)(2,1)}, u32[]{:S(2)}, u32[]{:S(2)}) async-start(bf16[16,64,512]{2,1,0:T(8,128)(2,1)} %bitcast.106), calls=%async_computation.3 | async-start | bytes 2097152 | tf_op jit(solution)/shard_map/all_to_all | solution.py:779
  670.7 121.1 %all-to-all-start.4 = ((bf16[16,128,512]{2,1,0:T(8,128)(2,1)}), bf16[16,128,512]{2,1,0:T(8,128)(2,1)}, u32[]{:S(2)}, u32[]{:S(2)}) async-start(bf16[16,128,512]{2,1,0:T(8,128)(2,1)} %get-tuple-element.93.high_pair), calls=%async_computation.4 | async-start | bytes 4194304 | tf_op jit(solution)/shard_map/all_to_all | solution.py:868
  676.7 382.0 %all-gather.17.cloned.1.call-start = ((), (), s32[]{:S(2)}) async-start(), calls=%async_computation.13 | async-start | bytes 9437184 | tf_op jit(solution)/shard_map/all_gather | solution.py:789
  887.9 101.7 %all-to-all-start.5 = ((bf16[16,128,512]{2,1,0:T(8,128)(2,1)}), bf16[16,128,512]{2,1,0:T(8,128)(2,1)}, u32[]{:S(2)}, u32[]{:S(2)}) async-start(bf16[16,128,512]{2,1,0:T(8,128)(2,1)} %get-tuple-element.96.first), calls=%async_computation.5 | async-start | bytes 4194304 | tf_op jit(solution)/shard_map/all_to_all | solution.py:868
  894.3 101.3 %copy-start.2 = (bf16[16,128,512]{2,1,0:T(8,128)(2,1)S(1)}, bf16[16,128,512]{2,1,0:T(8,128)(2,1)}, u32[]{:S(2)}) copy-start(bf16[16,128,512]{2,1,0:T(8,128)(2,1)} %get-tuple-element.93.high_pair) | copy-start | bytes 6291460
  989.6 31.3 %all-to-all-start.6 = ((bf16[16,64,512]{2,1,0:T(8,128)(2,1)}), bf16[16,64,512]{2,1,0:T(8,128)(2,1)}, u32[]{:S(2)}, u32[]{:S(2)}) async-start(bf16[16,64,512]{2,1,0:T(8,128)(2,1)} %get-tuple-element.98.query), calls=%async_computation.6 | async-start | bytes 2097152 | tf_op jit(solution)/shard_map/all_to_all | solution.py:868
  995.6 96.9 %all-gather.19.cloned.1.call-start = ((), (), s32[]{:S(2)}) async-start(), calls=%async_computation.14 | async-start | bytes 3620864 | tf_op jit(solution)/shard_map/all_gather | solution.py:899
  996.9 44.5 %copy-start.37 = (f32[1,1,2,512]{3,2,1,0:T(2,128)S(1)}, f32[1,1,2,512]{3,2,1,0:T(2,128)}, u32[]{:S(2)}) copy-start(f32[1,1,2,512]{3,2,1,0:T(2,128)} %get-tuple-element.148) | copy-start | bytes 12292
  996.9 44.5 %copy-start.32 = (f32[1,1,2,512]{3,2,1,0:T(2,128)S(1)}, f32[1,1,2,512]{3,2,1,0:T(2,128)}, u32[]{:S(2)}) copy-start(f32[1,1,2,512]{3,2,1,0:T(2,128)} %get-tuple-element.143) | copy-start | bytes 12292
  1035.9 37.2 %all-to-all-start.8 = ((bf16[16,128,256]{2,1,0:T(8,128)(2,1)}), bf16[16,128,256]{2,1,0:T(8,128)(2,1)S(1)}, u32[]{:S(2)}, u32[]{:S(2)}) async-start(bf16[16,128,256]{2,1,0:T(8,128)(2,1)} %get-tuple-element.104.second), calls=%async_computation.8 | async-start | bytes 2097152 | tf_op jit(solution)/shard_map/all_to_all | solution.py:868
  1041.4 17.3 %copy-start.29 = (f32[1,1,2,512]{3,1,2,0:T(1,128)}, f32[1,1,2,512]{3,1,2,0:T(1,128)S(1)}, u32[]{:S(2)}) copy-start(f32[1,1,2,512]{3,1,2,0:T(1,128)S(1)} %copy.56) | copy-start | bytes 12292
  (29 other events, 83.4 us)
Sparse Core Ops, SparseCore 0:
  23.7 170.4 all-gather.8
  195.7 33.0 all-gather.10
  230.3 103.9 all-gather.12
  335.8 103.9 all-gather.14
  553.2 394.3 all-reduce.2
  949.0 85.4 all-gather.16
  1036.8 55.4 all-gather.18
